TPU v7x, 32 devices: a whole 2x2x4 slice. The times are simulated.
32 devices in a mesh: br: 16 (over z, y, x), bus: 2 (over core).
Axes of the slice: x: 2, y: 2, z: 4, core: 2. Of those that a mesh axis runs over, the one named last changes fastest.
Arguments:
- net_load: bfloat16 [128, 60416], P('br', 'bus'), may hold values from -6 to 6
- release: float32 [128, 1024], P('br'), may hold values from 0 to 2
- plant_bus: int32 [1024], replicated, may hold values from 0 to 60415
- efficiency: float32 [1024], replicated, may hold values from 0.5 to 2
- ptdf: bfloat16 [2048, 60416], P('br', 'bus'), may hold values from -0.0234375 to 0.0234375
- branch_class: int32 [2048], P('br'), may hold values from 0 to 15
- class_limit: float32 [16], replicated, may hold values from 0.4 to 3
- class_price: float32 [16], replicated, may hold values from 0.5 to 5
Outputs:
- grad_bus: float32 [128, 60416], P('br', 'bus')
- grad_release: float32 [128, 1024], P('br')
All inputs are finite; a program needn't handle non-finite values.
Results may differ from a plain program's by a relative error of at most 0.0031.
Values may be sent and summed in bfloat16 or wider, within the bound.
No kernel may reach another device: no remote copies, remote signals or barrier semaphores. Data moves between devices by JAX's collectives and lax.ppermute only.
A program may use at most 64 MiB of HBM per device.

v0:
```python
import jax
import jax.numpy as jnp
from jax import lax
from jax.sharding import PartitionSpec as P

SMOOTH = 0.25


def shards(net_load, release, plant_bus, efficiency, ptdf, branch_class, class_limit, class_price):
    rows_local, bus_local = net_load.shape
    offset = lax.axis_index("bus") * bus_local
    columns = plant_bus - offset
    inside = ((columns >= 0) & (columns < bus_local)).astype(jnp.float32)
    clipped = jnp.clip(columns, 0, bus_local - 1)
    weighted = efficiency * inside
    inject = (
        net_load.astype(jnp.float32)
        .at[:, clipped]
        .add(release * weighted[None, :])
        .astype(jnp.bfloat16)
    )
    partial_flows = lax.dot_general(
        lax.all_gather(inject, "br", axis=0, tiled=True),
        ptdf,
        (((1,), (1,)), ((), ())),
        preferred_element_type=jnp.float32,
    )
    onehot = (branch_class[:, None] == jnp.arange(class_limit.shape[0])[None, :]).astype(
        jnp.float32
    )
    limit = jnp.sum(onehot * class_limit[None, :], axis=1)[None, :]
    price = jnp.sum(onehot * class_price[None, :], axis=1)[None, :]
    flows = lax.psum(partial_flows, "bus")
    upper = jax.nn.sigmoid((flows - limit) / SMOOTH)
    lower = jax.nn.sigmoid((-flows - limit) / SMOOTH)
    grad_flow = (price * (upper - lower)).astype(jnp.bfloat16)
    grad_bus = lax.psum_scatter(
        jnp.dot(grad_flow, ptdf, preferred_element_type=jnp.float32),
        "br",
        scatter_dimension=0,
        tiled=True,
    )
    picked = grad_bus[:, clipped] * weighted[None, :]
    grad_release = lax.psum(picked, "bus")
    return (grad_bus, grad_release)


def solution(mesh):
    placed = (P("br", "bus"), P("br", None), P(), P(), P("br", "bus"), P("br"), P(), P())
    return jax.shard_map(
        shards,
        mesh=mesh,
        in_specs=placed,
        out_specs=(P("br", "bus"), P("br", None)),
        check_vma=False,
    )
```

profile of v0, /device:TPU:0, one launch (start us, length us, event | category | flops | bytes accessed | tf_op | source)
XLA Modules:
  0.0 536.8 jit_solution(5691612177521432942)
XLA Ops:
  7.2 0.0 all-gather.2.cloned.1.call-start
  7.2 0.7 broadcast_clamp_fusion
  7.9 0.7 and_select_fusion
  8.6 0.8 multiply_bitcast_fusion.1
  9.4 0.2 copy.25
  9.6 7.6 %copy.24 = f32[8,30208]{0,1:T(8,128)} copy(bf16[8,30208]{1,0:T(8,128)(2,1)} %param.8) | data formatting | bytes 1449984 | tf_op jit(solution)/shard_map/convert_element_type | solution.py:17
  17.2 16.3 %scatter_fusion = f32[8,30208]{0,1:T(8,128)} fusion(f32[8,30208]{0,1:T(8,128)} %copy.24, s32[1024]{0:T(1024)S(1)} %get-tuple-element.13, f32[1024,8]{1,0:T(8,128)S(1)} %copy.25), kind=kCustom, calls=%fused_computation.1 | custom fusion | flops 8192 | bytes 102400 | tf_op jit(solution)/shard_map/scatter-add | solution.py:19
  33.4 8.1 %copy.26 = bf16[8,30208]{1,0:T(8,128)(2,1)} copy(f32[8,30208]{0,1:T(8,128)} %scatter_fusion) | data formatting | bytes 1449984 | tf_op jit(solution)/shard_map/scatter-add | solution.py:19
  41.5 0.0 all-gather.2.cloned.1.call-update
  41.6 0.0 copy-start
  41.6 0.0 copy-start.1
  41.6 0.0 copy-start.2
  41.6 0.0 all-reduce.2.cloned.1.call-start
  41.7 109.7 %all-gather.2.cloned.1.call-done = bf16[128,30208]{1,0:T(8,128)(2,1)} async-done(((bf16[8,30208]{1,0:T(8,128)(2,1)}), bf16[128,30208]{1,0:T(8,128)(2,1)}) %all-gather.2.cloned.1.call-update) | async-done | bytes 7733264 | tf_op jit(solution)/shard_map/all_gather | solution.py:23
  151.3 8.2 %fusion.7 = f32[128,128]{1,0:T(8,128)} fusion(bf16[128,30208]{1,0:T(8,128)(2,1)} %all-gather.2.cloned.1.call-done, bf16[128,30208]{1,0:T(8,128)(2,1)} %param.12), kind=kOutput, calls=%fused_computation.18 | convolution fusion | flops 989855744 | bytes 15532032 | tf_op jit(solution)/shard_map/dot_general | solution.py:22
  159.5 0.0 all-reduce.2.cloned.1.call-update
  159.5 0.0 reduce-scatter.2.cloned.1.call-start
  159.6 0.0 copy-done
  159.6 0.0 copy-done.1
  159.6 0.0 copy-done.2
  159.6 0.1 select_reduce_fusion.1
  159.7 15.9 %all-reduce.2.cloned.1.call-done = f32[128,128]{1,0:T(8,128)} async-done(((f32[128,128]{1,0:T(8,128)}), f32[128,128]{1,0:T(8,128)}) %all-reduce.2.cloned.1.call-update) | async-done | bytes 65552 | tf_op jit(solution)/shard_map/psum | solution.py:33
  175.6 10.8 %fusion = f32[128,30208]{1,0:T(8,128)} fusion(bf16[128,30208]{1,0:T(8,128)(2,1)} %param.12, f32[128,128]{1,0:T(8,128)} %all-reduce.2.cloned.1.call-done, f32[128]{0:T(128)S(1)} %get-tuple-element.11, f32[128]{0:T(128)S(1)} %get-tuple-element.10), kind=kOutput, calls=%fused_computation.4 | convolution fusion | flops 990085120 | bytes 23266304 | tf_op jit(solution)/shard_map/dot_general | solution.py:38
  186.4 0.0 reduce-scatter.2.cloned.1.call-update
  186.5 321.3 %reduce-scatter.2.cloned.1.call-done = f32[8,30208]{1,0:T(8,128)} async-done(((f32[128,30208]{1,0:T(8,128)}), f32[8,30208]{1,0:T(8,128)}) %reduce-scatter.2.cloned.1.call-update) | async-done | bytes 966672 | tf_op jit(solution)/shard_map/reduce_scatter | solution.py:37
  507.8 8.7 %copy.27 = f32[8,30208]{0,1:T(8,128)} copy(f32[8,30208]{1,0:T(8,128)} %reduce-scatter.2.cloned.1.call-done) | data formatting | bytes 1933312 | tf_op jit(solution)/shard_map/reduce_scatter | solution.py:37
  516.5 8.2 %gather_fusion = f32[1024,8]{1,0:T(8,128)S(1)} fusion(f32[8,30208]{0,1:T(8,128)} %copy.27, s32[1024]{0:T(1024)S(1)} %get-tuple-element.12), kind=kCustom, calls=%fused_computation | custom fusion | bytes 69632 | tf_op jit(solution)/shard_map/gather | solution.py:43
  524.7 0.2 multiply_bitcast_fusion
  524.9 4.5 psum.15
  529.5 0.8 copy.28
Async XLA Ops:
  7.2 144.2 %all-gather.2.cloned.1.call-start = ((), (), s32[]{:S(2)}) async-start(), calls=%async_computation.1 | async-start | bytes 8216576 | tf_op jit(solution)/shard_map/all_gather | solution.py:23
  41.6 118.0 %copy-start = (f32[16]{0:T(128)S(1)}, f32[16]{0:T(128)}, u32[]{:S(2)}) copy-start(f32[16]{0:T(128)} %param.15) | copy-start | bytes 196
  41.6 118.0 %copy-start.1 = (s32[128]{0:T(128)S(1)}, s32[128]{0:T(128)}, u32[]{:S(2)}) copy-start(s32[128]{0:T(128)} %param.13) | copy-start | bytes 1540
  41.6 118.0 %copy-start.2 = (f32[16]{0:T(128)S(1)}, f32[16]{0:T(128)}, u32[]{:S(2)}) copy-start(f32[16]{0:T(128)} %param.14) | copy-start | bytes 196
  41.6 134.0 %all-reduce.2.cloned.1.call-start = ((), (), s32[]{:S(2)}) async-start(), calls=%async_computation.2 | async-start | bytes 131072 | tf_op jit(solution)/shard_map/psum | solution.py:33
  159.5 348.3 %reduce-scatter.2.cloned.1.call-start = ((), (), s32[]{:S(2)}) async-start(), calls=%async_computation.3 | async-start | bytes 16433152 | tf_op jit(solution)/shard_map/reduce_scatter | solution.py:37
Sparse Core Ops, SparseCore 0:
  41.7 109.5 all-gather.1
  159.7 15.8 all-reduce.1
  186.6 321.1 reduce-scatter.1
where the time goes:
time: 542 us; the launch traced here: 537 us
  waiting for transfers between devices  447 us (82%)
  local copies, waits for them, and re-layouts  33.6 us (6%)
  matrix products  19 us (4%)
  other arithmetic  18.7 us (3%)
  between operations  13.8 us (3%)
    reduce_scatter x1, waiting for transfers between devices, shards(): lax.psum_scatter(jnp.dot(grad_flow, ptdf, preferred_element_type=jnp.floa...  321 us
    all_gather x1, waiting for transfers between devices, shards(): lax.all_gather(inject, 'br', axis=0, tiled=True)  110 us
    scatter-add x1, other arithmetic, shards(): inject = net_load.astype(jnp.float32).at[:, clipped].add(release * weight...  16.3 us
    psum x1, waiting for transfers between devices, shards(): flows = lax.psum(partial_flows, 'bus')  15.9 us
    dot_general x1, matrix products, shards(): jnp.dot(grad_flow, ptdf, preferred_element_type=jnp.float32)  10.8 us
  transfers between devices with their start and end apart: 3, of which 3 were waited for; matrix products, arithmetic and copies ran while one was open for 0% of the time, Pallas kernels for 0%

commit v1 on v0

v1 whole, which is shorter than its diff:
```python
import functools

import jax
import jax.numpy as jnp
from jax import lax
from jax.experimental import pallas as pl
from jax.experimental.pallas import tpu as pltpu
from jax.sharding import PartitionSpec as P

SMOOTH = 0.25
Z, Y, X = 0, 1, 2


def chip_box(count):
    bits = (count // 2).bit_length() - 1
    nx = 1 << (bits // 2)
    return count // (2 * nx), 2, nx


GATHER = [
    [(Z, -1, (-1, 0, 0)), (X, 1, (0, 0, 1)), (Y, 1, (0, 1, 0))],
    [(Z, -1, (2, 0, 0)), (X, 1, (-1, 0, 1)), (Y, 1, (0, 1, 1))],
    [(Z, 1, (1, 1, 0)), (X, 1, (2, 0, 1)), (Y, 1, (-1, 1, 1))],
    [(Z, 1, (1, 0, 0)), (X, 1, (1, 1, 1)), (Y, 1, (2, 1, 1))],
    [(Z, 1, (2, 1, 0)), (X, 1, (1, 0, 1)), (Y, 1, (-1, 1, 0))],
]
REDUCE = [
    [(Z, 1, (1, 0, 0)), (X, 1, (0, 0, 1)), (Y, 1, (0, 1, 0))],
    [(Z, 1, (2, 0, 0)), (X, 1, (1, 0, 1)), (Y, 1, (1, 1, 0))],
    [(Z, -1, (-1, 1, 0)), (X, 1, (2, 0, 1)), (Y, 1, (2, 1, 0))],
    [(Z, -1, (-1, 0, 0)), (X, 1, (1, 1, 1)), (Y, 1, (2, 1, 1))],
    [(Z, -1, (-1, 0, 1)), (X, 1, (-1, 1, 1)), (Y, 1, (0, 1, 1))],
]
BATCH_ENDS = (2, 3, 4)


def greedy(box):
    labels = [(z, y, x) for z in range(box[0]) for y in range(box[1]) for x in range(box[2])]
    have, rounds = {(0, 0, 0)}, []
    while len(have) < len(labels):
        taken, now = set(), []
        for axis in (Z, X, Y):
            shifts = (1, -1) if box[axis] > 2 else (1,)
            options = [
                (shift, label)
                for label in labels
                if label not in have and label not in taken
                for shift in shifts
                if step_back(label, axis, shift, box) in have
            ]
            if options:
                shift, label = options[0]
                now.append((axis, shift, label))
                taken.add(label)
        have |= taken
        rounds.append(now)
    return rounds


def step_back(label, axis, shift, box):
    moved = list(label)
    moved[axis] = (moved[axis] - shift) % box[axis]
    return tuple(moved)


def plan(box):
    if box == (4, 2, 2):
        wrap = lambda rounds: [
            [(a, s, tuple(c % n for c, n in zip(label, box))) for a, s, label in now] for now in rounds
        ]
        return wrap(GATHER), wrap(REDUCE), BATCH_ENDS
    rounds = greedy(box)
    return rounds, rounds, (len(rounds) - 1,)


def moves(axis, shift, box):
    pairs = []
    for z in range(box[0]):
        for y in range(box[1]):
            for x in range(box[2]):
                to = step_back((z, y, x), axis, -shift, box)
                pairs.append(((z * box[1] + y) * box[2] + x, (to[0] * box[1] + to[1]) * box[2] + to[2]))
    return pairs


def after(value, earlier):
    if earlier is None:
        return value
    return lax.optimization_barrier((value, earlier))[0]


def tile_of(width):
    groups = width // 128
    return 128 * max(n for n in range(1, 65) if groups % n == 0)


def inject_kernel(net_ref, weight_ref, column_ref, out_ref):
    rows, width = net_ref.shape
    groups = width // 128
    column = column_ref[...]
    place = jnp.where(column >= 0, column // 128, -1) - pl.program_id(0) * groups
    weight = weight_ref[...]
    high = weight.astype(jnp.bfloat16).astype(jnp.float32)
    low = weight - high
    lane = lax.broadcasted_iota(jnp.int32, (128, column.shape[1]), 0)
    lanes = jnp.where(lane == column % 128, 1.0, 0.0).astype(jnp.bfloat16)

    def spread(values):
        picked = [jnp.where(place == group, values, 0.0) for group in range(groups)]
        return lax.dot_general(
            jnp.concatenate(picked, axis=0).astype(jnp.bfloat16),
            lanes,
            (((1,), (1,)), ((), ())),
            preferred_element_type=jnp.float32,
        )

    added = spread(high) + spread(low)
    for group in range(groups):
        at = slice(group * 128, (group + 1) * 128)
        total = net_ref[:, at].astype(jnp.float32) + added[group * rows : (group + 1) * rows]
        out_ref[:, at] = total.astype(jnp.bfloat16)


def inject_of(net_load, weight, column):
    rows, width = net_load.shape
    short = -rows % 8
    if short:
        net_load = jnp.pad(net_load, ((0, short), (0, 0)))
        weight = jnp.pad(weight, ((0, short), (0, 0)))
    tile = tile_of(width)
    plants = weight.shape[1]
    out = pl.pallas_call(
        inject_kernel,
        grid=(width // tile,),
        in_specs=[
            pl.BlockSpec((rows + short, tile), lambda i: (0, i)),
            pl.BlockSpec((rows + short, plants), lambda i: (0, 0)),
            pl.BlockSpec((1, plants), lambda i: (0, 0)),
        ],
        out_specs=pl.BlockSpec((rows + short, tile), lambda i: (0, i)),
        out_shape=jax.ShapeDtypeStruct(net_load.shape, jnp.bfloat16),
        compiler_params=pltpu.CompilerParams(vmem_limit_bytes=32 << 20),
        name="inject",
    )(net_load, weight, column)
    return out[:rows] if short else out


def flows_kernel(count, *refs):
    blocks, ptdf_ref, out_ref = refs[:count], refs[count], refs[count + 1]

    @pl.when(pl.program_id(0) == 0)
    def _():
        out_ref[...] = jnp.zeros_like(out_ref)

    rows = jnp.concatenate([block[...].astype(jnp.float32) for block in blocks], axis=0)
    out_ref[...] += lax.dot_general(
        rows.astype(jnp.bfloat16), ptdf_ref[...], (((1,), (1,)), ((), ())), preferred_element_type=jnp.float32
    )


def flows_of(blocks, ptdf):
    rows, width = blocks[0].shape
    branches = ptdf.shape[0]
    if rows % 8:
        blocks = [jnp.pad(jnp.concatenate(blocks, axis=0), ((0, -rows * len(blocks) % 8), (0, 0)))]
    count = len(blocks)
    tile = tile_of(width)
    total = sum(block.shape[0] for block in blocks)
    return pl.pallas_call(
        functools.partial(flows_kernel, count),
        grid=(width // tile,),
        in_specs=[pl.BlockSpec((block.shape[0], tile), lambda i: (0, i)) for block in blocks]
        + [pl.BlockSpec((branches, tile), lambda i: (0, i))],
        out_specs=pl.BlockSpec((total, branches), lambda i: (0, 0)),
        out_shape=jax.ShapeDtypeStruct((total, branches), jnp.float32),
        compiler_params=pltpu.CompilerParams(vmem_limit_bytes=32 << 20),
        cost_estimate=pl.CostEstimate(
            flops=2 * total * branches * width, bytes_accessed=2 * (total + branches) * width, transcendentals=0
        ),
        name="flows",
    )(*blocks, ptdf)


def make_shards(box, buses):
    gather, reduce, ends = plan(box)
    own = (0, 0, 0)

    def shards(net_load, release, plant_bus, efficiency, ptdf, branch_class, class_limit, class_price):
        rows_local, bus_local = net_load.shape
        offset = lax.axis_index("bus") * bus_local
        columns = plant_bus - offset
        inside = ((columns >= 0) & (columns < bus_local)).astype(jnp.float32)
        clipped = jnp.clip(columns, 0, bus_local - 1)
        weighted = efficiency * inside
        inject = inject_of(net_load, release * weighted[None, :], jnp.where(inside > 0, columns, -1)[None, :])
        onehot = (branch_class[:, None] == jnp.arange(class_limit.shape[0])[None, :]).astype(jnp.float32)
        limit = jnp.sum(onehot * class_limit[None, :], axis=1)[None, :]
        price = jnp.sum(onehot * class_price[None, :], axis=1)[None, :]

        def partial_grads(blocks):
            flows = flows_of(blocks, ptdf)
            if buses == 2:
                flows = flows + lax.ppermute(flows, "bus", [(0, 1), (1, 0)])
            else:
                flows = lax.psum(flows, "bus")
            upper = jax.nn.sigmoid((flows - limit) / SMOOTH)
            lower = jax.nn.sigmoid((-flows - limit) / SMOOTH)
            grad_flow = (price * (upper - lower)).astype(jnp.bfloat16)
            part = jnp.dot(grad_flow, ptdf, preferred_element_type=jnp.float32)
            return [part[i * rows_local : (i + 1) * rows_local] for i in range(len(blocks))]

        have, parts, fresh, last = {own: inject}, {}, [own], {}
        for index, now in enumerate(gather):
            for axis, shift, label in now:
                block = after(have[step_back(label, axis, shift, box)], last.get(axis))
                have[label] = last[axis] = lax.ppermute(block, "br", moves(axis, shift, box))
                fresh.append(label)
            if index in ends:
                for label, part in zip(fresh, partial_grads([have[label] for label in fresh])):
                    parts[label] = part
                fresh = []

        for now in reversed(reduce):
            for axis, shift, label in reversed(now):
                block = after(parts[label].astype(jnp.bfloat16), last.get(axis))
                last[axis] = lax.ppermute(block, "br", moves(axis, -shift, box))
                to = step_back(label, axis, shift, box)
                parts[to] = parts[to] + last[axis].astype(jnp.float32)
        grad_bus = parts[own]
        picked = grad_bus[:, clipped] * weighted[None, :]
        grad_release = lax.psum(picked, "bus")
        return (grad_bus, grad_release)

    return shards


def solution(mesh):
    placed = (P("br", "bus"), P("br", None), P(), P(), P("br", "bus"), P("br"), P(), P())
    return jax.shard_map(
        make_shards(chip_box(mesh.shape["br"]), mesh.shape["bus"]),
        mesh=mesh,
        in_specs=placed,
        out_specs=(P("br", "bus"), P("br", None)),
        check_vma=False,
    )
```

time: 542 us -> 191 us (0.35)
  waiting for transfers between devices: 447 us -> 109 us
  starting transfers between devices: 0.12 us -> 30 us
  other arithmetic: 18.7 us -> 3.75 us
  Pallas kernels: 0 us -> 14 us
  matrix products: 19 us -> 5.89 us
  between operations: 13.8 us -> 0.87 us
  local copies, waits for them, and re-layouts: 33.6 us -> 23.4 us
    reduce_scatter x1 -> x0, waiting for transfers between devices: 321 us -> none  [shards(): lax.psum_scatter(jnp.dot(grad_flow, ptdf, preferred_element_type=jnp.floa...]
    all_gather x1 -> x0, waiting for transfers between devices: 110 us -> none  [shards(): lax.all_gather(inject, 'br', axis=0, tiled=True)]
    ppermute x0 -> x33, waiting for transfers between devices: none -> 109 us  [the longest x15 54.6 us: shards(): lax.ppermute(block, 'br', moves(axis, shift, box))]
    ppermute x0 -> x33, starting transfers between devices: none -> 30 us  [the longest x15 18.9 us: shards(): lax.ppermute(block, 'br', moves(axis, shift, box))]
    scatter-add x1 -> x0, other arithmetic: 16.3 us -> none  [shards(): inject = net_load.astype(jnp.float32).at[:, clipped].add(release * weight...]
    psum x1 -> x0, waiting for transfers between devices: 15.9 us -> none  [shards(): flows = lax.psum(partial_flows, 'bus')]
    pallas_call x0 -> x4, Pallas kernels: none -> 14 us  [the longest x3 11 us: flows_of(): pl.pallas_call(functools.partial(flows_kernel, count), grid=(width // til...]
    dot_general x2 -> x3, matrix products: 19 us -> 5.89 us  [partial_grads(): part = jnp.dot(grad_flow, ptdf, preferred_element_type=jnp.float32)]
  transfers between devices with their start and end apart: 3 -> 33, of which waited for: 3 -> 25; matrix products, arithmetic and copies ran while one was open for 0% -> 4% of each run, Pallas kernels for 0% -> 0%
where the time goes in v1:
time: 191 us
  waiting for transfers between devices  109 us (57%)
  starting transfers between devices  30 us (16%)
  local copies, waits for them, and re-layouts  23.4 us (12%)
  Pallas kernels  14 us (7%)
  matrix products  5.89 us (3%)
  blocking collectives  4.51 us (2%)
  other arithmetic  3.75 us (2%)
    ppermute x15, waiting for transfers between devices, shards(): lax.ppermute(block, 'br', moves(axis, shift, box))  54.6 us
    ppermute x15, waiting for transfers between devices, shards(): last[axis] = lax.ppermute(block, 'br', moves(axis, -shift, box))  54 us
    ppermute x15, starting transfers between devices, shards(): lax.ppermute(block, 'br', moves(axis, shift, box))  18.9 us
    pallas_call x3, Pallas kernels, flows_of(): pl.pallas_call(functools.partial(flows_kernel, count), grid=(width // til...  11 us
    ppermute x15, starting transfers between devices, shards(): last[axis] = lax.ppermute(block, 'br', moves(axis, -shift, box))  10.9 us
    add x1, local copies, waits for them, and re-layouts, shards(): parts[to] = parts[to] + last[axis].astype(jnp.float32)  8.39 us
    gather x1, local copies, waits for them, and re-layouts, shards(): picked = grad_bus[:, clipped] * weighted[None, :]  8.2 us
    dot_general x3, matrix products, partial_grads(): part = jnp.dot(grad_flow, ptdf, preferred_element_type=jnp.float32)  5.89 us
  transfers between devices with their start and end apart: 33, of which 25 were waited for; matrix products, arithmetic and copies ran while one was open for 4% of the time, Pallas kernels for 0%

profile of v1, /device:TPU:0, one launch (start us, length us, event | category | flops | bytes accessed | tf_op | source)
XLA Modules:
  0.0 191.0 jit_solution(1020923690720237065)
XLA Ops:
  0.7 0.7 fusion.29
  1.4 0.7 fusion.31
  2.1 0.8 broadcast_multiply_fusion.weight_ref
  2.8 1.0 copy-done.1
  3.9 3.0 %inject.1.refs_0_ = bf16[8,30208]{1,0:T(8,128)(2,1)S(1)} custom-call(bf16[8,30208]{1,0:T(8,128)(2,1)S(1)} %copy-done.1, f32[8,1024]{1,0:T(8,128)S(1)} %broadcast_multiply_fusion.weight_ref, s32[1,1024]{1,0:T(1,128)S(1)} %bitcast.8), custom_call_target="tpu_custom_call" | custom-call | tf_op jit(solution)/shard_map/inject/pallas_call | solution.py:132
  6.9 5.1 %collective-permute-start = (bf16[8,30208]{1,0:T(8,128)(2,1)S(1)}, bf16[8,30208]{1,0:T(8,128)(2,1)S(1)}, u32[]{:S(2)}, u32[]{:S(2)}) collective-permute-start(bf16[8,30208]{1,0:T(8,128)(2,1)S(1)} %inject.1.refs_0_), channel_id=1, source_target_pairs={{0,24},{2,26},{4,28},{6,30},{8,0},{10,2},{12,4},{14,6},{16,8},{18,... | collective-permute-start | bytes 1449992 | tf_op jit(solution)/shard_map/ppermute | solution.py:216
  12.0 1.5 collective-permute-start.1
  13.5 1.5 collective-permute-start.2
  15.0 7.3 %collective-permute-done.refs_1_ = bf16[8,30208]{1,0:T(8,128)(2,1)S(1)} collective-permute-done((bf16[8,30208]{1,0:T(8,128)(2,1)S(1)}, bf16[8,30208]{1,0:T(8,128)(2,1)S(1)}, u32[]{:S(2)}, u32[]{:S(2)}) %collective-permute-start) | collective-permute-done | bytes 483360 | tf_op jit(solution)/shard_map/ppermute | solution.py:216
  22.3 2.2 %collective-permute-done.1.refs_2_ = bf16[8,30208]{1,0:T(8,128)(2,1)S(1)} collective-permute-done((bf16[8,30208]{1,0:T(8,128)(2,1)S(1)}, bf16[8,30208]{1,0:T(8,128)(2,1)S(1)}, u32[]{:S(2)}, u32[]{:S(2)}) %collective-permute-start.1) | collective-permute-done | bytes 483360 | tf_op jit(solution)/shard_map/ppermute | solution.py:216
  24.5 1.5 collective-permute-start.4
  26.0 1.5 collective-permute-start.5
  27.5 2.1 %collective-permute-start.3 = (bf16[8,30208]{1,0:T(8,128)(2,1)S(1)}, bf16[8,30208]{1,0:T(8,128)(2,1)S(1)}, u32[]{:S(2)}, u32[]{:S(2)}) collective-permute-start(bf16[8,30208]{1,0:T(8,128)(2,1)S(1)} %collective-permute-done.refs_1_), channel_id=1, source_target_pairs={{0,24},{2,26},{4,28},{6,30},{8,0},{10,2},{12,4},{14,6},{16,8},{18,... | collective-permute-start | bytes 1449992 | tf_op jit(solution)/shard_map/ppermute | solution.py:216
  29.6 6.5 %collective-permute-done.4.refs_5_ = bf16[8,30208]{1,0:T(8,128)(2,1)S(1)} collective-permute-done((bf16[8,30208]{1,0:T(8,128)(2,1)S(1)}, bf16[8,30208]{1,0:T(8,128)(2,1)S(1)}, u32[]{:S(2)}, u32[]{:S(2)}) %collective-permute-start.4) | collective-permute-done | bytes 483360 | tf_op jit(solution)/shard_map/ppermute | solution.py:216
  36.1 1.2 collective-permute-done.5.refs_6_
  37.3 1.5 collective-permute-start.8
  38.9 1.4 collective-permute-done.3.refs_4_
  40.2 7.5 %collective-permute-done.8.refs_9_ = bf16[8,30208]{1,0:T(8,128)(2,1)S(1)} collective-permute-done((bf16[8,30208]{1,0:T(8,128)(2,1)S(1)}, bf16[8,30208]{1,0:T(8,128)(2,1)S(1)}, u32[]{:S(2)}, u32[]{:S(2)}) %collective-permute-start.8) | collective-permute-done | bytes 483360 | tf_op jit(solution)/shard_map/ppermute | solution.py:216
  47.7 1.2 collective-permute-done.7.refs_8_
  49.0 2.7 %collective-permute-done.6.refs_7_ = bf16[8,30208]{1,0:T(8,128)(2,1)S(1)} collective-permute-done((bf16[8,30208]{1,0:T(8,128)(2,1)S(1)}, bf16[8,30208]{1,0:T(8,128)(2,1)S(1)}, u32[]{:S(2)}, u32[]{:S(2)}) %collective-permute-start.6) | collective-permute-done | bytes 483360 | tf_op jit(solution)/shard_map/ppermute | solution.py:216
  51.7 3.2 %copy-done = bf16[128,30208]{1,0:T(8,128)(2,1)S(1)} copy-done((bf16[128,30208]{1,0:T(8,128)(2,1)S(1)}, bf16[128,30208]{1,0:T(8,128)(2,1)}, u32[]{:S(2)}) %copy-start) | copy-done | bytes 7733272
  54.9 3.9 %flows.3 = f32[80,128]{1,0:T(8,128)S(1)} custom-call(bf16[8,30208]{1,0:T(8,128)(2,1)S(1)} %inject.1.refs_0_, bf16[8,30208]{1,0:T(8,128)(2,1)S(1)} %collective-permute-done.refs_1_, bf16[8,30208]{1,0:T(8,128)(2,1)S(1)} %collective-permute-done.1.refs_2_, bf16[8,30208]{1,0:T(8,128)(2,1)S(1)} %collective-permute-done.2.refs_3_, ...), custom_call_target="tpu_custom_call" | custom-call | flops 618659840 | bytes 12566528 | tf_op jit(solution)/shard_map/flows/pallas_call | solution.py:169
  59.0 0.6 collective-permute-start.16
  59.5 1.5 collective-permute-start.14
  61.1 3.6 %fusion.41 = (bf16[80,30208]{1,0:T(8,128)(2,1)}, f32[80,30208]{1,0:T(8,128)S(1)}) fusion(bf16[128,30208]{1,0:T(8,128)(2,1)S(1)} %copy-done, f32[80,128]{1,0:T(8,128)S(1)} %flows.3, f32[80,128]{1,0:T(8,128)S(1)} %collective-permute-done.9, f32[128]{0:T(128)S(1)} %get-tuple-element.61, f32[128]{0:T(128)S(1)} %get-tuple-element.60), kind=kOutput, calls=%fused_computation.61 | convolution fusion | flops 621230080 | bytes 22316032 | tf_op jit(solution)/shard_map/dot_general | solution.py:209
  64.7 7.8 %collective-permute-done.16.refs_2_ = bf16[8,30208]{1,0:T(8,128)(2,1)S(1)} collective-permute-done((bf16[8,30208]{1,0:T(8,128)(2,1)S(1)}, bf16[8,30208]{1,0:T(8,128)(2,1)S(1)}, u32[]{:S(2)}, u32[]{:S(2)}) %collective-permute-start.16) | collective-permute-done | bytes 483360 | tf_op jit(solution)/shard_map/ppermute | solution.py:216
  72.5 0.2 collective-permute-done.14.refs_1_
  72.7 3.0 %collective-permute-done.10.refs_0_ = bf16[8,30208]{1,0:T(8,128)(2,1)S(1)} collective-permute-done((bf16[8,30208]{1,0:T(8,128)(2,1)S(1)}, bf16[8,30208]{1,0:T(8,128)(2,1)S(1)}, u32[]{:S(2)}, u32[]{:S(2)}) %collective-permute-start.10) | collective-permute-done | bytes 483360 | tf_op jit(solution)/shard_map/ppermute | solution.py:216
  75.7 3.5 %flows.5 = f32[24,128]{1,0:T(8,128)S(1)} custom-call(bf16[8,30208]{1,0:T(8,128)(2,1)S(1)} %collective-permute-done.10.refs_0_, bf16[8,30208]{1,0:T(8,128)(2,1)S(1)} %collective-permute-done.14.refs_1_, bf16[8,30208]{1,0:T(8,128)(2,1)S(1)} %collective-permute-done.16.refs_2_, bf16[128,30208]{1,0:T(8,128)(2,1)S(1)} %bitcast.7), custom_call_target="tpu_custom_call" | custom-call | flops 185597952 | bytes 9183232 | tf_op jit(solution)/shard_map/flows/pallas_call | solution.py:169
  79.4 1.6 fusion.38
  81.0 1.6 collective-permute-start.17
  82.6 0.5 collective-permute-start.15
  83.1 1.1 fusion.42
  84.2 10.3 %collective-permute-done.17.refs_2_ = bf16[8,30208]{1,0:T(8,128)(2,1)S(1)} collective-permute-done((bf16[8,30208]{1,0:T(8,128)(2,1)S(1)}, bf16[8,30208]{1,0:T(8,128)(2,1)S(1)}, u32[]{:S(2)}, u32[]{:S(2)}) %collective-permute-start.17) | collective-permute-done | bytes 483360 | tf_op jit(solution)/shard_map/ppermute | solution.py:216
  94.5 1.2 collective-permute-done.15.refs_1_
  95.7 2.0 %collective-permute-done.11.refs_0_ = bf16[8,30208]{1,0:T(8,128)(2,1)S(1)} collective-permute-done((bf16[8,30208]{1,0:T(8,128)(2,1)S(1)}, bf16[8,30208]{1,0:T(8,128)(2,1)S(1)}, u32[]{:S(2)}, u32[]{:S(2)}) %collective-permute-start.11) | collective-permute-done | bytes 483360 | tf_op jit(solution)/shard_map/ppermute | solution.py:216
  97.7 3.5 %flows.4 = f32[24,128]{1,0:T(8,128)S(1)} custom-call(bf16[8,30208]{1,0:T(8,128)(2,1)S(1)} %collective-permute-done.11.refs_0_, bf16[8,30208]{1,0:T(8,128)(2,1)S(1)} %collective-permute-done.15.refs_1_, bf16[8,30208]{1,0:T(8,128)(2,1)S(1)} %collective-permute-done.17.refs_2_, bf16[128,30208]{1,0:T(8,128)(2,1)S(1)} %bitcast.7), custom_call_target="tpu_custom_call" | custom-call | flops 185597952 | bytes 9183232 | tf_op jit(solution)/shard_map/flows/pallas_call | solution.py:169
  101.5 0.6 collective-permute-start.23
  102.0 1.5 collective-permute-start.19
  103.6 1.1 fusion.43
  104.8 10.2 %collective-permute-done.23 = bf16[8,30208]{1,0:T(8,128)(2,1)S(1)} collective-permute-done((bf16[8,30208]{1,0:T(8,128)(2,1)S(1)}, bf16[8,30208]{1,0:T(8,128)(2,1)S(1)}, u32[]{:S(2)}, u32[]{:S(2)}) %collective-permute-start.23) | collective-permute-done | bytes 483360 | tf_op jit(solution)/shard_map/ppermute | solution.py:226
  115.0 0.5 collective-permute-start.24
  115.5 1.5 collective-permute-start.22
  117.0 1.2 collective-permute-done.12
  118.3 9.3 %collective-permute-done.24 = bf16[8,30208]{1,0:T(8,128)(2,1)S(1)} collective-permute-done((bf16[8,30208]{1,0:T(8,128)(2,1)S(1)}, bf16[8,30208]{1,0:T(8,128)(2,1)S(1)}, u32[]{:S(2)}, u32[]{:S(2)}) %collective-permute-start.24) | collective-permute-done | bytes 483360 | tf_op jit(solution)/shard_map/ppermute | solution.py:226
  127.6 0.5 collective-permute-start.25
  128.3 1.6 collective-permute-start.28
  129.9 2.2 %collective-permute-done.13 = bf16[8,30208]{1,0:T(8,128)(2,1)S(1)} collective-permute-done((bf16[8,30208]{1,0:T(8,128)(2,1)S(1)}, bf16[8,30208]{1,0:T(8,128)(2,1)S(1)}, u32[]{:S(2)}, u32[]{:S(2)}) %collective-permute-start.13) | collective-permute-done | bytes 483360 | tf_op jit(solution)/shard_map/ppermute | solution.py:226
  132.1 7.3 %collective-permute-done.25 = bf16[8,30208]{1,0:T(8,128)(2,1)S(1)} collective-permute-done((bf16[8,30208]{1,0:T(8,128)(2,1)S(1)}, bf16[8,30208]{1,0:T(8,128)(2,1)S(1)}, u32[]{:S(2)}, u32[]{:S(2)}) %collective-permute-start.25) | collective-permute-done | bytes 483360 | tf_op jit(solution)/shard_map/ppermute | solution.py:226
  139.4 0.4 collective-permute-done.28
  139.8 5.4 %collective-permute-done.20 = bf16[8,30208]{1,0:T(8,128)(2,1)S(1)} collective-permute-done((bf16[8,30208]{1,0:T(8,128)(2,1)S(1)}, bf16[8,30208]{1,0:T(8,128)(2,1)S(1)}, u32[]{:S(2)}, u32[]{:S(2)}) %collective-permute-start.20) | collective-permute-done | bytes 483360 | tf_op jit(solution)/shard_map/ppermute | solution.py:226
  145.2 0.5 fusion.10
  145.7 2.6 %collective-permute-start.26 = (bf16[8,30208]{1,0:T(8,128)(2,1)S(1)}, bf16[8,30208]{1,0:T(8,128)(2,1)S(1)}, u32[]{:S(2)}, u32[]{:S(2)}) collective-permute-start(bf16[8,30208]{1,0:T(8,128)(2,1)S(1)} %get-tuple-element.49), channel_id=1, source_target_pairs={{0,4},{2,6},{4,0},{6,2},{8,12},{10,14},{12,8},{14,10},{16,20},{18,... | collective-permute-start | bytes 1449992 | tf_op jit(solution)/shard_map/ppermute | solution.py:226
  148.3 9.2 %collective-permute-done.26 = bf16[8,30208]{1,0:T(8,128)(2,1)S(1)} collective-permute-done((bf16[8,30208]{1,0:T(8,128)(2,1)S(1)}, bf16[8,30208]{1,0:T(8,128)(2,1)S(1)}, u32[]{:S(2)}, u32[]{:S(2)}) %collective-permute-start.26) | collective-permute-done | bytes 483360 | tf_op jit(solution)/shard_map/ppermute | solution.py:226
  157.5 2.0 %collective-permute-start.27 = (bf16[8,30208]{1,0:T(8,128)(2,1)S(1)}, bf16[8,30208]{1,0:T(8,128)(2,1)S(1)}, u32[]{:S(2)}, u32[]{:S(2)}) collective-permute-start(bf16[8,30208]{1,0:T(8,128)(2,1)S(1)} %get-tuple-element.50), channel_id=1, source_target_pairs={{0,4},{2,6},{4,0},{6,2},{8,12},{10,14},{12,8},{14,10},{16,20},{18,... | collective-permute-start | bytes 1449992 | tf_op jit(solution)/shard_map/ppermute | solution.py:226
  159.6 0.2 fusion.4
  159.9 6.4 %collective-permute-done.27 = bf16[8,30208]{1,0:T(8,128)(2,1)S(1)} collective-permute-done((bf16[8,30208]{1,0:T(8,128)(2,1)S(1)}, bf16[8,30208]{1,0:T(8,128)(2,1)S(1)}, u32[]{:S(2)}, u32[]{:S(2)}) %collective-permute-start.27) | collective-permute-done | bytes 483360 | tf_op jit(solution)/shard_map/ppermute | solution.py:226
  166.3 2.0 %collective-permute-done.30 = bf16[8,30208]{1,0:T(8,128)(2,1)S(1)} collective-permute-done((bf16[8,30208]{1,0:T(8,128)(2,1)S(1)}, bf16[8,30208]{1,0:T(8,128)(2,1)S(1)}, u32[]{:S(2)}, u32[]{:S(2)}) %collective-permute-start.30) | collective-permute-done | bytes 483360 | tf_op jit(solution)/shard_map/ppermute | solution.py:226
  168.3 0.3 collective-permute-done.32
  168.6 0.3 fusion.13
  168.9 8.4 %copy.12 = f32[8,30208]{0,1:T(8,128)} copy(f32[8,30208]{1,0:T(8,128)S(1)} %fusion.13) | data formatting | bytes 1933312 | tf_op jit(solution)/shard_map/add | solution.py:228
  177.3 8.2 %gather_fusion = f32[1024,8]{1,0:T(8,128)S(1)} fusion(f32[8,30208]{0,1:T(8,128)} %copy.12, s32[1024]{0:T(1024)S(1)} %get-tuple-element.74), kind=kCustom, calls=%fused_computation | custom fusion | bytes 69632 | tf_op jit(solution)/shard_map/gather | solution.py:230
  185.7 4.5 %psum.7 = f32[8,1024]{0,1:T(8,128)S(1)} all-reduce(f32[8,1024]{0,1:T(8,128)S(1)} %multiply_bitcast_fusion), channel_id=1, replica_groups=mesh['br'=16,'bus'=2] {'bus'}, use_global_device_ids=true, to_apply=%region_2.3 | all-reduce | flops 8192 | bytes 65536 | tf_op jit(solution)/shard_map/psum | solution.py:231
  190.2 0.8 copy.13
  (43 shorter events, 1.0 us)
Async XLA Ops:
  0.6 58.2 %copy-start.4 = (s32[128]{0:T(128)S(1)}, s32[128]{0:T(128)}, u32[]{:S(2)}) copy-start(s32[128]{0:T(128)} %param.13) | copy-start | bytes 1540
  0.6 58.2 %copy-start.5 = (f32[16]{0:T(128)S(1)}, f32[16]{0:T(128)}, u32[]{:S(2)}) copy-start(f32[16]{0:T(128)} %param.14) | copy-start | bytes 196
  0.7 58.2 %copy-start.3 = (f32[16]{0:T(128)S(1)}, f32[16]{0:T(128)}, u32[]{:S(2)}) copy-start(f32[16]{0:T(128)} %param.15) | copy-start | bytes 196
  2.8 1.0 copy-start.1
  6.9 15.4 %collective-permute-start = (bf16[8,30208]{1,0:T(8,128)(2,1)S(1)}, bf16[8,30208]{1,0:T(8,128)(2,1)S(1)}, u32[]{:S(2)}, u32[]{:S(2)}) collective-permute-start(bf16[8,30208]{1,0:T(8,128)(2,1)S(1)} %inject.1.refs_0_), channel_id=1, source_target_pairs={{0,24},{2,26},{4,28},{6,30},{8,0},{10,2},{12,4},{14,6},{16,8},{18,... | collective-permute-start | bytes 1449992 | tf_op jit(solution)/shard_map/ppermute | solution.py:216
  12.0 12.5 %collective-permute-start.1 = (bf16[8,30208]{1,0:T(8,128)(2,1)S(1)}, bf16[8,30208]{1,0:T(8,128)(2,1)S(1)}, u32[]{:S(2)}, u32[]{:S(2)}) collective-permute-start(bf16[8,30208]{1,0:T(8,128)(2,1)S(1)} %inject.1.refs_0_), channel_id=1, source_target_pairs={{0,2},{2,0},{4,6},{6,4},{8,10},{10,8},{12,14},{14,12},{16,18},{18,... | collective-permute-start | bytes 1449992 | tf_op jit(solution)/shard_map/ppermute | solution.py:216
  13.5 12.5 %collective-permute-start.2 = (bf16[8,30208]{1,0:T(8,128)(2,1)S(1)}, bf16[8,30208]{1,0:T(8,128)(2,1)S(1)}, u32[]{:S(2)}, u32[]{:S(2)}) collective-permute-start(bf16[8,30208]{1,0:T(8,128)(2,1)S(1)} %inject.1.refs_0_), channel_id=1, source_target_pairs={{0,4},{2,6},{4,0},{6,2},{8,12},{10,14},{12,8},{14,10},{16,20},{18,... | collective-permute-start | bytes 1449992 | tf_op jit(solution)/shard_map/ppermute | solution.py:216
  24.5 11.6 %collective-permute-start.4 = (bf16[8,30208]{1,0:T(8,128)(2,1)S(1)}, bf16[8,30208]{1,0:T(8,128)(2,1)S(1)}, u32[]{:S(2)}, u32[]{:S(2)}) collective-permute-start(bf16[8,30208]{1,0:T(8,128)(2,1)S(1)} %collective-permute-done.refs_1_), channel_id=1, source_target_pairs={{0,2},{2,0},{4,6},{6,4},{8,10},{10,8},{12,14},{14,12},{16,18},{18,... | collective-permute-start | bytes 1449992 | tf_op jit(solution)/shard_map/ppermute | solution.py:216
  26.0 11.3 %collective-permute-start.5 = (bf16[8,30208]{1,0:T(8,128)(2,1)S(1)}, bf16[8,30208]{1,0:T(8,128)(2,1)S(1)}, u32[]{:S(2)}, u32[]{:S(2)}) collective-permute-start(bf16[8,30208]{1,0:T(8,128)(2,1)S(1)} %collective-permute-done.1.refs_2_), channel_id=1, source_target_pairs={{0,4},{2,6},{4,0},{6,2},{8,12},{10,14},{12,8},{14,10},{16,20},{18,... | collective-permute-start | bytes 1449992 | tf_op jit(solution)/shard_map/ppermute | solution.py:216
  27.5 12.7 %collective-permute-start.3 = (bf16[8,30208]{1,0:T(8,128)(2,1)S(1)}, bf16[8,30208]{1,0:T(8,128)(2,1)S(1)}, u32[]{:S(2)}, u32[]{:S(2)}) collective-permute-start(bf16[8,30208]{1,0:T(8,128)(2,1)S(1)} %collective-permute-done.refs_1_), channel_id=1, source_target_pairs={{0,24},{2,26},{4,28},{6,30},{8,0},{10,2},{12,4},{14,6},{16,8},{18,... | collective-permute-start | bytes 1449992 | tf_op jit(solution)/shard_map/ppermute | solution.py:216
  37.3 10.4 %collective-permute-start.8 = (bf16[8,30208]{1,0:T(8,128)(2,1)S(1)}, bf16[8,30208]{1,0:T(8,128)(2,1)S(1)}, u32[]{:S(2)}, u32[]{:S(2)}) collective-permute-start(bf16[8,30208]{1,0:T(8,128)(2,1)S(1)} %collective-permute-done.4.refs_5_), channel_id=1, source_target_pairs={{0,4},{2,6},{4,0},{6,2},{8,12},{10,14},{12,8},{14,10},{16,20},{18,... | collective-permute-start | bytes 1449992 | tf_op jit(solution)/shard_map/ppermute | solution.py:216
  40.2 8.8 %collective-permute-start.7 = (bf16[8,30208]{1,0:T(8,128)(2,1)S(1)}, bf16[8,30208]{1,0:T(8,128)(2,1)S(1)}, u32[]{:S(2)}, u32[]{:S(2)}) collective-permute-start(bf16[8,30208]{1,0:T(8,128)(2,1)S(1)} %collective-permute-done.3.refs_4_), channel_id=1, source_target_pairs={{0,2},{2,0},{4,6},{6,4},{8,10},{10,8},{12,14},{14,12},{16,18},{18,... | collective-permute-start | bytes 1449992 | tf_op jit(solution)/shard_map/ppermute | solution.py:216
  40.2 11.5 %collective-permute-start.6 = (bf16[8,30208]{1,0:T(8,128)(2,1)S(1)}, bf16[8,30208]{1,0:T(8,128)(2,1)S(1)}, u32[]{:S(2)}, u32[]{:S(2)}) collective-permute-start(bf16[8,30208]{1,0:T(8,128)(2,1)S(1)} %collective-permute-done.2.refs_3_), channel_id=1, source_target_pairs={{0,8},{2,10},{4,12},{6,14},{8,16},{10,18},{12,20},{14,22},{16,24},... | collective-permute-start | bytes 1449992 | tf_op jit(solution)/shard_map/ppermute | solution.py:216
  51.7 3.2 %copy-start = (bf16[128,30208]{1,0:T(8,128)(2,1)S(1)}, bf16[128,30208]{1,0:T(8,128)(2,1)}, u32[]{:S(2)}) copy-start(bf16[128,30208]{1,0:T(8,128)(2,1)} %refs_3_.3) | copy-start | bytes 23199748
  54.9 20.8 %slice-start = ((s8[7733248]{0:T(1024)(128)(4,1)}), s8[3538944]{0:T(1024)(128)(4,1)S(1)}, s32[]{:S(2)}) async-start(s8[7733248]{0:T(1024)(128)(4,1)} %bitcast.6), calls=%async_computation | async-start | bytes 7077888
  58.8 2.3 %collective-permute-start.9 = (f32[80,128]{1,0:T(8,128)S(1)}, f32[80,128]{1,0:T(8,128)S(1)}, u32[]{:S(2)}, u32[]{:S(2)}) collective-permute-start(f32[80,128]{1,0:T(8,128)S(1)} %flows.3), channel_id=1, source_target_pairs={{0,1},{1,0},{2,3},{3,2},{4,5},{5,4},{6,7},{7,6},{8,9},{9,8},{10,11... | collective-permute-start | bytes 122888 | tf_op jit(solution)/shard_map/ppermute | solution.py:203
  59.0 13.5 %collective-permute-start.16 = (bf16[8,30208]{1,0:T(8,128)(2,1)S(1)}, bf16[8,30208]{1,0:T(8,128)(2,1)S(1)}, u32[]{:S(2)}, u32[]{:S(2)}) collective-permute-start(bf16[8,30208]{1,0:T(8,128)(2,1)S(1)} %collective-permute-done.7.refs_8_), channel_id=1, source_target_pairs={{0,4},{2,6},{4,0},{6,2},{8,12},{10,14},{12,8},{14,10},{16,20},{18,... | collective-permute-start | bytes 1449992 | tf_op jit(solution)/shard_map/ppermute | solution.py:216
  59.5 13.1 %collective-permute-start.14 = (bf16[8,30208]{1,0:T(8,128)(2,1)S(1)}, bf16[8,30208]{1,0:T(8,128)(2,1)S(1)}, u32[]{:S(2)}, u32[]{:S(2)}) collective-permute-start(bf16[8,30208]{1,0:T(8,128)(2,1)S(1)} %collective-permute-done.6.refs_7_), channel_id=1, source_target_pairs={{0,2},{2,0},{4,6},{6,4},{8,10},{10,8},{12,14},{14,12},{16,18},{18,... | collective-permute-start | bytes 1449992 | tf_op jit(solution)/shard_map/ppermute | solution.py:216
  61.1 14.7 %collective-permute-start.10 = (bf16[8,30208]{1,0:T(8,128)(2,1)S(1)}, bf16[8,30208]{1,0:T(8,128)(2,1)S(1)}, u32[]{:S(2)}, u32[]{:S(2)}) collective-permute-start(bf16[8,30208]{1,0:T(8,128)(2,1)S(1)} %inject.1.refs_0_), channel_id=1, source_target_pairs={{0,8},{2,10},{4,12},{6,14},{8,16},{10,18},{12,20},{14,22},{16,24},... | collective-permute-start | bytes 1449992 | tf_op jit(solution)/shard_map/ppermute | solution.py:216
  61.1 14.7 %slice-start.1 = ((s8[7733248]{0:T(1024)(128)(4,1)}), s8[4194304]{0:T(1024)(128)(4,1)S(1)}, s32[]{:S(2)}) async-start(s8[7733248]{0:T(1024)(128)(4,1)} %bitcast.6), calls=%async_computation.1 | async-start | bytes 8388608
  79.3 3.8 %collective-permute-start.21 = (f32[24,128]{1,0:T(8,128)S(1)}, f32[24,128]{1,0:T(8,128)S(1)}, u32[]{:S(2)}, u32[]{:S(2)}) collective-permute-start(f32[24,128]{1,0:T(8,128)S(1)} %flows.5), channel_id=1, source_target_pairs={{0,1},{1,0},{2,3},{3,2},{4,5},{5,4},{6,7},{7,6},{8,9},{9,8},{10,11... | collective-permute-start | bytes 36872 | tf_op jit(solution)/shard_map/ppermute | solution.py:203
  81.0 13.5 %collective-permute-start.17 = (bf16[8,30208]{1,0:T(8,128)(2,1)S(1)}, bf16[8,30208]{1,0:T(8,128)(2,1)S(1)}, u32[]{:S(2)}, u32[]{:S(2)}) collective-permute-start(bf16[8,30208]{1,0:T(8,128)(2,1)S(1)} %collective-permute-done.refs_1_), channel_id=1, source_target_pairs={{0,4},{2,6},{4,0},{6,2},{8,12},{10,14},{12,8},{14,10},{16,20},{18,... | collective-permute-start | bytes 1449992 | tf_op jit(solution)/shard_map/ppermute | solution.py:216
  82.6 13.2 %collective-permute-start.15 = (bf16[8,30208]{1,0:T(8,128)(2,1)S(1)}, bf16[8,30208]{1,0:T(8,128)(2,1)S(1)}, u32[]{:S(2)}, u32[]{:S(2)}) collective-permute-start(bf16[8,30208]{1,0:T(8,128)(2,1)S(1)} %collective-permute-done.10.refs_0_), channel_id=1, source_target_pairs={{0,2},{2,0},{4,6},{6,4},{8,10},{10,8},{12,14},{14,12},{16,18},{18,... | collective-permute-start | bytes 1449992 | tf_op jit(solution)/shard_map/ppermute | solution.py:216
  83.1 14.7 %collective-permute-start.11 = (bf16[8,30208]{1,0:T(8,128)(2,1)S(1)}, bf16[8,30208]{1,0:T(8,128)(2,1)S(1)}, u32[]{:S(2)}, u32[]{:S(2)}) collective-permute-start(bf16[8,30208]{1,0:T(8,128)(2,1)S(1)} %collective-permute-done.6.refs_7_), channel_id=1, source_target_pairs={{0,8},{2,10},{4,12},{6,14},{8,16},{10,18},{12,20},{14,22},{16,24},... | collective-permute-start | bytes 1449992 | tf_op jit(solution)/shard_map/ppermute | solution.py:216
  101.3 2.3 %collective-permute-start.18 = (f32[24,128]{1,0:T(8,128)S(1)}, f32[24,128]{1,0:T(8,128)S(1)}, u32[]{:S(2)}, u32[]{:S(2)}) collective-permute-start(f32[24,128]{1,0:T(8,128)S(1)} %flows.4), channel_id=1, source_target_pairs={{0,1},{1,0},{2,3},{3,2},{4,5},{5,4},{6,7},{7,6},{8,9},{9,8},{10,11... | collective-permute-start | bytes 36872 | tf_op jit(solution)/shard_map/ppermute | solution.py:203
  101.5 13.5 %collective-permute-start.23 = (bf16[8,30208]{1,0:T(8,128)(2,1)S(1)}, bf16[8,30208]{1,0:T(8,128)(2,1)S(1)}, u32[]{:S(2)}, u32[]{:S(2)}) collective-permute-start(bf16[8,30208]{1,0:T(8,128)(2,1)S(1)} %get-tuple-element.46), channel_id=1, source_target_pairs={{0,4},{2,6},{4,0},{6,2},{8,12},{10,14},{12,8},{14,10},{16,20},{18,... | collective-permute-start | bytes 1449992 | tf_op jit(solution)/shard_map/ppermute | solution.py:226
  102.0 13.4 %collective-permute-start.19 = (bf16[8,30208]{1,0:T(8,128)(2,1)S(1)}, bf16[8,30208]{1,0:T(8,128)(2,1)S(1)}, u32[]{:S(2)}, u32[]{:S(2)}) collective-permute-start(bf16[8,30208]{1,0:T(8,128)(2,1)S(1)} %get-tuple-element.43), channel_id=1, source_target_pairs={{0,2},{2,0},{4,6},{6,4},{8,10},{10,8},{12,14},{14,12},{16,18},{18,... | collective-permute-start | bytes 1449992 | tf_op jit(solution)/shard_map/ppermute | solution.py:226
  103.6 14.7 %collective-permute-start.12 = (bf16[8,30208]{1,0:T(8,128)(2,1)S(1)}, bf16[8,30208]{1,0:T(8,128)(2,1)S(1)}, u32[]{:S(2)}, u32[]{:S(2)}) collective-permute-start(bf16[8,30208]{1,0:T(8,128)(2,1)S(1)} %get-tuple-element.37), channel_id=1, source_target_pairs={{0,8},{2,10},{4,12},{6,14},{8,16},{10,18},{12,20},{14,22},{16,24},... | collective-permute-start | bytes 1449992 | tf_op jit(solution)/shard_map/ppermute | solution.py:226
  115.0 12.7 %collective-permute-start.24 = (bf16[8,30208]{1,0:T(8,128)(2,1)S(1)}, bf16[8,30208]{1,0:T(8,128)(2,1)S(1)}, u32[]{:S(2)}, u32[]{:S(2)}) collective-permute-start(bf16[8,30208]{1,0:T(8,128)(2,1)S(1)} %get-tuple-element.47), channel_id=1, source_target_pairs={{0,4},{2,6},{4,0},{6,2},{8,12},{10,14},{12,8},{14,10},{16,20},{18,... | collective-permute-start | bytes 1449992 | tf_op jit(solution)/shard_map/ppermute | solution.py:226
  115.5 12.8 %collective-permute-start.22 = (bf16[8,30208]{1,0:T(8,128)(2,1)S(1)}, bf16[8,30208]{1,0:T(8,128)(2,1)S(1)}, u32[]{:S(2)}, u32[]{:S(2)}) collective-permute-start(bf16[8,30208]{1,0:T(8,128)(2,1)S(1)} %get-tuple-element.45), channel_id=1, source_target_pairs={{0,2},{2,0},{4,6},{6,4},{8,10},{10,8},{12,14},{14,12},{16,18},{18,... | collective-permute-start | bytes 1449992 | tf_op jit(solution)/shard_map/ppermute | solution.py:226
  118.2 13.8 %collective-permute-start.13 = (bf16[8,30208]{1,0:T(8,128)(2,1)S(1)}, bf16[8,30208]{1,0:T(8,128)(2,1)S(1)}, u32[]{:S(2)}, u32[]{:S(2)}) collective-permute-start(bf16[8,30208]{1,0:T(8,128)(2,1)S(1)} %get-tuple-element.38), channel_id=1, source_target_pairs={{0,8},{2,10},{4,12},{6,14},{8,16},{10,18},{12,20},{14,22},{16,24},... | collective-permute-start | bytes 1449992 | tf_op jit(solution)/shard_map/ppermute | solution.py:226
  127.6 11.8 %collective-permute-start.25 = (bf16[8,30208]{1,0:T(8,128)(2,1)S(1)}, bf16[8,30208]{1,0:T(8,128)(2,1)S(1)}, u32[]{:S(2)}, u32[]{:S(2)}) collective-permute-start(bf16[8,30208]{1,0:T(8,128)(2,1)S(1)} %get-tuple-element.48), channel_id=1, source_target_pairs={{0,4},{2,6},{4,0},{6,2},{8,12},{10,14},{12,8},{14,10},{16,20},{18,... | collective-permute-start | bytes 1449992 | tf_op jit(solution)/shard_map/ppermute | solution.py:226
  128.3 11.6 %collective-permute-start.28 = (bf16[8,30208]{1,0:T(8,128)(2,1)S(1)}, bf16[8,30208]{1,0:T(8,128)(2,1)S(1)}, u32[]{:S(2)}, u32[]{:S(2)}) collective-permute-start(bf16[8,30208]{1,0:T(8,128)(2,1)S(1)} %fusion.5), channel_id=1, source_target_pairs={{0,2},{2,0},{4,6},{6,4},{8,10},{10,8},{12,14},{14,12},{16,18},{18,... | collective-permute-start | bytes 1449992 | tf_op jit(solution)/shard_map/ppermute | solution.py:226
  132.0 13.2 %collective-permute-start.20 = (bf16[8,30208]{1,0:T(8,128)(2,1)S(1)}, bf16[8,30208]{1,0:T(8,128)(2,1)S(1)}, u32[]{:S(2)}, u32[]{:S(2)}) collective-permute-start(bf16[8,30208]{1,0:T(8,128)(2,1)S(1)} %fusion.9), channel_id=1, source_target_pairs={{0,8},{2,10},{4,12},{6,14},{8,16},{10,18},{12,20},{14,22},{16,24},... | collective-permute-start | bytes 1449992 | tf_op jit(solution)/shard_map/ppermute | solution.py:226
  145.7 11.8 %collective-permute-start.26 = (bf16[8,30208]{1,0:T(8,128)(2,1)S(1)}, bf16[8,30208]{1,0:T(8,128)(2,1)S(1)}, u32[]{:S(2)}, u32[]{:S(2)}) collective-permute-start(bf16[8,30208]{1,0:T(8,128)(2,1)S(1)} %get-tuple-element.49), channel_id=1, source_target_pairs={{0,4},{2,6},{4,0},{6,2},{8,12},{10,14},{12,8},{14,10},{16,20},{18,... | collective-permute-start | bytes 1449992 | tf_op jit(solution)/shard_map/ppermute | solution.py:226
  148.3 11.2 %collective-permute-start.29 = (bf16[8,30208]{1,0:T(8,128)(2,1)S(1)}, bf16[8,30208]{1,0:T(8,128)(2,1)S(1)}, u32[]{:S(2)}, u32[]{:S(2)}) collective-permute-start(bf16[8,30208]{1,0:T(8,128)(2,1)S(1)} %get-tuple-element.52), channel_id=1, source_target_pairs={{0,2},{2,0},{4,6},{6,4},{8,10},{10,8},{12,14},{14,12},{16,18},{18,... | collective-permute-start | bytes 1449992 | tf_op jit(solution)/shard_map/ppermute | solution.py:226
  148.3 11.2 %collective-permute-start.31 = (bf16[8,30208]{1,0:T(8,128)(2,1)S(1)}, bf16[8,30208]{1,0:T(8,128)(2,1)S(1)}, u32[]{:S(2)}, u32[]{:S(2)}) collective-permute-start(bf16[8,30208]{1,0:T(8,128)(2,1)S(1)} %get-tuple-element.54), channel_id=1, source_target_pairs={{0,24},{2,26},{4,28},{6,30},{8,0},{10,2},{12,4},{14,6},{16,8},{18,... | collective-permute-start | bytes 1449992 | tf_op jit(solution)/shard_map/ppermute | solution.py:226
  157.5 8.7 %collective-permute-start.27 = (bf16[8,30208]{1,0:T(8,128)(2,1)S(1)}, bf16[8,30208]{1,0:T(8,128)(2,1)S(1)}, u32[]{:S(2)}, u32[]{:S(2)}) collective-permute-start(bf16[8,30208]{1,0:T(8,128)(2,1)S(1)} %get-tuple-element.50), channel_id=1, source_target_pairs={{0,4},{2,6},{4,0},{6,2},{8,12},{10,14},{12,8},{14,10},{16,20},{18,... | collective-permute-start | bytes 1449992 | tf_op jit(solution)/shard_map/ppermute | solution.py:226
  159.5 8.7 %collective-permute-start.30 = (bf16[8,30208]{1,0:T(8,128)(2,1)S(1)}, bf16[8,30208]{1,0:T(8,128)(2,1)S(1)}, u32[]{:S(2)}, u32[]{:S(2)}) collective-permute-start(bf16[8,30208]{1,0:T(8,128)(2,1)S(1)} %get-tuple-element.53), channel_id=1, source_target_pairs={{0,2},{2,0},{4,6},{6,4},{8,10},{10,8},{12,14},{14,12},{16,18},{18,... | collective-permute-start | bytes 1449992 | tf_op jit(solution)/shard_map/ppermute | solution.py:226
  159.8 8.8 %collective-permute-start.32 = (bf16[8,30208]{1,0:T(8,128)(2,1)S(1)}, bf16[8,30208]{1,0:T(8,128)(2,1)S(1)}, u32[]{:S(2)}, u32[]{:S(2)}) collective-permute-start(bf16[8,30208]{1,0:T(8,128)(2,1)S(1)} %fusion.4), channel_id=1, source_target_pairs={{0,24},{2,26},{4,28},{6,30},{8,0},{10,2},{12,4},{14,6},{16,8},{18,... | collective-permute-start | bytes 1449992 | tf_op jit(solution)/shard_map/ppermute | solution.py:226
  168.9 8.4 %copy-start.2 = (f32[8,30208]{1,0:T(8,128)}, f32[8,30208]{1,0:T(8,128)S(1)}, u32[]{:S(2)}) copy-start(f32[8,30208]{1,0:T(8,128)S(1)} %fusion.13) | copy-start | bytes 2899972

commit v2 on v1

--- a/solution.py
+++ b/solution.py
@@ -94,16 +94,23 @@
     return 128 * max(n for n in range(1, 65) if groups % n == 0)
 
 
-def inject_kernel(net_ref, weight_ref, column_ref, out_ref):
+def scatter_lanes(column):
+    lane = lax.broadcasted_iota(jnp.int32, (128, column.shape[1]), 0)
+    return jnp.where(lane == column % 128, 1.0, 0.0).astype(jnp.bfloat16)
+
+
+def split_high(value):
+    high = value.astype(jnp.bfloat16)
+    return high, (value - high.astype(jnp.float32)).astype(jnp.bfloat16)
+
+
+def inject_kernel(bus_ref, net_ref, release_ref, efficiency_ref, plant_ref, out_ref):
     rows, width = net_ref.shape
     groups = width // 128
-    column = column_ref[...]
-    place = jnp.where(column >= 0, column // 128, -1) - pl.program_id(0) * groups
-    weight = weight_ref[...]
-    high = weight.astype(jnp.bfloat16).astype(jnp.float32)
-    low = weight - high
-    lane = lax.broadcasted_iota(jnp.int32, (128, column.shape[1]), 0)
-    lanes = jnp.where(lane == column % 128, 1.0, 0.0).astype(jnp.bfloat16)
+    column = plant_ref[...]
+    place = column // 128 - (bus_ref[0] * pl.num_programs(0) + pl.program_id(0)) * groups
+    weight = release_ref[...] * efficiency_ref[...]
+    lanes = scatter_lanes(column)
 
     def spread(values):
         picked = [jnp.where(place == group, values, 0.0) for group in range(groups)]
@@ -114,34 +121,43 @@
             preferred_element_type=jnp.float32,
         )
 
-    added = spread(high) + spread(low)
+    high, low = split_high(weight)
+    added = spread(high.astype(jnp.float32)) + spread(low.astype(jnp.float32))
     for group in range(groups):
         at = slice(group * 128, (group + 1) * 128)
         total = net_ref[:, at].astype(jnp.float32) + added[group * rows : (group + 1) * rows]
         out_ref[:, at] = total.astype(jnp.bfloat16)
 
 
-def inject_of(net_load, weight, column):
+FREE = pl.CostEstimate(flops=0, bytes_accessed=0, transcendentals=0)
+LARGE = pltpu.CompilerParams(vmem_limit_bytes=20 << 20)
+
+
+def inject_of(bus, net_load, release, efficiency, plant_bus):
     rows, width = net_load.shape
     short = -rows % 8
     if short:
         net_load = jnp.pad(net_load, ((0, short), (0, 0)))
-        weight = jnp.pad(weight, ((0, short), (0, 0)))
+        release = jnp.pad(release, ((0, short), (0, 0)))
     tile = tile_of(width)
-    plants = weight.shape[1]
+    plants = release.shape[1]
+    whole = pl.BlockSpec((1, plants), lambda i: (0, 0))
     out = pl.pallas_call(
         inject_kernel,
         grid=(width // tile,),
         in_specs=[
+            pl.BlockSpec(memory_space=pltpu.SMEM),
             pl.BlockSpec((rows + short, tile), lambda i: (0, i)),
             pl.BlockSpec((rows + short, plants), lambda i: (0, 0)),
-            pl.BlockSpec((1, plants), lambda i: (0, 0)),
+            whole,
+            whole,
         ],
         out_specs=pl.BlockSpec((rows + short, tile), lambda i: (0, i)),
         out_shape=jax.ShapeDtypeStruct(net_load.shape, jnp.bfloat16),
-        compiler_params=pltpu.CompilerParams(vmem_limit_bytes=32 << 20),
+        compiler_params=LARGE,
+        cost_estimate=FREE,
         name="inject",
-    )(net_load, weight, column)
+    )(bus, net_load, release, efficiency[None, :], plant_bus[None, :])
     return out[:rows] if short else out
 
 
@@ -173,12 +189,91 @@
         + [pl.BlockSpec((branches, tile), lambda i: (0, i))],
         out_specs=pl.BlockSpec((total, branches), lambda i: (0, 0)),
         out_shape=jax.ShapeDtypeStruct((total, branches), jnp.float32),
-        compiler_params=pltpu.CompilerParams(vmem_limit_bytes=32 << 20),
-        cost_estimate=pl.CostEstimate(
-            flops=2 * total * branches * width, bytes_accessed=2 * (total + branches) * width, transcendentals=0
-        ),
+        compiler_params=LARGE,
+        cost_estimate=FREE,
         name="flows",
     )(*blocks, ptdf)
+
+
+def grad_flow_of(flows, limit, price):
+    upper = jax.nn.sigmoid((flows - limit) / SMOOTH)
+    lower = jax.nn.sigmoid((-flows - limit) / SMOOTH)
+    return (price * (upper - lower)).astype(jnp.bfloat16)
+
+
+def grads_kernel(rows, mine_ref, other_ref, limit_ref, price_ref, ptdf_ref, *out_refs):
+    grad_flow = grad_flow_of(mine_ref[...] + other_ref[...], limit_ref[...], price_ref[...])
+    part = jnp.dot(grad_flow, ptdf_ref[...], preferred_element_type=jnp.float32)
+    for index, out_ref in enumerate(out_refs):
+        out_ref[...] = part[index * rows : (index + 1) * rows].astype(out_ref.dtype)
+
+
+def grads_of(mine, other, limit, price, ptdf, rows, types):
+    branches, width = ptdf.shape
+    if rows % 8:
+        part = jnp.dot(grad_flow_of(mine + other, limit, price), ptdf, preferred_element_type=jnp.float32)
+        return [part[i * rows : (i + 1) * rows] for i in range(len(types))]
+    tile = tile_of(width)
+    flow_spec = pl.BlockSpec(mine.shape, lambda i: (0, 0))
+    class_spec = pl.BlockSpec((1, branches), lambda i: (0, 0))
+    return pl.pallas_call(
+        functools.partial(grads_kernel, rows),
+        grid=(width // tile,),
+        in_specs=[flow_spec, flow_spec, class_spec, class_spec, pl.BlockSpec((branches, tile), lambda i: (0, i))],
+        out_specs=[pl.BlockSpec((rows, tile), lambda i: (0, i)) for _ in types],
+        out_shape=[jax.ShapeDtypeStruct((rows, width), dtype) for dtype in types],
+        compiler_params=LARGE,
+        cost_estimate=FREE,
+        name="grads",
+    )(mine, other, limit, price, ptdf)
+
+
+def pick_kernel(bus_ref, grad_ref, plant_ref, out_ref):
+    rows, width = grad_ref.shape
+    groups = width // 128
+    column = plant_ref[...]
+    place = column // 128 - (bus_ref[0] * pl.num_programs(0) + pl.program_id(0)) * groups
+    lanes = scatter_lanes(column)
+    stacked = jnp.concatenate([grad_ref[:, g * 128 : (g + 1) * 128] for g in range(groups)], axis=0)
+    high, low = split_high(stacked)
+    found = jnp.dot(
+        jnp.concatenate([high, low], axis=1),
+        jnp.concatenate([lanes, lanes], axis=0),
+        preferred_element_type=jnp.float32,
+    )
+    total = jnp.zeros(out_ref.shape, jnp.float32)
+    for group in range(groups):
+        total += jnp.where(place == group, found[group * rows : (group + 1) * rows], 0.0)
+
+    @pl.when(pl.program_id(0) == 0)
+    def _():
+        out_ref[...] = jnp.zeros_like(out_ref)
+
+    out_ref[...] += total
+
+
+def pick_of(bus, grad, plant_bus):
+    rows, width = grad.shape
+    short = -rows % 8
+    if short:
+        grad = jnp.pad(grad, ((0, short), (0, 0)))
+    tile = tile_of(width)
+    plants = plant_bus.shape[0]
+    out = pl.pallas_call(
+        pick_kernel,
+        grid=(width // tile,),
+        in_specs=[
+            pl.BlockSpec(memory_space=pltpu.SMEM),
+            pl.BlockSpec((rows + short, tile), lambda i: (0, i)),
+            pl.BlockSpec((1, plants), lambda i: (0, 0)),
+        ],
+        out_specs=pl.BlockSpec((rows + short, plants), lambda i: (0, 0)),
+        out_shape=jax.ShapeDtypeStruct((rows + short, plants), jnp.float32),
+        compiler_params=LARGE,
+        cost_estimate=FREE,
+        name="pick",
+    )(bus, grad, plant_bus[None, :])
+    return out[:rows] if short else out
 
 
 def make_shards(box, buses):
@@ -186,49 +281,51 @@
     own = (0, 0, 0)
 
     def shards(net_load, release, plant_bus, efficiency, ptdf, branch_class, class_limit, class_price):
-        rows_local, bus_local = net_load.shape
-        offset = lax.axis_index("bus") * bus_local
-        columns = plant_bus - offset
-        inside = ((columns >= 0) & (columns < bus_local)).astype(jnp.float32)
-        clipped = jnp.clip(columns, 0, bus_local - 1)
-        weighted = efficiency * inside
-        inject = inject_of(net_load, release * weighted[None, :], jnp.where(inside > 0, columns, -1)[None, :])
+        rows = net_load.shape[0]
+        bus = lax.axis_index("bus").astype(jnp.int32)[None]
+        inject = inject_of(bus, net_load, release, efficiency, plant_bus)
         onehot = (branch_class[:, None] == jnp.arange(class_limit.shape[0])[None, :]).astype(jnp.float32)
         limit = jnp.sum(onehot * class_limit[None, :], axis=1)[None, :]
         price = jnp.sum(onehot * class_price[None, :], axis=1)[None, :]
 
-        def partial_grads(blocks):
-            flows = flows_of(blocks, ptdf)
+        def over_bus(value):
             if buses == 2:
-                flows = flows + lax.ppermute(flows, "bus", [(0, 1), (1, 0)])
-            else:
-                flows = lax.psum(flows, "bus")
-            upper = jax.nn.sigmoid((flows - limit) / SMOOTH)
-            lower = jax.nn.sigmoid((-flows - limit) / SMOOTH)
-            grad_flow = (price * (upper - lower)).astype(jnp.bfloat16)
-            part = jnp.dot(grad_flow, ptdf, preferred_element_type=jnp.float32)
-            return [part[i * rows_local : (i + 1) * rows_local] for i in range(len(blocks))]
+                return value, lax.ppermute(value, "bus", [(0, 1), (1, 0)])
+            return lax.psum(value, "bus"), jnp.zeros_like(value)
+
+        targets = {step_back(label, axis, shift, box) for now in reduce for axis, shift, label in now}
+
+        def flows_now(labels):
+            return over_bus(flows_of([have[label] for label in labels], ptdf))
+
+        def grads_now(labels, flows):
+            types = [jnp.float32 if label in targets else jnp.bfloat16 for label in labels]
+            parts.update(zip(labels, grads_of(*flows, limit, price, ptdf, rows, types)))
 
         have, parts, fresh, last = {own: inject}, {}, [own], {}
+        marks = {}
         for index, now in enumerate(gather):
             for axis, shift, label in now:
                 block = after(have[step_back(label, axis, shift, box)], last.get(axis))
+                block = after(block, marks.pop(index, None))
                 have[label] = last[axis] = lax.ppermute(block, "br", moves(axis, shift, box))
                 fresh.append(label)
             if index in ends:
-                for label, part in zip(fresh, partial_grads([have[label] for label in fresh])):
-                    parts[label] = part
+                flows = flows_now(fresh)
+                grads_now(fresh, flows)
+                marks[index + 2] = flows[0]
                 fresh = []
 
-        for now in reversed(reduce):
+        for index, now in enumerate(reversed(reduce), len(gather)):
             for axis, shift, label in reversed(now):
                 block = after(parts[label].astype(jnp.bfloat16), last.get(axis))
+                block = after(block, marks.pop(index, None))
                 last[axis] = lax.ppermute(block, "br", moves(axis, -shift, box))
                 to = step_back(label, axis, shift, box)
                 parts[to] = parts[to] + last[axis].astype(jnp.float32)
         grad_bus = parts[own]
-        picked = grad_bus[:, clipped] * weighted[None, :]
-        grad_release = lax.psum(picked, "bus")
+        mine, other = over_bus(pick_of(bus, grad_bus, plant_bus))
+        grad_release = (mine + other) * efficiency[None, :]
         return (grad_bus, grad_release)
 
     return shards

time: 191 us -> 141 us (0.74)
  waiting for transfers between devices: 109 us -> 69.8 us
  local copies, waits for them, and re-layouts: 23.4 us -> 6.39 us
  starting transfers between devices: 30 us -> 38.8 us
  Pallas kernels: 14 us -> 22.7 us
  matrix products: 5.89 us -> 0 us
  blocking collectives: 4.51 us -> 0 us
    ppermute x15, waiting for transfers between devices: 54.6 us -> 24.8 us  [shards(): lax.ppermute(block, 'br', moves(axis, shift, box))]
    ppermute x15, waiting for transfers between devices: 54 us -> 42.7 us  [shards(): last[axis] = lax.ppermute(block, 'br', moves(axis, -shift, box))]
    pallas_call x0 -> x4, Pallas kernels: none -> 8.72 us  [the longest x3 6.72 us: grads_of(): pl.pallas_call(functools.partial(grads_kernel, rows), grid=(width // tile...]
    add x1 -> x0, local copies, waits for them, and re-layouts: 8.39 us -> none  [shards(): parts[to] = parts[to] + last[axis].astype(jnp.float32)]
    gather x1 -> x0, local copies, waits for them, and re-layouts: 8.2 us -> none  [shards(): picked = grad_bus[:, clipped] * weighted[None, :]]
    ppermute x15, starting transfers between devices: 18.9 us -> 25 us  [shards(): lax.ppermute(block, 'br', moves(axis, shift, box))]
    dot_general x3 -> x0, matrix products: 5.89 us -> none  [partial_grads(): part = jnp.dot(grad_flow, ptdf, preferred_element_type=jnp.float32)]
    psum x1 -> x0, blocking collectives: 4.51 us -> none  [shards(): grad_release = lax.psum(picked, 'bus')]
  transfers between devices with their start and end apart: 33 -> 34, of which waited for: 25 -> 16; matrix products, arithmetic and copies ran while one was open for 4% -> 1% of each run, Pallas kernels for 0% -> 13%
where the time goes in v2:
time: 141 us
  waiting for transfers between devices  69.8 us (50%)
  starting transfers between devices  38.8 us (28%)
  Pallas kernels  22.7 us (16%)
  local copies, waits for them, and re-layouts  6.39 us (5%)
  other arithmetic  2 us (1%)
    ppermute x15, waiting for transfers between devices, shards(): last[axis] = lax.ppermute(block, 'br', moves(axis, -shift, box))  42.7 us
    ppermute x15, starting transfers between devices, shards(): lax.ppermute(block, 'br', moves(axis, shift, box))  25 us
    ppermute x15, waiting for transfers between devices, shards(): lax.ppermute(block, 'br', moves(axis, shift, box))  24.8 us
    ppermute x15, starting transfers between devices, shards(): last[axis] = lax.ppermute(block, 'br', moves(axis, -shift, box))  13.2 us
    pallas_call x3, Pallas kernels, flows_of(): pl.pallas_call(functools.partial(flows_kernel, count), grid=(width // til...  11 us
    pallas_call x3, Pallas kernels, grads_of(): pl.pallas_call(functools.partial(grads_kernel, rows), grid=(width // tile...  6.72 us
    unnamed x24, local copies, waits for them, and re-layouts  6.39 us
    pallas_call x1, Pallas kernels, inject_of(): pl.pallas_call(inject_kernel, grid=(width // tile,), in_specs=[pl.BlockSp...  3.05 us
  transfers between devices with their start and end apart: 34, of which 16 were waited for; matrix products, arithmetic and copies ran while one was open for 1% of the time, Pallas kernels for 13%

profile of v2, /device:TPU:0, one launch (start us, length us, event | category | flops | bytes accessed | tf_op | source)
XLA Modules:
  0.0 140.6 jit_solution(627999706791009962)
XLA Ops:
  0.7 1.0 copy-done.3
  1.7 0.8 copy-done.4
  2.5 0.7 copy-done.5
  3.2 0.7 copy-done.7
  3.8 3.0 %inject.1.refs_0_ = bf16[8,30208]{1,0:T(8,128)(2,1)S(1)} custom-call(s32[1]{0:T(128)} %bitcast.bus_ref, bf16[8,30208]{1,0:T(8,128)(2,1)S(1)} %copy-done.3, f32[8,1024]{1,0:T(8,128)S(1)} %copy-done.4, f32[1,1024]{1,0:T(1,128)S(1)} %bitcast.7, s32[1,1024]{1,0:T(1,128)S(1)} %bitcast.5), custom_call_target="tpu_custom_call" | custom-call | tf_op jit(solution)/shard_map/inject/pallas_call | solution.py:145
  6.9 5.1 %collective-permute-start = (bf16[8,30208]{1,0:T(8,128)(2,1)S(1)}, bf16[8,30208]{1,0:T(8,128)(2,1)S(1)}, u32[]{:S(2)}, u32[]{:S(2)}) collective-permute-start(bf16[8,30208]{1,0:T(8,128)(2,1)S(1)} %inject.1.refs_0_), channel_id=1, source_target_pairs={{0,24},{2,26},{4,28},{6,30},{8,0},{10,2},{12,4},{14,6},{16,8},{18,... | collective-permute-start | bytes 1449992 | tf_op jit(solution)/shard_map/ppermute | solution.py:311
  12.0 1.5 %collective-permute-start.1 = (bf16[8,30208]{1,0:T(8,128)(2,1)S(1)}, bf16[8,30208]{1,0:T(8,128)(2,1)S(1)}, u32[]{:S(2)}, u32[]{:S(2)}) collective-permute-start(bf16[8,30208]{1,0:T(8,128)(2,1)S(1)} %inject.1.refs_0_), channel_id=1, source_target_pairs={{0,2},{2,0},{4,6},{6,4},{8,10},{10,8},{12,14},{14,12},{16,18},{18,... | collective-permute-start | bytes 1449992 | tf_op jit(solution)/shard_map/ppermute | solution.py:311
  13.5 1.5 %collective-permute-start.2 = (bf16[8,30208]{1,0:T(8,128)(2,1)S(1)}, bf16[8,30208]{1,0:T(8,128)(2,1)S(1)}, u32[]{:S(2)}, u32[]{:S(2)}) collective-permute-start(bf16[8,30208]{1,0:T(8,128)(2,1)S(1)} %inject.1.refs_0_), channel_id=1, source_target_pairs={{0,4},{2,6},{4,0},{6,2},{8,12},{10,14},{12,8},{14,10},{16,20},{18,... | collective-permute-start | bytes 1449992 | tf_op jit(solution)/shard_map/ppermute | solution.py:311
  15.0 7.3 %collective-permute-done.refs_1_ = bf16[8,30208]{1,0:T(8,128)(2,1)S(1)} collective-permute-done((bf16[8,30208]{1,0:T(8,128)(2,1)S(1)}, bf16[8,30208]{1,0:T(8,128)(2,1)S(1)}, u32[]{:S(2)}, u32[]{:S(2)}) %collective-permute-start) | collective-permute-done | bytes 483360 | tf_op jit(solution)/shard_map/ppermute | solution.py:311
  22.3 4.3 %collective-permute-start.3 = (bf16[8,30208]{1,0:T(8,128)(2,1)S(1)}, bf16[8,30208]{1,0:T(8,128)(2,1)S(1)}, u32[]{:S(2)}, u32[]{:S(2)}) collective-permute-start(bf16[8,30208]{1,0:T(8,128)(2,1)S(1)} %collective-permute-done.refs_1_), channel_id=1, source_target_pairs={{0,24},{2,26},{4,28},{6,30},{8,0},{10,2},{12,4},{14,6},{16,8},{18,... | collective-permute-start | bytes 1449992 | tf_op jit(solution)/shard_map/ppermute | solution.py:311
  26.6 1.5 %collective-permute-start.4 = (bf16[8,30208]{1,0:T(8,128)(2,1)S(1)}, bf16[8,30208]{1,0:T(8,128)(2,1)S(1)}, u32[]{:S(2)}, u32[]{:S(2)}) collective-permute-start(bf16[8,30208]{1,0:T(8,128)(2,1)S(1)} %collective-permute-done.refs_1_), channel_id=1, source_target_pairs={{0,2},{2,0},{4,6},{6,4},{8,10},{10,8},{12,14},{14,12},{16,18},{18,... | collective-permute-start | bytes 1449992 | tf_op jit(solution)/shard_map/ppermute | solution.py:311
  28.1 1.5 %collective-permute-start.5 = (bf16[8,30208]{1,0:T(8,128)(2,1)S(1)}, bf16[8,30208]{1,0:T(8,128)(2,1)S(1)}, u32[]{:S(2)}, u32[]{:S(2)}) collective-permute-start(bf16[8,30208]{1,0:T(8,128)(2,1)S(1)} %collective-permute-done.1.refs_2_), channel_id=1, source_target_pairs={{0,4},{2,6},{4,0},{6,2},{8,12},{10,14},{12,8},{14,10},{16,20},{18,... | collective-permute-start | bytes 1449992 | tf_op jit(solution)/shard_map/ppermute | solution.py:311
  29.6 7.9 %collective-permute-done.3.refs_4_ = bf16[8,30208]{1,0:T(8,128)(2,1)S(1)} collective-permute-done((bf16[8,30208]{1,0:T(8,128)(2,1)S(1)}, bf16[8,30208]{1,0:T(8,128)(2,1)S(1)}, u32[]{:S(2)}, u32[]{:S(2)}) %collective-permute-start.3) | collective-permute-done | bytes 483360 | tf_op jit(solution)/shard_map/ppermute | solution.py:311
  37.5 0.7 collective-permute-done.4.refs_5_
  38.2 1.5 %collective-permute-start.7 = (bf16[8,30208]{1,0:T(8,128)(2,1)S(1)}, bf16[8,30208]{1,0:T(8,128)(2,1)S(1)}, u32[]{:S(2)}, u32[]{:S(2)}) collective-permute-start(bf16[8,30208]{1,0:T(8,128)(2,1)S(1)} %collective-permute-done.3.refs_4_), channel_id=1, source_target_pairs={{0,2},{2,0},{4,6},{6,4},{8,10},{10,8},{12,14},{14,12},{16,18},{18,... | collective-permute-start | bytes 1449992 | tf_op jit(solution)/shard_map/ppermute | solution.py:311
  39.7 1.5 %collective-permute-start.8 = (bf16[8,30208]{1,0:T(8,128)(2,1)S(1)}, bf16[8,30208]{1,0:T(8,128)(2,1)S(1)}, u32[]{:S(2)}, u32[]{:S(2)}) collective-permute-start(bf16[8,30208]{1,0:T(8,128)(2,1)S(1)} %collective-permute-done.4.refs_5_), channel_id=1, source_target_pairs={{0,4},{2,6},{4,0},{6,2},{8,12},{10,14},{12,8},{14,10},{16,20},{18,... | collective-permute-start | bytes 1449992 | tf_op jit(solution)/shard_map/ppermute | solution.py:311
  41.2 8.3 %collective-permute-done.6.refs_7_ = bf16[8,30208]{1,0:T(8,128)(2,1)S(1)} collective-permute-done((bf16[8,30208]{1,0:T(8,128)(2,1)S(1)}, bf16[8,30208]{1,0:T(8,128)(2,1)S(1)}, u32[]{:S(2)}, u32[]{:S(2)}) %collective-permute-start.6) | collective-permute-done | bytes 483360 | tf_op jit(solution)/shard_map/ppermute | solution.py:311
  49.6 1.5 %collective-permute-start.14 = (bf16[8,30208]{1,0:T(8,128)(2,1)S(1)}, bf16[8,30208]{1,0:T(8,128)(2,1)S(1)}, u32[]{:S(2)}, u32[]{:S(2)}) collective-permute-start(bf16[8,30208]{1,0:T(8,128)(2,1)S(1)} %collective-permute-done.6.refs_7_), channel_id=1, source_target_pairs={{0,2},{2,0},{4,6},{6,4},{8,10},{10,8},{12,14},{14,12},{16,18},{18,... | collective-permute-start | bytes 1449992 | tf_op jit(solution)/shard_map/ppermute | solution.py:311
  51.0 1.5 %collective-permute-start.16 = (bf16[8,30208]{1,0:T(8,128)(2,1)S(1)}, bf16[8,30208]{1,0:T(8,128)(2,1)S(1)}, u32[]{:S(2)}, u32[]{:S(2)}) collective-permute-start(bf16[8,30208]{1,0:T(8,128)(2,1)S(1)} %collective-permute-done.7.refs_8_), channel_id=1, source_target_pairs={{0,4},{2,6},{4,0},{6,2},{8,12},{10,14},{12,8},{14,10},{16,20},{18,... | collective-permute-start | bytes 1449992 | tf_op jit(solution)/shard_map/ppermute | solution.py:311
  52.6 3.2 %copy-done = bf16[128,30208]{1,0:T(8,128)(2,1)S(1)} copy-done((bf16[128,30208]{1,0:T(8,128)(2,1)S(1)}, bf16[128,30208]{1,0:T(8,128)(2,1)}, u32[]{:S(2)}) %copy-start) | copy-done | bytes 7733272
  55.8 3.9 %flows.3.mine_ref = f32[80,128]{1,0:T(8,128)S(1)} custom-call(bf16[8,30208]{1,0:T(8,128)(2,1)S(1)} %inject.1.refs_0_, bf16[8,30208]{1,0:T(8,128)(2,1)S(1)} %collective-permute-done.refs_1_, bf16[8,30208]{1,0:T(8,128)(2,1)S(1)} %collective-permute-done.1.refs_2_, bf16[8,30208]{1,0:T(8,128)(2,1)S(1)} %collective-permute-done.2.refs_3_, ...), custom_call_target="tpu_custom_call" | custom-call | tf_op jit(solution)/shard_map/flows/pallas_call | solution.py:185
  59.6 0.6 collective-permute-done.10.refs_0_
  60.2 1.0 collective-permute-start.11
  61.2 1.0 collective-permute-start.15
  62.3 1.5 %collective-permute-start.17 = (bf16[8,30208]{1,0:T(8,128)(2,1)S(1)}, bf16[8,30208]{1,0:T(8,128)(2,1)S(1)}, u32[]{:S(2)}, u32[]{:S(2)}) collective-permute-start(bf16[8,30208]{1,0:T(8,128)(2,1)S(1)} %collective-permute-done.refs_1_), channel_id=1, source_target_pairs={{0,4},{2,6},{4,0},{6,2},{8,12},{10,14},{12,8},{14,10},{16,20},{18,... | collective-permute-start | bytes 1449992 | tf_op jit(solution)/shard_map/ppermute | solution.py:311
  63.8 0.1 select_reduce_fusion
  63.9 1.1 collective-permute-done.9.other_ref
  65.0 2.5 %grads.3 = (f32[8,30208]{1,0:T(8,128)S(1)}, bf16[8,30208]{1,0:T(8,128)(2,1)S(1)}, f32[8,30208]{1,0:T(8,128)S(1)}, f32[8,30208]{1,0:T(8,128)S(1)}, f32[8,30208]{1...) custom-call(f32[80,128]{1,0:T(8,128)S(1)} %flows.3.mine_ref, ...), custom_call_target="tpu_custom_call" | custom-call | tf_op jit(solution)/shard_map/grads/pallas_call | solution.py:219
  67.5 3.6 %flows.5.mine_ref = f32[24,128]{1,0:T(8,128)S(1)} custom-call(bf16[8,30208]{1,0:T(8,128)(2,1)S(1)} %collective-permute-done.10.refs_0_, bf16[8,30208]{1,0:T(8,128)(2,1)S(1)} %collective-permute-done.14.refs_1_, bf16[8,30208]{1,0:T(8,128)(2,1)S(1)} %collective-permute-done.16.refs_2_, bf16[128,30208]{1,0:T(8,128)(2,1)S(1)} %copy-done.1), custom_call_target="tpu_custom_call" | custom-call | tf_op jit(solution)/shard_map/flows/pallas_call | solution.py:185
  71.1 1.6 %collective-permute-start.12 = (bf16[8,30208]{1,0:T(8,128)(2,1)S(1)}, bf16[8,30208]{1,0:T(8,128)(2,1)S(1)}, u32[]{:S(2)}, u32[]{:S(2)}) collective-permute-start(bf16[8,30208]{1,0:T(8,128)(2,1)S(1)} %get-tuple-element.60), channel_id=1, source_target_pairs={{0,8},{2,10},{4,12},{6,14},{8,16},{10,18},{12,20},{14,22},{16,24},... | collective-permute-start | bytes 1449992 | tf_op jit(solution)/shard_map/ppermute | solution.py:323
  72.7 1.0 collective-permute-start.19
  73.6 1.5 %collective-permute-start.23 = (bf16[8,30208]{1,0:T(8,128)(2,1)S(1)}, bf16[8,30208]{1,0:T(8,128)(2,1)S(1)}, u32[]{:S(2)}, u32[]{:S(2)}) collective-permute-start(bf16[8,30208]{1,0:T(8,128)(2,1)S(1)} %get-tuple-element.78), channel_id=1, source_target_pairs={{0,4},{2,6},{4,0},{6,2},{8,12},{10,14},{12,8},{14,10},{16,20},{18,... | collective-permute-start | bytes 1449992 | tf_op jit(solution)/shard_map/ppermute | solution.py:323
  75.1 3.5 %flows.4.mine_ref = f32[24,128]{1,0:T(8,128)S(1)} custom-call(bf16[8,30208]{1,0:T(8,128)(2,1)S(1)} %collective-permute-done.11.refs_0_, bf16[8,30208]{1,0:T(8,128)(2,1)S(1)} %collective-permute-done.15.refs_1_, bf16[8,30208]{1,0:T(8,128)(2,1)S(1)} %collective-permute-done.17.refs_2_, bf16[128,30208]{1,0:T(8,128)(2,1)S(1)} %copy-done.1), custom_call_target="tpu_custom_call" | custom-call | tf_op jit(solution)/shard_map/flows/pallas_call | solution.py:185
  78.7 0.6 collective-permute-start.18
  79.3 2.1 %grads.5 = (f32[8,30208]{1,0:T(8,128)S(1)}, bf16[8,30208]{1,0:T(8,128)(2,1)S(1)}, bf16[8,30208]{1,0:T(8,128)(2,1)S(1)}) custom-call(f32[24,128]{1,0:T(8,128)S(1)} %flows.5.mine_ref, f32[24,128]{1,0:T(8,128)S(1)} %collective-permute-done.21.other_ref, f32[1,128]{1,0:T(1,128)S(1)} %bitcast.12, f32[1,128]{1,0:T(1,128)S(1)} %bitcast.9, ...), custom_call_target="tpu_custom_call" | custom-call | tf_op jit(solution)/shard_map/grads/pallas_call | solution.py:219
  81.4 2.1 %grads.4 = (bf16[8,30208]{1,0:T(8,128)(2,1)S(1)}, bf16[8,30208]{1,0:T(8,128)(2,1)S(1)}, f32[8,30208]{1,0:T(8,128)S(1)}) custom-call(f32[24,128]{1,0:T(8,128)S(1)} %flows.4.mine_ref, f32[24,128]{1,0:T(8,128)S(1)} %collective-permute-done.18.other_ref, f32[1,128]{1,0:T(1,128)S(1)} %bitcast.13, f32[1,128]{1,0:T(1,128)S(1)} %bitcast.10, ...), custom_call_target="tpu_custom_call" | custom-call | tf_op jit(solution)/shard_map/grads/pallas_call | solution.py:219
  83.5 2.8 %collective-permute-done.12 = bf16[8,30208]{1,0:T(8,128)(2,1)S(1)} collective-permute-done((bf16[8,30208]{1,0:T(8,128)(2,1)S(1)}, bf16[8,30208]{1,0:T(8,128)(2,1)S(1)}, u32[]{:S(2)}, u32[]{:S(2)}) %collective-permute-start.12) | collective-permute-done | bytes 483360 | tf_op jit(solution)/shard_map/ppermute | solution.py:323
  86.3 0.5 collective-permute-start.22
  86.9 1.4 collective-permute-start.24
  88.2 0.1 add_convert_fusion.3
  88.4 0.1 add_convert_fusion.6
  88.5 12.2 %collective-permute-done.13 = bf16[8,30208]{1,0:T(8,128)(2,1)S(1)} collective-permute-done((bf16[8,30208]{1,0:T(8,128)(2,1)S(1)}, bf16[8,30208]{1,0:T(8,128)(2,1)S(1)}, u32[]{:S(2)}, u32[]{:S(2)}) %collective-permute-start.13) | collective-permute-done | bytes 483360 | tf_op jit(solution)/shard_map/ppermute | solution.py:323
  100.8 0.1 add_convert_fusion.2
  100.9 0.3 collective-permute-start.28
  101.2 0.1 add_convert_fusion.4
  101.3 11.2 %collective-permute-done.25 = bf16[8,30208]{1,0:T(8,128)(2,1)S(1)} collective-permute-done((bf16[8,30208]{1,0:T(8,128)(2,1)S(1)}, bf16[8,30208]{1,0:T(8,128)(2,1)S(1)}, u32[]{:S(2)}, u32[]{:S(2)}) %collective-permute-start.25) | collective-permute-done | bytes 483360 | tf_op jit(solution)/shard_map/ppermute | solution.py:323
  112.4 0.3 collective-permute-start.26
  112.7 0.2 collective-permute-start.29
  112.9 0.2 add_convert_fusion.1
  113.1 1.2 collective-permute-done.20
  114.3 2.4 %collective-permute-start.31 = (bf16[8,30208]{1,0:T(8,128)(2,1)S(1)}, bf16[8,30208]{1,0:T(8,128)(2,1)S(1)}, u32[]{:S(2)}, u32[]{:S(2)}) collective-permute-start(bf16[8,30208]{1,0:T(8,128)(2,1)S(1)} %add_convert_fusion.1), channel_id=1, source_target_pairs={{0,24},{2,26},{4,28},{6,30},{8,0},{10,2},{12,4},{14,6},{16,8},{18,... | collective-permute-start | bytes 1449992 | tf_op jit(solution)/shard_map/ppermute | solution.py:323
  116.7 0.1 add_convert_fusion.5
  116.8 6.8 %collective-permute-done.26 = bf16[8,30208]{1,0:T(8,128)(2,1)S(1)} collective-permute-done((bf16[8,30208]{1,0:T(8,128)(2,1)S(1)}, bf16[8,30208]{1,0:T(8,128)(2,1)S(1)}, u32[]{:S(2)}, u32[]{:S(2)}) %collective-permute-start.26) | collective-permute-done | bytes 483360 | tf_op jit(solution)/shard_map/ppermute | solution.py:323
  123.6 0.3 collective-permute-start.27
  123.9 1.3 collective-permute-done.31
  125.2 0.2 add_convert_fusion
  125.5 3.8 %collective-permute-start.32 = (bf16[8,30208]{1,0:T(8,128)(2,1)S(1)}, bf16[8,30208]{1,0:T(8,128)(2,1)S(1)}, u32[]{:S(2)}, u32[]{:S(2)}) collective-permute-start(bf16[8,30208]{1,0:T(8,128)(2,1)S(1)} %add_convert_fusion), channel_id=1, source_target_pairs={{0,24},{2,26},{4,28},{6,30},{8,0},{10,2},{12,4},{14,6},{16,8},{18,... | collective-permute-start | bytes 1449992 | tf_op jit(solution)/shard_map/ppermute | solution.py:323
  129.3 4.3 %collective-permute-done.27 = bf16[8,30208]{1,0:T(8,128)(2,1)S(1)} collective-permute-done((bf16[8,30208]{1,0:T(8,128)(2,1)S(1)}, bf16[8,30208]{1,0:T(8,128)(2,1)S(1)}, u32[]{:S(2)}, u32[]{:S(2)}) %collective-permute-start.27) | collective-permute-done | bytes 483360 | tf_op jit(solution)/shard_map/ppermute | solution.py:323
  133.6 0.3 collective-permute-done.30
  133.9 2.5 %collective-permute-done.32 = bf16[8,30208]{1,0:T(8,128)(2,1)S(1)} collective-permute-done((bf16[8,30208]{1,0:T(8,128)(2,1)S(1)}, bf16[8,30208]{1,0:T(8,128)(2,1)S(1)}, u32[]{:S(2)}, u32[]{:S(2)}) %collective-permute-start.32) | collective-permute-done | bytes 483360 | tf_op jit(solution)/shard_map/ppermute | solution.py:323
  136.4 0.3 convert_add_fusion.grad_ref
  136.7 2.0 %pick.1 = f32[8,1024]{1,0:T(8,128)S(1)} custom-call(s32[1]{0:T(128)} %bitcast.bus_ref, f32[8,30208]{1,0:T(8,128)S(1)} %convert_add_fusion.grad_ref, s32[1,1024]{1,0:T(1,128)S(1)} %bitcast.6), custom_call_target="tpu_custom_call" | custom-call | tf_op jit(solution)/shard_map/pick/pallas_call | solution.py:262
  138.8 1.2 collective-permute-done.33
  140.0 0.6 add_multiply_fusion
  (46 shorter events, 0.2 us)
Async XLA Ops:
  0.6 63.2 %copy-start.10 = (s32[128]{0:T(128)S(1)}, s32[128]{0:T(128)}, u32[]{:S(2)}) copy-start(s32[128]{0:T(128)} %param.13) | copy-start | bytes 1540
  0.6 63.1 %copy-start.11 = (f32[16]{0:T(128)S(1)}, f32[16]{0:T(128)}, u32[]{:S(2)}) copy-start(f32[16]{0:T(128)} %param.14) | copy-start | bytes 196
  0.7 63.1 %copy-start.9 = (f32[16]{0:T(128)S(1)}, f32[16]{0:T(128)}, u32[]{:S(2)}) copy-start(f32[16]{0:T(128)} %param.15) | copy-start | bytes 196
  0.7 1.0 copy-start.3
  1.7 0.8 copy-start.4
  2.5 0.7 copy-start.5
  3.2 0.7 copy-start.7
  6.9 15.4 %collective-permute-start = (bf16[8,30208]{1,0:T(8,128)(2,1)S(1)}, bf16[8,30208]{1,0:T(8,128)(2,1)S(1)}, u32[]{:S(2)}, u32[]{:S(2)}) collective-permute-start(bf16[8,30208]{1,0:T(8,128)(2,1)S(1)} %inject.1.refs_0_), channel_id=1, source_target_pairs={{0,24},{2,26},{4,28},{6,30},{8,0},{10,2},{12,4},{14,6},{16,8},{18,... | collective-permute-start | bytes 1449992 | tf_op jit(solution)/shard_map/ppermute | solution.py:311
  12.0 14.6 %collective-permute-start.1 = (bf16[8,30208]{1,0:T(8,128)(2,1)S(1)}, bf16[8,30208]{1,0:T(8,128)(2,1)S(1)}, u32[]{:S(2)}, u32[]{:S(2)}) collective-permute-start(bf16[8,30208]{1,0:T(8,128)(2,1)S(1)} %inject.1.refs_0_), channel_id=1, source_target_pairs={{0,2},{2,0},{4,6},{6,4},{8,10},{10,8},{12,14},{14,12},{16,18},{18,... | collective-permute-start | bytes 1449992 | tf_op jit(solution)/shard_map/ppermute | solution.py:311
  13.5 14.6 %collective-permute-start.2 = (bf16[8,30208]{1,0:T(8,128)(2,1)S(1)}, bf16[8,30208]{1,0:T(8,128)(2,1)S(1)}, u32[]{:S(2)}, u32[]{:S(2)}) collective-permute-start(bf16[8,30208]{1,0:T(8,128)(2,1)S(1)} %inject.1.refs_0_), channel_id=1, source_target_pairs={{0,4},{2,6},{4,0},{6,2},{8,12},{10,14},{12,8},{14,10},{16,20},{18,... | collective-permute-start | bytes 1449992 | tf_op jit(solution)/shard_map/ppermute | solution.py:311
  22.3 15.2 %collective-permute-start.3 = (bf16[8,30208]{1,0:T(8,128)(2,1)S(1)}, bf16[8,30208]{1,0:T(8,128)(2,1)S(1)}, u32[]{:S(2)}, u32[]{:S(2)}) collective-permute-start(bf16[8,30208]{1,0:T(8,128)(2,1)S(1)} %collective-permute-done.refs_1_), channel_id=1, source_target_pairs={{0,24},{2,26},{4,28},{6,30},{8,0},{10,2},{12,4},{14,6},{16,8},{18,... | collective-permute-start | bytes 1449992 | tf_op jit(solution)/shard_map/ppermute | solution.py:311
  26.6 11.6 %collective-permute-start.4 = (bf16[8,30208]{1,0:T(8,128)(2,1)S(1)}, bf16[8,30208]{1,0:T(8,128)(2,1)S(1)}, u32[]{:S(2)}, u32[]{:S(2)}) collective-permute-start(bf16[8,30208]{1,0:T(8,128)(2,1)S(1)} %collective-permute-done.refs_1_), channel_id=1, source_target_pairs={{0,2},{2,0},{4,6},{6,4},{8,10},{10,8},{12,14},{14,12},{16,18},{18,... | collective-permute-start | bytes 1449992 | tf_op jit(solution)/shard_map/ppermute | solution.py:311
  28.1 11.6 %collective-permute-start.5 = (bf16[8,30208]{1,0:T(8,128)(2,1)S(1)}, bf16[8,30208]{1,0:T(8,128)(2,1)S(1)}, u32[]{:S(2)}, u32[]{:S(2)}) collective-permute-start(bf16[8,30208]{1,0:T(8,128)(2,1)S(1)} %collective-permute-done.1.refs_2_), channel_id=1, source_target_pairs={{0,4},{2,6},{4,0},{6,2},{8,12},{10,14},{12,8},{14,10},{16,20},{18,... | collective-permute-start | bytes 1449992 | tf_op jit(solution)/shard_map/ppermute | solution.py:311
  37.5 12.0 %collective-permute-start.6 = (bf16[8,30208]{1,0:T(8,128)(2,1)S(1)}, bf16[8,30208]{1,0:T(8,128)(2,1)S(1)}, u32[]{:S(2)}, u32[]{:S(2)}) collective-permute-start(bf16[8,30208]{1,0:T(8,128)(2,1)S(1)} %collective-permute-done.2.refs_3_), channel_id=1, source_target_pairs={{0,8},{2,10},{4,12},{6,14},{8,16},{10,18},{12,20},{14,22},{16,24},... | collective-permute-start | bytes 1449992 | tf_op jit(solution)/shard_map/ppermute | solution.py:311
  38.2 11.3 %collective-permute-start.7 = (bf16[8,30208]{1,0:T(8,128)(2,1)S(1)}, bf16[8,30208]{1,0:T(8,128)(2,1)S(1)}, u32[]{:S(2)}, u32[]{:S(2)}) collective-permute-start(bf16[8,30208]{1,0:T(8,128)(2,1)S(1)} %collective-permute-done.3.refs_4_), channel_id=1, source_target_pairs={{0,2},{2,0},{4,6},{6,4},{8,10},{10,8},{12,14},{14,12},{16,18},{18,... | collective-permute-start | bytes 1449992 | tf_op jit(solution)/shard_map/ppermute | solution.py:311
  39.7 11.3 %collective-permute-start.8 = (bf16[8,30208]{1,0:T(8,128)(2,1)S(1)}, bf16[8,30208]{1,0:T(8,128)(2,1)S(1)}, u32[]{:S(2)}, u32[]{:S(2)}) collective-permute-start(bf16[8,30208]{1,0:T(8,128)(2,1)S(1)} %collective-permute-done.4.refs_5_), channel_id=1, source_target_pairs={{0,4},{2,6},{4,0},{6,2},{8,12},{10,14},{12,8},{14,10},{16,20},{18,... | collective-permute-start | bytes 1449992 | tf_op jit(solution)/shard_map/ppermute | solution.py:311
  49.5 10.7 %collective-permute-start.10 = (bf16[8,30208]{1,0:T(8,128)(2,1)S(1)}, bf16[8,30208]{1,0:T(8,128)(2,1)S(1)}, u32[]{:S(2)}, u32[]{:S(2)}) collective-permute-start(bf16[8,30208]{1,0:T(8,128)(2,1)S(1)} %inject.1.refs_0_), channel_id=1, source_target_pairs={{0,8},{2,10},{4,12},{6,14},{8,16},{10,18},{12,20},{14,22},{16,24},... | collective-permute-start | bytes 1449992 | tf_op jit(solution)/shard_map/ppermute | solution.py:311
  49.6 11.7 %collective-permute-start.14 = (bf16[8,30208]{1,0:T(8,128)(2,1)S(1)}, bf16[8,30208]{1,0:T(8,128)(2,1)S(1)}, u32[]{:S(2)}, u32[]{:S(2)}) collective-permute-start(bf16[8,30208]{1,0:T(8,128)(2,1)S(1)} %collective-permute-done.6.refs_7_), channel_id=1, source_target_pairs={{0,2},{2,0},{4,6},{6,4},{8,10},{10,8},{12,14},{14,12},{16,18},{18,... | collective-permute-start | bytes 1449992 | tf_op jit(solution)/shard_map/ppermute | solution.py:311
  51.0 11.2 %collective-permute-start.16 = (bf16[8,30208]{1,0:T(8,128)(2,1)S(1)}, bf16[8,30208]{1,0:T(8,128)(2,1)S(1)}, u32[]{:S(2)}, u32[]{:S(2)}) collective-permute-start(bf16[8,30208]{1,0:T(8,128)(2,1)S(1)} %collective-permute-done.7.refs_8_), channel_id=1, source_target_pairs={{0,4},{2,6},{4,0},{6,2},{8,12},{10,14},{12,8},{14,10},{16,20},{18,... | collective-permute-start | bytes 1449992 | tf_op jit(solution)/shard_map/ppermute | solution.py:311
  52.6 3.2 %copy-start = (bf16[128,30208]{1,0:T(8,128)(2,1)S(1)}, bf16[128,30208]{1,0:T(8,128)(2,1)}, u32[]{:S(2)}) copy-start(bf16[128,30208]{1,0:T(8,128)(2,1)} %ptdf_ref.5) | copy-start | bytes 23199748
  55.8 9.2 %copy-start.1 = (bf16[128,30208]{1,0:T(8,128)(2,1)S(1)}, bf16[128,30208]{1,0:T(8,128)(2,1)}, u32[]{:S(2)}) copy-start(bf16[128,30208]{1,0:T(8,128)(2,1)} %ptdf_ref.5) | copy-start | bytes 23199748
  60.2 10.9 %collective-permute-start.11 = (bf16[8,30208]{1,0:T(8,128)(2,1)S(1)}, bf16[8,30208]{1,0:T(8,128)(2,1)S(1)}, u32[]{:S(2)}, u32[]{:S(2)}) collective-permute-start(bf16[8,30208]{1,0:T(8,128)(2,1)S(1)} %collective-permute-done.6.refs_7_), channel_id=1, source_target_pairs={{0,8},{2,10},{4,12},{6,14},{8,16},{10,18},{12,20},{14,22},{16,24},... | collective-permute-start | bytes 1449992 | tf_op jit(solution)/shard_map/ppermute | solution.py:311
  61.2 11.4 %collective-permute-start.15 = (bf16[8,30208]{1,0:T(8,128)(2,1)S(1)}, bf16[8,30208]{1,0:T(8,128)(2,1)S(1)}, u32[]{:S(2)}, u32[]{:S(2)}) collective-permute-start(bf16[8,30208]{1,0:T(8,128)(2,1)S(1)} %collective-permute-done.10.refs_0_), channel_id=1, source_target_pairs={{0,2},{2,0},{4,6},{6,4},{8,10},{10,8},{12,14},{14,12},{16,18},{18,... | collective-permute-start | bytes 1449992 | tf_op jit(solution)/shard_map/ppermute | solution.py:311
  62.3 11.3 %collective-permute-start.17 = (bf16[8,30208]{1,0:T(8,128)(2,1)S(1)}, bf16[8,30208]{1,0:T(8,128)(2,1)S(1)}, u32[]{:S(2)}, u32[]{:S(2)}) collective-permute-start(bf16[8,30208]{1,0:T(8,128)(2,1)S(1)} %collective-permute-done.refs_1_), channel_id=1, source_target_pairs={{0,4},{2,6},{4,0},{6,2},{8,12},{10,14},{12,8},{14,10},{16,20},{18,... | collective-permute-start | bytes 1449992 | tf_op jit(solution)/shard_map/ppermute | solution.py:311
  63.8 1.2 collective-permute-start.9
  71.1 15.2 %collective-permute-start.12 = (bf16[8,30208]{1,0:T(8,128)(2,1)S(1)}, bf16[8,30208]{1,0:T(8,128)(2,1)S(1)}, u32[]{:S(2)}, u32[]{:S(2)}) collective-permute-start(bf16[8,30208]{1,0:T(8,128)(2,1)S(1)} %get-tuple-element.60), channel_id=1, source_target_pairs={{0,8},{2,10},{4,12},{6,14},{8,16},{10,18},{12,20},{14,22},{16,24},... | collective-permute-start | bytes 1449992 | tf_op jit(solution)/shard_map/ppermute | solution.py:323
  72.7 13.7 %collective-permute-start.19 = (bf16[8,30208]{1,0:T(8,128)(2,1)S(1)}, bf16[8,30208]{1,0:T(8,128)(2,1)S(1)}, u32[]{:S(2)}, u32[]{:S(2)}) collective-permute-start(bf16[8,30208]{1,0:T(8,128)(2,1)S(1)} %get-tuple-element.69), channel_id=1, source_target_pairs={{0,2},{2,0},{4,6},{6,4},{8,10},{10,8},{12,14},{14,12},{16,18},{18,... | collective-permute-start | bytes 1449992 | tf_op jit(solution)/shard_map/ppermute | solution.py:323
  73.6 13.3 %collective-permute-start.23 = (bf16[8,30208]{1,0:T(8,128)(2,1)S(1)}, bf16[8,30208]{1,0:T(8,128)(2,1)S(1)}, u32[]{:S(2)}, u32[]{:S(2)}) collective-permute-start(bf16[8,30208]{1,0:T(8,128)(2,1)S(1)} %get-tuple-element.78), channel_id=1, source_target_pairs={{0,4},{2,6},{4,0},{6,2},{8,12},{10,14},{12,8},{14,10},{16,20},{18,... | collective-permute-start | bytes 1449992 | tf_op jit(solution)/shard_map/ppermute | solution.py:323
  75.1 4.1 %collective-permute-start.21 = (f32[24,128]{1,0:T(8,128)S(1)}, f32[24,128]{1,0:T(8,128)S(1)}, u32[]{:S(2)}, u32[]{:S(2)}) collective-permute-start(f32[24,128]{1,0:T(8,128)S(1)} %flows.5.mine_ref), channel_id=1, source_target_pairs={{0,1},{1,0},{2,3},{3,2},{4,5},{5,4},{6,7},{7,6},{8,9},{9,8},{10,11... | collective-permute-start | bytes 36872 | tf_op jit(solution)/shard_map/ppermute | solution.py:293
  78.7 2.7 %collective-permute-start.18 = (f32[24,128]{1,0:T(8,128)S(1)}, f32[24,128]{1,0:T(8,128)S(1)}, u32[]{:S(2)}, u32[]{:S(2)}) collective-permute-start(f32[24,128]{1,0:T(8,128)S(1)} %flows.4.mine_ref), channel_id=1, source_target_pairs={{0,1},{1,0},{2,3},{3,2},{4,5},{5,4},{6,7},{7,6},{8,9},{9,8},{10,11... | collective-permute-start | bytes 36872 | tf_op jit(solution)/shard_map/ppermute | solution.py:293
  86.3 14.4 %collective-permute-start.13 = (bf16[8,30208]{1,0:T(8,128)(2,1)S(1)}, bf16[8,30208]{1,0:T(8,128)(2,1)S(1)}, u32[]{:S(2)}, u32[]{:S(2)}) collective-permute-start(bf16[8,30208]{1,0:T(8,128)(2,1)S(1)} %get-tuple-element.61), channel_id=1, source_target_pairs={{0,8},{2,10},{4,12},{6,14},{8,16},{10,18},{12,20},{14,22},{16,24},... | collective-permute-start | bytes 1449992 | tf_op jit(solution)/shard_map/ppermute | solution.py:323
  86.3 14.5 %collective-permute-start.22 = (bf16[8,30208]{1,0:T(8,128)(2,1)S(1)}, bf16[8,30208]{1,0:T(8,128)(2,1)S(1)}, u32[]{:S(2)}, u32[]{:S(2)}) collective-permute-start(bf16[8,30208]{1,0:T(8,128)(2,1)S(1)} %get-tuple-element.73), channel_id=1, source_target_pairs={{0,2},{2,0},{4,6},{6,4},{8,10},{10,8},{12,14},{14,12},{16,18},{18,... | collective-permute-start | bytes 1449992 | tf_op jit(solution)/shard_map/ppermute | solution.py:323
  86.9 13.9 %collective-permute-start.24 = (bf16[8,30208]{1,0:T(8,128)(2,1)S(1)}, bf16[8,30208]{1,0:T(8,128)(2,1)S(1)}, u32[]{:S(2)}, u32[]{:S(2)}) collective-permute-start(bf16[8,30208]{1,0:T(8,128)(2,1)S(1)} %get-tuple-element.80), channel_id=1, source_target_pairs={{0,4},{2,6},{4,0},{6,2},{8,12},{10,14},{12,8},{14,10},{16,20},{18,... | collective-permute-start | bytes 1449992 | tf_op jit(solution)/shard_map/ppermute | solution.py:323
  88.5 48.2 %copy-start.6 = (s32[1024]{0:T(1024)S(1)}, s32[1024]{0:T(1024)}, u32[]{:S(2)}) copy-start(s32[1024]{0:T(1024)} %param.10) | copy-start | bytes 12292
  100.7 13.6 %collective-permute-start.20 = (bf16[8,30208]{1,0:T(8,128)(2,1)S(1)}, bf16[8,30208]{1,0:T(8,128)(2,1)S(1)}, u32[]{:S(2)}, u32[]{:S(2)}) collective-permute-start(bf16[8,30208]{1,0:T(8,128)(2,1)S(1)} %add_convert_fusion.6), channel_id=1, source_target_pairs={{0,8},{2,10},{4,12},{6,14},{8,16},{10,18},{12,20},{14,22},{16,24},... | collective-permute-start | bytes 1449992 | tf_op jit(solution)/shard_map/ppermute | solution.py:323
  100.7 11.7 %collective-permute-start.25 = (bf16[8,30208]{1,0:T(8,128)(2,1)S(1)}, bf16[8,30208]{1,0:T(8,128)(2,1)S(1)}, u32[]{:S(2)}, u32[]{:S(2)}) collective-permute-start(bf16[8,30208]{1,0:T(8,128)(2,1)S(1)} %get-tuple-element.81), channel_id=1, source_target_pairs={{0,4},{2,6},{4,0},{6,2},{8,12},{10,14},{12,8},{14,10},{16,20},{18,... | collective-permute-start | bytes 1449992 | tf_op jit(solution)/shard_map/ppermute | solution.py:323
  100.7 39.3 %copy-start.8 = (f32[1024]{0:T(1024)S(1)}, f32[1024]{0:T(1024)}, u32[]{:S(2)}) copy-start(f32[1024]{0:T(1024)} %param.11) | copy-start | bytes 12292
  100.9 11.8 %collective-permute-start.28 = (bf16[8,30208]{1,0:T(8,128)(2,1)S(1)}, bf16[8,30208]{1,0:T(8,128)(2,1)S(1)}, u32[]{:S(2)}, u32[]{:S(2)}) collective-permute-start(bf16[8,30208]{1,0:T(8,128)(2,1)S(1)} %add_convert_fusion.2), channel_id=1, source_target_pairs={{0,2},{2,0},{4,6},{6,4},{8,10},{10,8},{12,14},{14,12},{16,18},{18,... | collective-permute-start | bytes 1449992 | tf_op jit(solution)/shard_map/ppermute | solution.py:323
  112.4 11.2 %collective-permute-start.26 = (bf16[8,30208]{1,0:T(8,128)(2,1)S(1)}, bf16[8,30208]{1,0:T(8,128)(2,1)S(1)}, u32[]{:S(2)}, u32[]{:S(2)}) collective-permute-start(bf16[8,30208]{1,0:T(8,128)(2,1)S(1)} %add_convert_fusion.4), channel_id=1, source_target_pairs={{0,4},{2,6},{4,0},{6,2},{8,12},{10,14},{12,8},{14,10},{16,20},{18,... | collective-permute-start | bytes 1449992 | tf_op jit(solution)/shard_map/ppermute | solution.py:323
  112.7 11.2 %collective-permute-start.29 = (bf16[8,30208]{1,0:T(8,128)(2,1)S(1)}, bf16[8,30208]{1,0:T(8,128)(2,1)S(1)}, u32[]{:S(2)}, u32[]{:S(2)}) collective-permute-start(bf16[8,30208]{1,0:T(8,128)(2,1)S(1)} %get-tuple-element.88), channel_id=1, source_target_pairs={{0,2},{2,0},{4,6},{6,4},{8,10},{10,8},{12,14},{14,12},{16,18},{18,... | collective-permute-start | bytes 1449992 | tf_op jit(solution)/shard_map/ppermute | solution.py:323
  114.3 10.9 %collective-permute-start.31 = (bf16[8,30208]{1,0:T(8,128)(2,1)S(1)}, bf16[8,30208]{1,0:T(8,128)(2,1)S(1)}, u32[]{:S(2)}, u32[]{:S(2)}) collective-permute-start(bf16[8,30208]{1,0:T(8,128)(2,1)S(1)} %add_convert_fusion.1), channel_id=1, source_target_pairs={{0,24},{2,26},{4,28},{6,30},{8,0},{10,2},{12,4},{14,6},{16,8},{18,... | collective-permute-start | bytes 1449992 | tf_op jit(solution)/shard_map/ppermute | solution.py:323
  123.6 9.9 %collective-permute-start.27 = (bf16[8,30208]{1,0:T(8,128)(2,1)S(1)}, bf16[8,30208]{1,0:T(8,128)(2,1)S(1)}, u32[]{:S(2)}, u32[]{:S(2)}) collective-permute-start(bf16[8,30208]{1,0:T(8,128)(2,1)S(1)} %add_convert_fusion.5), channel_id=1, source_target_pairs={{0,4},{2,6},{4,0},{6,2},{8,12},{10,14},{12,8},{14,10},{16,20},{18,... | collective-permute-start | bytes 1449992 | tf_op jit(solution)/shard_map/ppermute | solution.py:323
  123.9 9.9 %collective-permute-start.30 = (bf16[8,30208]{1,0:T(8,128)(2,1)S(1)}, bf16[8,30208]{1,0:T(8,128)(2,1)S(1)}, u32[]{:S(2)}, u32[]{:S(2)}) collective-permute-start(bf16[8,30208]{1,0:T(8,128)(2,1)S(1)} %add_convert_fusion.3), channel_id=1, source_target_pairs={{0,2},{2,0},{4,6},{6,4},{8,10},{10,8},{12,14},{14,12},{16,18},{18,... | collective-permute-start | bytes 1449992 | tf_op jit(solution)/shard_map/ppermute | solution.py:323
  125.5 10.9 %collective-permute-start.32 = (bf16[8,30208]{1,0:T(8,128)(2,1)S(1)}, bf16[8,30208]{1,0:T(8,128)(2,1)S(1)}, u32[]{:S(2)}, u32[]{:S(2)}) collective-permute-start(bf16[8,30208]{1,0:T(8,128)(2,1)S(1)} %add_convert_fusion), channel_id=1, source_target_pairs={{0,24},{2,26},{4,28},{6,30},{8,0},{10,2},{12,4},{14,6},{16,8},{18,... | collective-permute-start | bytes 1449992 | tf_op jit(solution)/shard_map/ppermute | solution.py:323
  136.7 3.9 %copy-start.2 = (f32[8,30208]{1,0:T(8,128)}, f32[8,30208]{1,0:T(8,128)S(1)}, u32[]{:S(2)}) copy-start(f32[8,30208]{1,0:T(8,128)S(1)} %convert_add_fusion.grad_ref) | copy-start | bytes 2899972
  138.7 1.3 collective-permute-start.33

commit v3 on v2

v3 whole, which is shorter than its diff:
```python
import functools

import jax
import jax.numpy as jnp
from jax import lax
from jax.experimental import pallas as pl
from jax.experimental.pallas import tpu as pltpu
from jax.sharding import PartitionSpec as P

SMOOTH = 0.25
Z, Y, X = 0, 1, 2
GATHER, REDUCE, FLOWS, GRADS = 0, 1, 2, 3


def chip_box(count):
    bits = (count // 2).bit_length() - 1
    nx = 1 << (bits // 2)
    return count // (2 * nx), 2, nx


PLAN = [
    (GATHER, Z, -1, (-1, 0, 0), ()),
    (GATHER, X, 1, (0, 0, 1), ()),
    (GATHER, Y, 1, (0, 1, 0), ()),
    (GATHER, Z, -1, (2, 0, 0), (0,)),
    (GATHER, X, 1, (-1, 0, 1), (1,)),
    (GATHER, Y, 1, (0, 1, 1), (2,)),
    (GATHER, Z, 1, (1, 1, 0), (3,)),
    (GATHER, X, 1, (2, 0, 1), (4,)),
    (GATHER, Y, 1, (-1, 1, 1), (5,)),
    (FLOWS, 0, [(0, 0, 0), (-1, 0, 0), (0, 0, 1), (0, 1, 0), (2, 0, 0), (-1, 0, 1), (0, 1, 1), (1, 1, 0), (2, 0, 1), (-1, 1, 1)], ()),
    (GRADS, 0),
    (GATHER, Z, 1, (1, 0, 0), (6,)),
    (GATHER, X, 1, (1, 1, 1), (7,)),
    (GATHER, Y, 1, (2, 1, 1), (8,)),
    (FLOWS, 1, [(1, 0, 0), (1, 1, 1), (2, 1, 1)], ()),
    (GRADS, 1),
    (GATHER, Z, 1, (2, 1, 0), (9, 11)),
    (GATHER, X, 1, (1, 0, 1), (9, 12)),
    (GATHER, Y, 1, (-1, 1, 0), (9, 13)),
    (FLOWS, 2, [(2, 1, 0), (1, 0, 1), (-1, 1, 0)], ()),
    (GRADS, 2),
    (REDUCE, Y, 1, (0, 1, 1), (14, 18)),
    (REDUCE, X, 1, (-1, 1, 1), (14, 17)),
    (REDUCE, Z, -1, (-1, 0, 1), (14, 16)),
    (REDUCE, Y, 1, (2, 1, 1), (19, 21)),
    (REDUCE, X, 1, (1, 1, 1), (19, 22)),
    (REDUCE, Z, -1, (-1, 0, 0), (19, 23)),
    (REDUCE, Y, 1, (2, 1, 0), (24,)),
    (REDUCE, X, 1, (2, 0, 1), (25,)),
    (REDUCE, Z, -1, (-1, 1, 0), (26,)),
    (REDUCE, Y, 1, (1, 1, 0), (27,)),
    (REDUCE, X, 1, (1, 0, 1), (28,)),
    (REDUCE, Z, 1, (2, 0, 0), (29,)),
    (REDUCE, Y, 1, (0, 1, 0), (30,)),
    (REDUCE, X, 1, (0, 0, 1), (31,)),
    (REDUCE, Z, 1, (1, 0, 0), (32,)),
]


def greedy(box):
    labels = [(z, y, x) for z in range(box[0]) for y in range(box[1]) for x in range(box[2])]
    have, sends = {(0, 0, 0)}, []
    while len(have) < len(labels):
        taken = set()
        for axis in (Z, X, Y):
            shifts = (1, -1) if box[axis] > 2 else (1,)
            options = [
                (shift, label)
                for label in labels
                if label not in have and label not in taken
                for shift in shifts
                if step_back(label, axis, shift, box) in have
            ]
            if options:
                shift, label = options[0]
                sends.append((axis, shift, label))
                taken.add(label)
        have |= taken
    return sends


def step_back(label, axis, shift, box):
    moved = list(label)
    moved[axis] = (moved[axis] - shift) % box[axis]
    return tuple(moved)


def plan(box):
    if box == (4, 2, 2):
        wrap = lambda label: tuple(c % n for c, n in zip(label, box))
        steps = []
        for step in PLAN:
            if step[0] in (GATHER, REDUCE):
                step = (*step[:3], wrap(step[3]), step[4])
            elif step[0] == FLOWS:
                step = (*step[:2], [wrap(label) for label in step[2]], step[3])
            steps.append(step)
        return steps
    sends = greedy(box)
    steps = [(GATHER, *send, ()) for send in sends]
    steps += [(FLOWS, 0, [(0, 0, 0)] + [label for _, _, label in sends], ()), (GRADS, 0)]
    return steps + [(REDUCE, *send, ()) for send in reversed(sends)]


def moves(axis, shift, box):
    pairs = []
    for z in range(box[0]):
        for y in range(box[1]):
            for x in range(box[2]):
                to = step_back((z, y, x), axis, -shift, box)
                pairs.append(((z * box[1] + y) * box[2] + x, (to[0] * box[1] + to[1]) * box[2] + to[2]))
    return pairs


def after(value, earlier):
    if not earlier:
        return value
    return lax.optimization_barrier((value, *earlier))[0]


SPLIT = 1


def tile_of(width):
    groups = width // 128
    return 128 * max(n for n in range(1, 65) if groups % n == 0)


def part_specs(rows, width):
    tile = tile_of(width // SPLIT)
    steps = width // SPLIT // tile
    return steps, tile, [pl.BlockSpec((rows, tile), lambda i, h=h: (0, h * steps + i)) for h in range(SPLIT)]


def scatter_lanes(column):
    lane = lax.broadcasted_iota(jnp.int32, (128, column.shape[1]), 0)
    return jnp.where(lane == column % 128, 1.0, 0.0).astype(jnp.bfloat16)


def split_high(value):
    high = value.astype(jnp.bfloat16)
    return high, (value - high.astype(jnp.float32)).astype(jnp.bfloat16)


def place_of(bus_ref, column, part, groups):
    tile = (bus_ref[0] * SPLIT + part) * pl.num_programs(0) + pl.program_id(0)
    return column // 128 - tile * groups


def inject_kernel(bus_ref, release_ref, efficiency_ref, plant_ref, *refs):
    net_refs, out_refs = refs[:SPLIT], refs[SPLIT:]
    rows, width = net_refs[0].shape
    groups = width // 128
    column = plant_ref[...]
    lanes = scatter_lanes(column)
    high, low = split_high(release_ref[...] * efficiency_ref[...])

    for part in range(SPLIT):
        place = place_of(bus_ref, column, part, groups)

        def spread(values):
            picked = [jnp.where(place == group, values, 0.0) for group in range(groups)]
            return lax.dot_general(
                jnp.concatenate(picked, axis=0).astype(jnp.bfloat16),
                lanes,
                (((1,), (1,)), ((), ())),
                preferred_element_type=jnp.float32,
            )

        added = spread(high.astype(jnp.float32)) + spread(low.astype(jnp.float32))
        for group in range(groups):
            at = slice(group * 128, (group + 1) * 128)
            total = net_refs[part][:, at].astype(jnp.float32) + added[group * rows : (group + 1) * rows]
            out_refs[part][:, at] = total.astype(jnp.bfloat16)


FREE = pl.CostEstimate(flops=0, bytes_accessed=0, transcendentals=0)


def vmem(mebibytes):
    return pltpu.CompilerParams(vmem_limit_bytes=mebibytes << 20)


def inject_of(bus, net_load, release, efficiency, plant_bus):
    rows, width = net_load.shape
    short = -rows % 8
    if short:
        net_load = jnp.pad(net_load, ((0, short), (0, 0)))
        release = jnp.pad(release, ((0, short), (0, 0)))
    steps, tile, specs = part_specs(rows + short, width)
    plants = release.shape[1]
    whole = pl.BlockSpec((1, plants), lambda i: (0, 0))
    outs = pl.pallas_call(
        inject_kernel,
        grid=(steps,),
        in_specs=[
            pl.BlockSpec(memory_space=pltpu.SMEM),
            pl.BlockSpec((rows + short, plants), lambda i: (0, 0)),
            whole,
            whole,
            *specs,
        ],
        out_specs=[pl.BlockSpec((rows + short, tile), lambda i: (0, i))] * SPLIT,
        out_shape=[jax.ShapeDtypeStruct((rows + short, width // SPLIT), jnp.bfloat16)] * SPLIT,
        compiler_params=vmem(60),
        cost_estimate=FREE,
        name="inject",
    )(bus, release, efficiency[None, :], plant_bus[None, :], *[net_load] * SPLIT)
    return [out[:rows] if short else out for out in outs]


def flows_kernel(count, *refs):
    blocks, ptdf_refs, out_ref = refs[: count * SPLIT], refs[count * SPLIT : -1], refs[-1]

    @pl.when(pl.program_id(0) == 0)
    def _():
        out_ref[...] = jnp.zeros_like(out_ref)

    total = out_ref[...]
    for part in range(SPLIT):
        rows = jnp.concatenate([block[...].astype(jnp.float32) for block in blocks[part::SPLIT]], axis=0)
        total += lax.dot_general(
            rows.astype(jnp.bfloat16),
            ptdf_refs[part][...],
            (((1,), (1,)), ((), ())),
            preferred_element_type=jnp.float32,
        )
    out_ref[...] = total


def flows_of(blocks, ptdf):
    rows = blocks[0][0].shape[0]
    branches, width = ptdf.shape
    if rows % 8:
        short = -rows * len(blocks) % 8
        blocks = [[jnp.pad(jnp.concatenate(part, axis=0), ((0, short), (0, 0))) for part in zip(*blocks)]]
        rows = blocks[0][0].shape[0]
    count = len(blocks)
    steps, tile, ptdf_specs = part_specs(branches, width)
    return pl.pallas_call(
        functools.partial(flows_kernel, count),
        grid=(steps,),
        in_specs=[pl.BlockSpec((rows, tile), lambda i: (0, i))] * (count * SPLIT) + ptdf_specs,
        out_specs=pl.BlockSpec((count * rows, branches), lambda i: (0, 0)),
        out_shape=jax.ShapeDtypeStruct((count * rows, branches), jnp.float32),
        compiler_params=vmem(24),
        cost_estimate=FREE,
        name="flows",
    )(*[part for block in blocks for part in block], *[ptdf] * SPLIT)


def grad_flow_of(flows, limit, price):
    upper = jax.nn.sigmoid((flows - limit) / SMOOTH)
    lower = jax.nn.sigmoid((-flows - limit) / SMOOTH)
    return (price * (upper - lower)).astype(jnp.bfloat16)


def grads_kernel(rows, mine_ref, other_ref, limit_ref, price_ref, *refs):
    ptdf_refs, out_refs = refs[:SPLIT], refs[SPLIT:]
    grad_flow = grad_flow_of(mine_ref[...] + other_ref[...], limit_ref[...], price_ref[...])
    for part in range(SPLIT):
        grads = jnp.dot(grad_flow, ptdf_refs[part][...], preferred_element_type=jnp.float32)
        for index, out_ref in enumerate(out_refs[part::SPLIT]):
            out_ref[...] = grads[index * rows : (index + 1) * rows].astype(out_ref.dtype)


def grads_of(mine, other, limit, price, ptdf, rows, types):
    branches, width = ptdf.shape
    if rows % 8:
        grads = jnp.dot(grad_flow_of(mine + other, limit, price), ptdf, preferred_element_type=jnp.float32)
        return [jnp.split(grads[i * rows : (i + 1) * rows], SPLIT, axis=1) for i in range(len(types))]
    steps, tile, ptdf_specs = part_specs(branches, width)
    flow_spec = pl.BlockSpec(mine.shape, lambda i: (0, 0))
    class_spec = pl.BlockSpec((1, branches), lambda i: (0, 0))
    outs = pl.pallas_call(
        functools.partial(grads_kernel, rows),
        grid=(steps,),
        in_specs=[flow_spec, flow_spec, class_spec, class_spec, *ptdf_specs],
        out_specs=[pl.BlockSpec((rows, tile), lambda i: (0, i))] * (len(types) * SPLIT),
        out_shape=[jax.ShapeDtypeStruct((rows, width // SPLIT), dtype) for dtype in types for _ in range(SPLIT)],
        compiler_params=vmem(32),
        cost_estimate=FREE,
        name="grads",
    )(mine, other, limit, price, *[ptdf] * SPLIT)
    return [outs[i * SPLIT : (i + 1) * SPLIT] for i in range(len(types))]


def finish_kernel(terms, bus_ref, plant_ref, *refs):
    grad_ref, found_ref = refs[-2:]
    rows, half = refs[0].shape
    groups = half // 128
    column = plant_ref[...]
    lanes = scatter_lanes(column)
    lanes = jnp.concatenate([lanes, lanes], axis=0)
    picked = jnp.zeros(found_ref.shape, jnp.float32)
    for part in range(SPLIT):
        grad = refs[part][...]
        for term in range(1, terms):
            grad += refs[term * SPLIT + part][...].astype(jnp.float32)
        grad_ref[:, part * half : (part + 1) * half] = grad
        place = place_of(bus_ref, column, part, groups)
        high, low = split_high(jnp.concatenate([grad[:, g * 128 : (g + 1) * 128] for g in range(groups)], axis=0))
        found = jnp.dot(jnp.concatenate([high, low], axis=1), lanes, preferred_element_type=jnp.float32)
        for group in range(groups):
            picked += jnp.where(place == group, found[group * rows : (group + 1) * rows], 0.0)
    found_ref[...] = picked


def finish_of(bus, plant_bus, terms):
    rows, half = terms[0][0].shape
    short = -rows % 8
    if short:
        terms = [[jnp.pad(part, ((0, short), (0, 0))) for part in term] for term in terms]
    plants = plant_bus.shape[0]
    grad, found = pl.pallas_call(
        functools.partial(finish_kernel, len(terms)),
        grid=(1,),
        in_specs=[pl.BlockSpec(memory_space=pltpu.SMEM), pl.BlockSpec((1, plants), lambda i: (0, 0))]
        + [pl.BlockSpec((rows + short, half), lambda i: (0, 0))] * (len(terms) * SPLIT),
        out_specs=[
            pl.BlockSpec((rows + short, SPLIT * half), lambda i: (0, 0)),
            pl.BlockSpec((rows + short, plants), lambda i: (0, 0)),
        ],
        out_shape=[
            jax.ShapeDtypeStruct((rows + short, SPLIT * half), jnp.float32),
            jax.ShapeDtypeStruct((rows + short, plants), jnp.float32),
        ],
        compiler_params=vmem(48),
        cost_estimate=FREE,
        name="finish",
    )(bus, plant_bus[None, :], *[part for term in terms for part in term])
    return (grad[:rows], found[:rows]) if short else (grad, found)


def total_of(terms):
    totals = []
    for part, *more in zip(*terms):
        for term in more:
            part = part + term.astype(jnp.float32)
        totals.append(part.astype(jnp.bfloat16))
    return totals


def make_shards(box, buses):
    steps = plan(box)
    targets = {step_back(step[3], step[1], step[2], box) for step in steps if step[0] == REDUCE}
    own = (0, 0, 0)

    def shards(net_load, release, plant_bus, efficiency, ptdf, branch_class, class_limit, class_price):
        rows = net_load.shape[0]
        bus = lax.axis_index("bus").astype(jnp.int32)[None]
        inject = inject_of(bus, net_load, release, efficiency, plant_bus)
        onehot = (branch_class[:, None] == jnp.arange(class_limit.shape[0])[None, :]).astype(jnp.float32)
        limit = jnp.sum(onehot * class_limit[None, :], axis=1)[None, :]
        price = jnp.sum(onehot * class_price[None, :], axis=1)[None, :]

        def over_bus(value):
            if buses == 2:
                return value, lax.ppermute(value, "bus", [(0, 1), (1, 0)])
            return lax.psum(value, "bus"), jnp.zeros_like(value)

        have, terms, flows, over = {own: inject}, {}, {}, []
        for step in steps:
            if step[0] == FLOWS:
                _, batch, labels, waits = step
                blocks = [have[label] for label in labels]
                blocks[-1] = [after(part, [over[i] for i in waits]) for part in blocks[-1]]
                flows[batch] = labels, over_bus(flows_of(blocks, ptdf))
                over.append(flows[batch][1][0])
            elif step[0] == GRADS:
                labels, sides = flows[step[1]]
                types = [jnp.float32 if label in targets else jnp.bfloat16 for label in labels]
                parts = grads_of(*sides, limit, price, ptdf, rows, types)
                terms.update((label, [part]) for label, part in zip(labels, parts))
                over.append(parts[0][0])
            else:
                kind, axis, shift, label, waits = step
                near = step_back(label, axis, shift, box)
                block = have[near] if kind == GATHER else total_of(terms[label])
                waits = [over[i] for i in waits]
                pairs = moves(axis, shift if kind == GATHER else -shift, box)
                with jax.named_scope(f"send_{len(over)}"):
                    came = [lax.ppermute(after(part, waits), "br", pairs) for part in block]
                if kind == GATHER:
                    have[label] = came
                else:
                    terms[near].append(came)
                over.append(came[-1])
        grad_bus, found = finish_of(bus, plant_bus, terms[own])
        mine, other = over_bus(found)
        grad_release = (mine + other) * efficiency[None, :]
        return (grad_bus, grad_release)

    return shards


def solution(mesh):
    placed = (P("br", "bus"), P("br", None), P(), P(), P("br", "bus"), P("br"), P(), P())
    return jax.shard_map(
        make_shards(chip_box(mesh.shape["br"]), mesh.shape["bus"]),
        mesh=mesh,
        in_specs=placed,
        out_specs=(P("br", "bus"), P("br", None)),
        check_vma=False,
    )
```

time: 141 us -> 137 us (0.972)
  waiting for transfers between devices: 69.8 us -> 65.3 us
  local copies, waits for them, and re-layouts: 6.39 us -> 4.25 us
  Pallas kernels: 22.7 us -> 24.4 us
    ppermute x30, waiting for transfers between devices: 67.5 us -> 63 us  [shards(): came = [lax.ppermute(after(part, waits), 'br', pairs) for part in block]]
    unnamed x24 -> x16, local copies, waits for them, and re-layouts: 6.39 us -> 4.25 us
    pallas_call x8, Pallas kernels: 22.7 us -> 24.4 us  [the longest x3 11 us: flows_of(): pl.pallas_call(functools.partial(flows_kernel, count), grid=(steps,), in_...]
    ppermute x30, starting transfers between devices: 38.2 us -> 39.6 us  [shards(): came = [lax.ppermute(after(part, waits), 'br', pairs) for part in block]]
  transfers between devices with their start and end apart: 34 -> 34, of which waited for: 16 -> 18; matrix products, arithmetic and copies ran while one was open for 1% -> 1% of each run, Pallas kernels for 13% -> 13%
where the time goes in v3:
time: 137 us
  waiting for transfers between devices  65.3 us (48%)
  starting transfers between devices  40.2 us (29%)
  Pallas kernels  24.4 us (18%)
  local copies, waits for them, and re-layouts  4.25 us (3%)
  other arithmetic  1.67 us (1%)
    ppermute x30, waiting for transfers between devices, shards(): came = [lax.ppermute(after(part, waits), 'br', pairs) for part in block]  63 us
    ppermute x30, starting transfers between devices, shards(): came = [lax.ppermute(after(part, waits), 'br', pairs) for part in block]  39.6 us
    pallas_call x3, Pallas kernels, flows_of(): pl.pallas_call(functools.partial(flows_kernel, count), grid=(steps,), in_...  11 us
    pallas_call x3, Pallas kernels, grads_of(): pl.pallas_call(functools.partial(grads_kernel, rows), grid=(steps,), in_s...  6.72 us
    pallas_call x1, Pallas kernels, inject_of(): pl.pallas_call(inject_kernel, grid=(steps,), in_specs=[pl.BlockSpec(memor...  4.83 us
    unnamed x16, local copies, waits for them, and re-layouts  4.25 us
  transfers between devices with their start and end apart: 34, of which 18 were waited for; matrix products, arithmetic and copies ran while one was open for 1% of the time, Pallas kernels for 13%

profile of v3, /device:TPU:0, one launch (start us, length us, event | category | flops | bytes accessed | tf_op | source)
XLA Modules:
  0.0 136.6 jit_solution(15308083348207289494)
XLA Ops:
  0.7 4.8 %inject.1.refs_0_ = bf16[8,30208]{1,0:T(8,128)(2,1)} custom-call(s32[1]{0:T(128)} %bitcast.bus_ref, f32[8,1024]{1,0:T(8,128)} %release_ref.1, f32[1,1024]{1,0:T(1,128)} %bitcast.13, s32[1,1024]{1,0:T(1,128)} %bitcast.5, bf16[8,30208]{1,0:T(8,128)(2,1)} %refs_0_.4), custom_call_target="tpu_custom_call" | custom-call | tf_op jit(solution)/shard_map/inject/pallas_call | solution.py:194
  5.5 5.0 %collective-permute-start = (bf16[8,30208]{1,0:T(8,128)(2,1)}, bf16[8,30208]{1,0:T(8,128)(2,1)S(1)}, u32[]{:S(2)}, u32[]{:S(2)}) collective-permute-start(bf16[8,30208]{1,0:T(8,128)(2,1)} %inject.1.refs_0_), channel_id=1, source_target_pairs={{0,24},{2,26},{4,28},{6,30},{8,0},{10,2},{12,4},{14,6},{16,8},{18,... | collective-permute-start | bytes 1449992 | tf_op jit(solution)/shard_map/send_0/ppermute | solution.py:384
  10.5 1.5 %collective-permute-start.1 = (bf16[8,30208]{1,0:T(8,128)(2,1)}, bf16[8,30208]{1,0:T(8,128)(2,1)S(1)}, u32[]{:S(2)}, u32[]{:S(2)}) collective-permute-start(bf16[8,30208]{1,0:T(8,128)(2,1)} %inject.1.refs_0_), channel_id=1, source_target_pairs={{0,2},{2,0},{4,6},{6,4},{8,10},{10,8},{12,14},{14,12},{16,18},{18,... | collective-permute-start | bytes 1449992 | tf_op jit(solution)/shard_map/send_1/ppermute | solution.py:384
  12.0 1.5 %collective-permute-start.2 = (bf16[8,30208]{1,0:T(8,128)(2,1)}, bf16[8,30208]{1,0:T(8,128)(2,1)S(1)}, u32[]{:S(2)}, u32[]{:S(2)}) collective-permute-start(bf16[8,30208]{1,0:T(8,128)(2,1)} %inject.1.refs_0_), channel_id=1, source_target_pairs={{0,4},{2,6},{4,0},{6,2},{8,12},{10,14},{12,8},{14,10},{16,20},{18,... | collective-permute-start | bytes 1449992 | tf_op jit(solution)/shard_map/send_2/ppermute | solution.py:384
  13.6 7.6 %collective-permute-done.refs_1_ = bf16[8,30208]{1,0:T(8,128)(2,1)S(1)} collective-permute-done((bf16[8,30208]{1,0:T(8,128)(2,1)}, bf16[8,30208]{1,0:T(8,128)(2,1)S(1)}, u32[]{:S(2)}, u32[]{:S(2)}) %collective-permute-start) | collective-permute-done | bytes 483360 | tf_op jit(solution)/shard_map/send_0/ppermute | solution.py:384
  21.2 4.2 %collective-permute-start.3 = (bf16[8,30208]{1,0:T(8,128)(2,1)S(1)}, bf16[8,30208]{1,0:T(8,128)(2,1)S(1)}, u32[]{:S(2)}, u32[]{:S(2)}) collective-permute-start(bf16[8,30208]{1,0:T(8,128)(2,1)S(1)} %collective-permute-done.refs_1_), channel_id=1, source_target_pairs={{0,24},{2,26},{4,28},{6,30},{8,0},{10,2},{12,4},{14,6},{16,8},{18,... | collective-permute-start | bytes 1449992 | tf_op jit(solution)/shard_map/send_3/ppermute | solution.py:384
  25.3 1.5 %collective-permute-start.4 = (bf16[8,30208]{1,0:T(8,128)(2,1)S(1)}, bf16[8,30208]{1,0:T(8,128)(2,1)S(1)}, u32[]{:S(2)}, u32[]{:S(2)}) collective-permute-start(bf16[8,30208]{1,0:T(8,128)(2,1)S(1)} %collective-permute-done.refs_1_), channel_id=1, source_target_pairs={{0,2},{2,0},{4,6},{6,4},{8,10},{10,8},{12,14},{14,12},{16,18},{18,... | collective-permute-start | bytes 1449992 | tf_op jit(solution)/shard_map/send_4/ppermute | solution.py:384
  26.8 1.5 %collective-permute-start.5 = (bf16[8,30208]{1,0:T(8,128)(2,1)S(1)}, bf16[8,30208]{1,0:T(8,128)(2,1)S(1)}, u32[]{:S(2)}, u32[]{:S(2)}) collective-permute-start(bf16[8,30208]{1,0:T(8,128)(2,1)S(1)} %collective-permute-done.1.refs_2_), channel_id=1, source_target_pairs={{0,4},{2,6},{4,0},{6,2},{8,12},{10,14},{12,8},{14,10},{16,20},{18,... | collective-permute-start | bytes 1449992 | tf_op jit(solution)/shard_map/send_5/ppermute | solution.py:384
  28.4 7.9 %collective-permute-done.3.refs_4_ = bf16[8,30208]{1,0:T(8,128)(2,1)S(1)} collective-permute-done((bf16[8,30208]{1,0:T(8,128)(2,1)S(1)}, bf16[8,30208]{1,0:T(8,128)(2,1)S(1)}, u32[]{:S(2)}, u32[]{:S(2)}) %collective-permute-start.3) | collective-permute-done | bytes 483360 | tf_op jit(solution)/shard_map/send_3/ppermute | solution.py:384
  36.3 0.7 collective-permute-done.4.refs_5_
  37.0 1.5 %collective-permute-start.7 = (bf16[8,30208]{1,0:T(8,128)(2,1)S(1)}, bf16[8,30208]{1,0:T(8,128)(2,1)S(1)}, u32[]{:S(2)}, u32[]{:S(2)}) collective-permute-start(bf16[8,30208]{1,0:T(8,128)(2,1)S(1)} %collective-permute-done.3.refs_4_), channel_id=1, source_target_pairs={{0,2},{2,0},{4,6},{6,4},{8,10},{10,8},{12,14},{14,12},{16,18},{18,... | collective-permute-start | bytes 1449992 | tf_op jit(solution)/shard_map/send_7/ppermute | solution.py:384
  38.5 1.5 %collective-permute-start.8 = (bf16[8,30208]{1,0:T(8,128)(2,1)S(1)}, bf16[8,30208]{1,0:T(8,128)(2,1)S(1)}, u32[]{:S(2)}, u32[]{:S(2)}) collective-permute-start(bf16[8,30208]{1,0:T(8,128)(2,1)S(1)} %collective-permute-done.4.refs_5_), channel_id=1, source_target_pairs={{0,4},{2,6},{4,0},{6,2},{8,12},{10,14},{12,8},{14,10},{16,20},{18,... | collective-permute-start | bytes 1449992 | tf_op jit(solution)/shard_map/send_8/ppermute | solution.py:384
  40.0 8.3 %collective-permute-done.6.refs_7_ = bf16[8,30208]{1,0:T(8,128)(2,1)S(1)} collective-permute-done((bf16[8,30208]{1,0:T(8,128)(2,1)S(1)}, bf16[8,30208]{1,0:T(8,128)(2,1)S(1)}, u32[]{:S(2)}, u32[]{:S(2)}) %collective-permute-start.6) | collective-permute-done | bytes 483360 | tf_op jit(solution)/shard_map/send_6/ppermute | solution.py:384
  48.3 1.5 %collective-permute-start.12 = (bf16[8,30208]{1,0:T(8,128)(2,1)S(1)}, bf16[8,30208]{1,0:T(8,128)(2,1)S(1)}, u32[]{:S(2)}, u32[]{:S(2)}) collective-permute-start(bf16[8,30208]{1,0:T(8,128)(2,1)S(1)} %collective-permute-done.6.refs_7_), channel_id=1, source_target_pairs={{0,2},{2,0},{4,6},{6,4},{8,10},{10,8},{12,14},{14,12},{16,18},{18,... | collective-permute-start | bytes 1449992 | tf_op jit(solution)/shard_map/send_12/ppermute | solution.py:384
  49.8 1.5 %collective-permute-start.14 = (bf16[8,30208]{1,0:T(8,128)(2,1)S(1)}, bf16[8,30208]{1,0:T(8,128)(2,1)S(1)}, u32[]{:S(2)}, u32[]{:S(2)}) collective-permute-start(bf16[8,30208]{1,0:T(8,128)(2,1)S(1)} %collective-permute-done.7.refs_8_), channel_id=1, source_target_pairs={{0,4},{2,6},{4,0},{6,2},{8,12},{10,14},{12,8},{14,10},{16,20},{18,... | collective-permute-start | bytes 1449992 | tf_op jit(solution)/shard_map/send_13/ppermute | solution.py:384
  51.3 3.2 %copy-done = bf16[128,30208]{1,0:T(8,128)(2,1)S(1)} copy-done((bf16[128,30208]{1,0:T(8,128)(2,1)S(1)}, bf16[128,30208]{1,0:T(8,128)(2,1)}, u32[]{:S(2)}) %copy-start) | copy-done | bytes 7733272
  54.5 1.0 copy-done.2
  55.5 3.9 %flows.3.mine_ref = f32[80,128]{1,0:T(8,128)S(1)} custom-call(bf16[8,30208]{1,0:T(8,128)(2,1)S(1)} %copy-done.2, bf16[8,30208]{1,0:T(8,128)(2,1)S(1)} %collective-permute-done.refs_1_, bf16[8,30208]{1,0:T(8,128)(2,1)S(1)} %collective-permute-done.1.refs_2_, bf16[8,30208]{1,0:T(8,128)(2,1)S(1)} %collective-permute-done.2.refs_3_, ...), custom_call_target="tpu_custom_call" | custom-call | tf_op jit(solution)/shard_map/flows/pallas_call | solution.py:241
  59.4 1.4 collective-permute-start.11
  60.8 0.5 collective-permute-start.13
  61.3 1.4 %collective-permute-start.15 = (bf16[8,30208]{1,0:T(8,128)(2,1)S(1)}, bf16[8,30208]{1,0:T(8,128)(2,1)S(1)}, u32[]{:S(2)}, u32[]{:S(2)}) collective-permute-start(bf16[8,30208]{1,0:T(8,128)(2,1)S(1)} %collective-permute-done.refs_1_), channel_id=1, source_target_pairs={{0,4},{2,6},{4,0},{6,2},{8,12},{10,14},{12,8},{14,10},{16,20},{18,... | collective-permute-start | bytes 1449992 | tf_op jit(solution)/shard_map/send_18/ppermute | solution.py:384
  62.8 0.1 select_reduce_fusion
  62.8 1.1 collective-permute-done.9.other_ref
  64.0 2.5 %grads.3 = (f32[8,30208]{1,0:T(8,128)S(1)}, bf16[8,30208]{1,0:T(8,128)(2,1)S(1)}, f32[8,30208]{1,0:T(8,128)S(1)}, f32[8,30208]{1,0:T(8,128)S(1)}, f32[8,30208]{1...) custom-call(f32[80,128]{1,0:T(8,128)S(1)} %flows.3.mine_ref, ...), custom_call_target="tpu_custom_call" | custom-call | tf_op jit(solution)/shard_map/grads/pallas_call | solution.py:276
  66.5 3.6 %flows.5.mine_ref = f32[24,128]{1,0:T(8,128)S(1)} custom-call(bf16[8,30208]{1,0:T(8,128)(2,1)S(1)} %collective-permute-done.10.refs_0_, bf16[8,30208]{1,0:T(8,128)(2,1)S(1)} %collective-permute-done.12.refs_1_, bf16[8,30208]{1,0:T(8,128)(2,1)S(1)} %collective-permute-done.14.refs_2_, bf16[128,30208]{1,0:T(8,128)(2,1)S(1)} %copy-done.1), custom_call_target="tpu_custom_call" | custom-call | tf_op jit(solution)/shard_map/flows/pallas_call | solution.py:241
  70.0 0.5 collective-permute-done.11.refs_0_
  70.6 1.1 collective-permute-start.16
  71.7 1.5 %collective-permute-start.19 = (bf16[8,30208]{1,0:T(8,128)(2,1)S(1)}, bf16[8,30208]{1,0:T(8,128)(2,1)S(1)}, u32[]{:S(2)}, u32[]{:S(2)}) collective-permute-start(bf16[8,30208]{1,0:T(8,128)(2,1)S(1)} %get-tuple-element.67), channel_id=1, source_target_pairs={{0,2},{2,0},{4,6},{6,4},{8,10},{10,8},{12,14},{14,12},{16,18},{18,... | collective-permute-start | bytes 1449992 | tf_op jit(solution)/shard_map/send_22/ppermute | solution.py:384
  73.2 1.5 %collective-permute-start.23 = (bf16[8,30208]{1,0:T(8,128)(2,1)S(1)}, bf16[8,30208]{1,0:T(8,128)(2,1)S(1)}, u32[]{:S(2)}, u32[]{:S(2)}) collective-permute-start(bf16[8,30208]{1,0:T(8,128)(2,1)S(1)} %get-tuple-element.75), channel_id=1, source_target_pairs={{0,4},{2,6},{4,0},{6,2},{8,12},{10,14},{12,8},{14,10},{16,20},{18,... | collective-permute-start | bytes 1449992 | tf_op jit(solution)/shard_map/send_21/ppermute | solution.py:384
  74.7 3.5 %flows.4.mine_ref = f32[24,128]{1,0:T(8,128)S(1)} custom-call(bf16[8,30208]{1,0:T(8,128)(2,1)S(1)} %collective-permute-done.11.refs_0_, bf16[8,30208]{1,0:T(8,128)(2,1)S(1)} %collective-permute-done.13.refs_1_, bf16[8,30208]{1,0:T(8,128)(2,1)S(1)} %collective-permute-done.15.refs_2_, bf16[128,30208]{1,0:T(8,128)(2,1)S(1)} %copy-done.1), custom_call_target="tpu_custom_call" | custom-call | tf_op jit(solution)/shard_map/flows/pallas_call | solution.py:241
  78.2 0.6 collective-permute-start.18
  78.8 2.1 %grads.5 = (f32[8,30208]{1,0:T(8,128)S(1)}, bf16[8,30208]{1,0:T(8,128)(2,1)S(1)}, bf16[8,30208]{1,0:T(8,128)(2,1)S(1)}) custom-call(f32[24,128]{1,0:T(8,128)S(1)} %flows.5.mine_ref, f32[24,128]{1,0:T(8,128)S(1)} %collective-permute-done.21.other_ref, f32[1,128]{1,0:T(1,128)S(1)} %bitcast.11, f32[1,128]{1,0:T(1,128)S(1)} %bitcast.8, ...), custom_call_target="tpu_custom_call" | custom-call | tf_op jit(solution)/shard_map/grads/pallas_call | solution.py:276
  80.9 2.1 %grads.4 = (bf16[8,30208]{1,0:T(8,128)(2,1)S(1)}, bf16[8,30208]{1,0:T(8,128)(2,1)S(1)}, f32[8,30208]{1,0:T(8,128)S(1)}) custom-call(f32[24,128]{1,0:T(8,128)S(1)} %flows.4.mine_ref, f32[24,128]{1,0:T(8,128)S(1)} %collective-permute-done.18.other_ref, f32[1,128]{1,0:T(1,128)S(1)} %bitcast.12, f32[1,128]{1,0:T(1,128)S(1)} %bitcast.9, ...), custom_call_target="tpu_custom_call" | custom-call | tf_op jit(solution)/shard_map/grads/pallas_call | solution.py:276
  83.1 2.2 %collective-permute-done.16 = bf16[8,30208]{1,0:T(8,128)(2,1)S(1)} collective-permute-done((bf16[8,30208]{1,0:T(8,128)(2,1)S(1)}, bf16[8,30208]{1,0:T(8,128)(2,1)S(1)}, u32[]{:S(2)}, u32[]{:S(2)}) %collective-permute-start.16) | collective-permute-done | bytes 483360 | tf_op jit(solution)/shard_map/send_23/ppermute | solution.py:384
  85.3 1.0 collective-permute-start.22
  86.3 1.5 %collective-permute-start.24 = (bf16[8,30208]{1,0:T(8,128)(2,1)S(1)}, bf16[8,30208]{1,0:T(8,128)(2,1)S(1)}, u32[]{:S(2)}, u32[]{:S(2)}) collective-permute-start(bf16[8,30208]{1,0:T(8,128)(2,1)S(1)} %get-tuple-element.76), channel_id=1, source_target_pairs={{0,4},{2,6},{4,0},{6,2},{8,12},{10,14},{12,8},{14,10},{16,20},{18,... | collective-permute-start | bytes 1449992 | tf_op jit(solution)/shard_map/send_24/ppermute | solution.py:384
  87.8 0.2 add_convert_fusion.3
  88.0 0.1 add_convert_fusion.6
  88.1 11.1 %collective-permute-done.17.refs_1_ = bf16[8,30208]{1,0:T(8,128)(2,1)S(1)} collective-permute-done((bf16[8,30208]{1,0:T(8,128)(2,1)S(1)}, bf16[8,30208]{1,0:T(8,128)(2,1)S(1)}, u32[]{:S(2)}, u32[]{:S(2)}) %collective-permute-start.17) | collective-permute-done | bytes 483360 | tf_op jit(solution)/shard_map/send_26/ppermute | solution.py:384
  99.2 0.4 collective-permute-start.25
  99.5 0.1 add_convert_fusion.2
  99.6 0.6 collective-permute-start.28
  100.3 0.1 add_convert_fusion.4
  100.4 10.0 %collective-permute-done.25 = bf16[8,30208]{1,0:T(8,128)(2,1)S(1)} collective-permute-done((bf16[8,30208]{1,0:T(8,128)(2,1)S(1)}, bf16[8,30208]{1,0:T(8,128)(2,1)S(1)}, u32[]{:S(2)}, u32[]{:S(2)}) %collective-permute-start.25) | collective-permute-done | bytes 483360 | tf_op jit(solution)/shard_map/send_27/ppermute | solution.py:384
  110.4 0.3 collective-permute-start.26
  110.6 0.1 collective-permute-done.28
  110.8 0.6 collective-permute-start.29
  111.4 0.2 add_convert_fusion.1
  111.5 0.6 collective-permute-done.20
  112.2 2.6 %collective-permute-start.31 = (bf16[8,30208]{1,0:T(8,128)(2,1)S(1)}, bf16[8,30208]{1,0:T(8,128)(2,1)S(1)}, u32[]{:S(2)}, u32[]{:S(2)}) collective-permute-start(bf16[8,30208]{1,0:T(8,128)(2,1)S(1)} %add_convert_fusion.1), channel_id=1, source_target_pairs={{0,24},{2,26},{4,28},{6,30},{8,0},{10,2},{12,4},{14,6},{16,8},{18,... | collective-permute-start | bytes 1449992 | tf_op jit(solution)/shard_map/send_32/ppermute | solution.py:384
  114.8 0.1 add_convert_fusion.5
  114.9 6.7 %collective-permute-done.26 = bf16[8,30208]{1,0:T(8,128)(2,1)S(1)} collective-permute-done((bf16[8,30208]{1,0:T(8,128)(2,1)S(1)}, bf16[8,30208]{1,0:T(8,128)(2,1)S(1)}, u32[]{:S(2)}, u32[]{:S(2)}) %collective-permute-start.26) | collective-permute-done | bytes 483360 | tf_op jit(solution)/shard_map/send_30/ppermute | solution.py:384
  121.6 0.3 collective-permute-start.27
  121.9 0.1 collective-permute-done.29
  122.0 0.6 collective-permute-start.30
  122.6 0.5 collective-permute-done.31
  123.1 0.2 add_convert_fusion
  123.3 3.0 %collective-permute-start.32 = (bf16[8,30208]{1,0:T(8,128)(2,1)S(1)}, bf16[8,30208]{1,0:T(8,128)(2,1)S(1)}, u32[]{:S(2)}, u32[]{:S(2)}) collective-permute-start(bf16[8,30208]{1,0:T(8,128)(2,1)S(1)} %add_convert_fusion), channel_id=1, source_target_pairs={{0,24},{2,26},{4,28},{6,30},{8,0},{10,2},{12,4},{14,6},{16,8},{18,... | collective-permute-start | bytes 1449992 | tf_op jit(solution)/shard_map/send_35/ppermute | solution.py:384
  126.4 4.6 %collective-permute-done.27.refs_2_ = bf16[8,30208]{1,0:T(8,128)(2,1)S(1)} collective-permute-done((bf16[8,30208]{1,0:T(8,128)(2,1)S(1)}, bf16[8,30208]{1,0:T(8,128)(2,1)S(1)}, u32[]{:S(2)}, u32[]{:S(2)}) %collective-permute-start.27) | collective-permute-done | bytes 483360 | tf_op jit(solution)/shard_map/send_33/ppermute | solution.py:384
  131.0 0.2 collective-permute-done.30.refs_3_
  131.2 1.7 %collective-permute-done.32.refs_4_ = bf16[8,30208]{1,0:T(8,128)(2,1)S(1)} collective-permute-done((bf16[8,30208]{1,0:T(8,128)(2,1)S(1)}, bf16[8,30208]{1,0:T(8,128)(2,1)S(1)}, u32[]{:S(2)}, u32[]{:S(2)}) %collective-permute-start.32) | collective-permute-done | bytes 483360 | tf_op jit(solution)/shard_map/send_35/ppermute | solution.py:384
  132.9 1.9 %finish.1 = (f32[8,30208]{1,0:T(8,128)}, f32[8,1024]{1,0:T(8,128)S(1)}) custom-call(s32[1]{0:T(128)} %bitcast.bus_ref, s32[1,1024]{1,0:T(1,128)S(1)} %bitcast.6, f32[8,30208]{1,0:T(8,128)S(1)} %get-tuple-element.53.refs_0_, bf16[8,30208]{1,0:T(8,128)(2,1)S(1)} %collective-permute-done.17.refs_1_, bf16[8,30208]{1,0:T(8,128)(2,1)S(1)} %collective-permute-done.27.refs_2_, ...), custom_call_target="tpu_custom_call" | custom-call | tf_op jit(solution)/shard_map/finish/pallas_call | solution.py:316
  134.7 1.2 collective-permute-done.33
  136.0 0.6 add_multiply_fusion
  (37 shorter events, 0.1 us)
Async XLA Ops:
  0.6 62.1 %copy-start.5 = (f32[16]{0:T(128)S(1)}, f32[16]{0:T(128)}, u32[]{:S(2)}) copy-start(f32[16]{0:T(128)} %param.15) | copy-start | bytes 196
  0.6 62.1 %copy-start.6 = (s32[128]{0:T(128)S(1)}, s32[128]{0:T(128)}, u32[]{:S(2)}) copy-start(s32[128]{0:T(128)} %param.13) | copy-start | bytes 1540
  0.7 62.1 %copy-start.7 = (f32[16]{0:T(128)S(1)}, f32[16]{0:T(128)}, u32[]{:S(2)}) copy-start(f32[16]{0:T(128)} %param.14) | copy-start | bytes 196
  5.5 15.7 %collective-permute-start = (bf16[8,30208]{1,0:T(8,128)(2,1)}, bf16[8,30208]{1,0:T(8,128)(2,1)S(1)}, u32[]{:S(2)}, u32[]{:S(2)}) collective-permute-start(bf16[8,30208]{1,0:T(8,128)(2,1)} %inject.1.refs_0_), channel_id=1, source_target_pairs={{0,24},{2,26},{4,28},{6,30},{8,0},{10,2},{12,4},{14,6},{16,8},{18,... | collective-permute-start | bytes 1449992 | tf_op jit(solution)/shard_map/send_0/ppermute | solution.py:384
  10.5 14.8 %collective-permute-start.1 = (bf16[8,30208]{1,0:T(8,128)(2,1)}, bf16[8,30208]{1,0:T(8,128)(2,1)S(1)}, u32[]{:S(2)}, u32[]{:S(2)}) collective-permute-start(bf16[8,30208]{1,0:T(8,128)(2,1)} %inject.1.refs_0_), channel_id=1, source_target_pairs={{0,2},{2,0},{4,6},{6,4},{8,10},{10,8},{12,14},{14,12},{16,18},{18,... | collective-permute-start | bytes 1449992 | tf_op jit(solution)/shard_map/send_1/ppermute | solution.py:384
  12.0 14.8 %collective-permute-start.2 = (bf16[8,30208]{1,0:T(8,128)(2,1)}, bf16[8,30208]{1,0:T(8,128)(2,1)S(1)}, u32[]{:S(2)}, u32[]{:S(2)}) collective-permute-start(bf16[8,30208]{1,0:T(8,128)(2,1)} %inject.1.refs_0_), channel_id=1, source_target_pairs={{0,4},{2,6},{4,0},{6,2},{8,12},{10,14},{12,8},{14,10},{16,20},{18,... | collective-permute-start | bytes 1449992 | tf_op jit(solution)/shard_map/send_2/ppermute | solution.py:384
  21.2 15.1 %collective-permute-start.3 = (bf16[8,30208]{1,0:T(8,128)(2,1)S(1)}, bf16[8,30208]{1,0:T(8,128)(2,1)S(1)}, u32[]{:S(2)}, u32[]{:S(2)}) collective-permute-start(bf16[8,30208]{1,0:T(8,128)(2,1)S(1)} %collective-permute-done.refs_1_), channel_id=1, source_target_pairs={{0,24},{2,26},{4,28},{6,30},{8,0},{10,2},{12,4},{14,6},{16,8},{18,... | collective-permute-start | bytes 1449992 | tf_op jit(solution)/shard_map/send_3/ppermute | solution.py:384
  25.3 11.6 %collective-permute-start.4 = (bf16[8,30208]{1,0:T(8,128)(2,1)S(1)}, bf16[8,30208]{1,0:T(8,128)(2,1)S(1)}, u32[]{:S(2)}, u32[]{:S(2)}) collective-permute-start(bf16[8,30208]{1,0:T(8,128)(2,1)S(1)} %collective-permute-done.refs_1_), channel_id=1, source_target_pairs={{0,2},{2,0},{4,6},{6,4},{8,10},{10,8},{12,14},{14,12},{16,18},{18,... | collective-permute-start | bytes 1449992 | tf_op jit(solution)/shard_map/send_4/ppermute | solution.py:384
  26.8 11.6 %collective-permute-start.5 = (bf16[8,30208]{1,0:T(8,128)(2,1)S(1)}, bf16[8,30208]{1,0:T(8,128)(2,1)S(1)}, u32[]{:S(2)}, u32[]{:S(2)}) collective-permute-start(bf16[8,30208]{1,0:T(8,128)(2,1)S(1)} %collective-permute-done.1.refs_2_), channel_id=1, source_target_pairs={{0,4},{2,6},{4,0},{6,2},{8,12},{10,14},{12,8},{14,10},{16,20},{18,... | collective-permute-start | bytes 1449992 | tf_op jit(solution)/shard_map/send_5/ppermute | solution.py:384
  36.3 12.0 %collective-permute-start.6 = (bf16[8,30208]{1,0:T(8,128)(2,1)S(1)}, bf16[8,30208]{1,0:T(8,128)(2,1)S(1)}, u32[]{:S(2)}, u32[]{:S(2)}) collective-permute-start(bf16[8,30208]{1,0:T(8,128)(2,1)S(1)} %collective-permute-done.2.refs_3_), channel_id=1, source_target_pairs={{0,8},{2,10},{4,12},{6,14},{8,16},{10,18},{12,20},{14,22},{16,24},... | collective-permute-start | bytes 1449992 | tf_op jit(solution)/shard_map/send_6/ppermute | solution.py:384
  37.0 11.3 %collective-permute-start.7 = (bf16[8,30208]{1,0:T(8,128)(2,1)S(1)}, bf16[8,30208]{1,0:T(8,128)(2,1)S(1)}, u32[]{:S(2)}, u32[]{:S(2)}) collective-permute-start(bf16[8,30208]{1,0:T(8,128)(2,1)S(1)} %collective-permute-done.3.refs_4_), channel_id=1, source_target_pairs={{0,2},{2,0},{4,6},{6,4},{8,10},{10,8},{12,14},{14,12},{16,18},{18,... | collective-permute-start | bytes 1449992 | tf_op jit(solution)/shard_map/send_7/ppermute | solution.py:384
  38.5 11.3 %collective-permute-start.8 = (bf16[8,30208]{1,0:T(8,128)(2,1)S(1)}, bf16[8,30208]{1,0:T(8,128)(2,1)S(1)}, u32[]{:S(2)}, u32[]{:S(2)}) collective-permute-start(bf16[8,30208]{1,0:T(8,128)(2,1)S(1)} %collective-permute-done.4.refs_5_), channel_id=1, source_target_pairs={{0,4},{2,6},{4,0},{6,2},{8,12},{10,14},{12,8},{14,10},{16,20},{18,... | collective-permute-start | bytes 1449992 | tf_op jit(solution)/shard_map/send_8/ppermute | solution.py:384
  48.3 11.1 %collective-permute-start.10 = (bf16[8,30208]{1,0:T(8,128)(2,1)}, bf16[8,30208]{1,0:T(8,128)(2,1)S(1)}, u32[]{:S(2)}, u32[]{:S(2)}) collective-permute-start(bf16[8,30208]{1,0:T(8,128)(2,1)} %inject.1.refs_0_), channel_id=1, source_target_pairs={{0,8},{2,10},{4,12},{6,14},{8,16},{10,18},{12,20},{14,22},{16,24},... | collective-permute-start | bytes 1449992 | tf_op jit(solution)/shard_map/send_11/ppermute | solution.py:384
  48.3 12.5 %collective-permute-start.12 = (bf16[8,30208]{1,0:T(8,128)(2,1)S(1)}, bf16[8,30208]{1,0:T(8,128)(2,1)S(1)}, u32[]{:S(2)}, u32[]{:S(2)}) collective-permute-start(bf16[8,30208]{1,0:T(8,128)(2,1)S(1)} %collective-permute-done.6.refs_7_), channel_id=1, source_target_pairs={{0,2},{2,0},{4,6},{6,4},{8,10},{10,8},{12,14},{14,12},{16,18},{18,... | collective-permute-start | bytes 1449992 | tf_op jit(solution)/shard_map/send_12/ppermute | solution.py:384
  49.8 11.5 %collective-permute-start.14 = (bf16[8,30208]{1,0:T(8,128)(2,1)S(1)}, bf16[8,30208]{1,0:T(8,128)(2,1)S(1)}, u32[]{:S(2)}, u32[]{:S(2)}) collective-permute-start(bf16[8,30208]{1,0:T(8,128)(2,1)S(1)} %collective-permute-done.7.refs_8_), channel_id=1, source_target_pairs={{0,4},{2,6},{4,0},{6,2},{8,12},{10,14},{12,8},{14,10},{16,20},{18,... | collective-permute-start | bytes 1449992 | tf_op jit(solution)/shard_map/send_13/ppermute | solution.py:384
  51.3 3.2 %copy-start = (bf16[128,30208]{1,0:T(8,128)(2,1)S(1)}, bf16[128,30208]{1,0:T(8,128)(2,1)}, u32[]{:S(2)}) copy-start(bf16[128,30208]{1,0:T(8,128)(2,1)} %refs_0_.7) | copy-start | bytes 23199748
  54.5 1.0 copy-start.2
  55.5 8.4 %copy-start.1 = (bf16[128,30208]{1,0:T(8,128)(2,1)S(1)}, bf16[128,30208]{1,0:T(8,128)(2,1)}, u32[]{:S(2)}) copy-start(bf16[128,30208]{1,0:T(8,128)(2,1)} %refs_0_.7) | copy-start | bytes 23199748
  59.4 11.1 %collective-permute-start.11 = (bf16[8,30208]{1,0:T(8,128)(2,1)S(1)}, bf16[8,30208]{1,0:T(8,128)(2,1)S(1)}, u32[]{:S(2)}, u32[]{:S(2)}) collective-permute-start(bf16[8,30208]{1,0:T(8,128)(2,1)S(1)} %collective-permute-done.6.refs_7_), channel_id=1, source_target_pairs={{0,8},{2,10},{4,12},{6,14},{8,16},{10,18},{12,20},{14,22},{16,24},... | collective-permute-start | bytes 1449992 | tf_op jit(solution)/shard_map/send_16/ppermute | solution.py:384
  60.8 10.9 %collective-permute-start.13 = (bf16[8,30208]{1,0:T(8,128)(2,1)S(1)}, bf16[8,30208]{1,0:T(8,128)(2,1)S(1)}, u32[]{:S(2)}, u32[]{:S(2)}) collective-permute-start(bf16[8,30208]{1,0:T(8,128)(2,1)S(1)} %collective-permute-done.10.refs_0_), channel_id=1, source_target_pairs={{0,2},{2,0},{4,6},{6,4},{8,10},{10,8},{12,14},{14,12},{16,18},{18,... | collective-permute-start | bytes 1449992 | tf_op jit(solution)/shard_map/send_17/ppermute | solution.py:384
  61.3 11.8 %collective-permute-start.15 = (bf16[8,30208]{1,0:T(8,128)(2,1)S(1)}, bf16[8,30208]{1,0:T(8,128)(2,1)S(1)}, u32[]{:S(2)}, u32[]{:S(2)}) collective-permute-start(bf16[8,30208]{1,0:T(8,128)(2,1)S(1)} %collective-permute-done.refs_1_), channel_id=1, source_target_pairs={{0,4},{2,6},{4,0},{6,2},{8,12},{10,14},{12,8},{14,10},{16,20},{18,... | collective-permute-start | bytes 1449992 | tf_op jit(solution)/shard_map/send_18/ppermute | solution.py:384
  62.7 1.2 collective-permute-start.9
  70.6 14.7 %collective-permute-start.16 = (bf16[8,30208]{1,0:T(8,128)(2,1)S(1)}, bf16[8,30208]{1,0:T(8,128)(2,1)S(1)}, u32[]{:S(2)}, u32[]{:S(2)}) collective-permute-start(bf16[8,30208]{1,0:T(8,128)(2,1)S(1)} %get-tuple-element.62), channel_id=1, source_target_pairs={{0,8},{2,10},{4,12},{6,14},{8,16},{10,18},{12,20},{14,22},{16,24},... | collective-permute-start | bytes 1449992 | tf_op jit(solution)/shard_map/send_23/ppermute | solution.py:384
  71.7 13.6 %collective-permute-start.19 = (bf16[8,30208]{1,0:T(8,128)(2,1)S(1)}, bf16[8,30208]{1,0:T(8,128)(2,1)S(1)}, u32[]{:S(2)}, u32[]{:S(2)}) collective-permute-start(bf16[8,30208]{1,0:T(8,128)(2,1)S(1)} %get-tuple-element.67), channel_id=1, source_target_pairs={{0,2},{2,0},{4,6},{6,4},{8,10},{10,8},{12,14},{14,12},{16,18},{18,... | collective-permute-start | bytes 1449992 | tf_op jit(solution)/shard_map/send_22/ppermute | solution.py:384
  73.2 13.1 %collective-permute-start.23 = (bf16[8,30208]{1,0:T(8,128)(2,1)S(1)}, bf16[8,30208]{1,0:T(8,128)(2,1)S(1)}, u32[]{:S(2)}, u32[]{:S(2)}) collective-permute-start(bf16[8,30208]{1,0:T(8,128)(2,1)S(1)} %get-tuple-element.75), channel_id=1, source_target_pairs={{0,4},{2,6},{4,0},{6,2},{8,12},{10,14},{12,8},{14,10},{16,20},{18,... | collective-permute-start | bytes 1449992 | tf_op jit(solution)/shard_map/send_21/ppermute | solution.py:384
  74.7 4.1 %collective-permute-start.21 = (f32[24,128]{1,0:T(8,128)S(1)}, f32[24,128]{1,0:T(8,128)S(1)}, u32[]{:S(2)}, u32[]{:S(2)}) collective-permute-start(f32[24,128]{1,0:T(8,128)S(1)} %flows.5.mine_ref), channel_id=1, source_target_pairs={{0,1},{1,0},{2,3},{3,2},{4,5},{5,4},{6,7},{7,6},{8,9},{9,8},{10,11... | collective-permute-start | bytes 36872 | tf_op jit(solution)/shard_map/ppermute | solution.py:360
  78.2 2.7 %collective-permute-start.18 = (f32[24,128]{1,0:T(8,128)S(1)}, f32[24,128]{1,0:T(8,128)S(1)}, u32[]{:S(2)}, u32[]{:S(2)}) collective-permute-start(f32[24,128]{1,0:T(8,128)S(1)} %flows.4.mine_ref), channel_id=1, source_target_pairs={{0,1},{1,0},{2,3},{3,2},{4,5},{5,4},{6,7},{7,6},{8,9},{9,8},{10,11... | collective-permute-start | bytes 36872 | tf_op jit(solution)/shard_map/ppermute | solution.py:360
  85.3 13.9 %collective-permute-start.17 = (bf16[8,30208]{1,0:T(8,128)(2,1)S(1)}, bf16[8,30208]{1,0:T(8,128)(2,1)S(1)}, u32[]{:S(2)}, u32[]{:S(2)}) collective-permute-start(bf16[8,30208]{1,0:T(8,128)(2,1)S(1)} %get-tuple-element.63), channel_id=1, source_target_pairs={{0,8},{2,10},{4,12},{6,14},{8,16},{10,18},{12,20},{14,22},{16,24},... | collective-permute-start | bytes 1449992 | tf_op jit(solution)/shard_map/send_26/ppermute | solution.py:384
  85.3 14.3 %collective-permute-start.22 = (bf16[8,30208]{1,0:T(8,128)(2,1)S(1)}, bf16[8,30208]{1,0:T(8,128)(2,1)S(1)}, u32[]{:S(2)}, u32[]{:S(2)}) collective-permute-start(bf16[8,30208]{1,0:T(8,128)(2,1)S(1)} %get-tuple-element.71), channel_id=1, source_target_pairs={{0,2},{2,0},{4,6},{6,4},{8,10},{10,8},{12,14},{14,12},{16,18},{18,... | collective-permute-start | bytes 1449992 | tf_op jit(solution)/shard_map/send_25/ppermute | solution.py:384
  86.3 12.9 %collective-permute-start.24 = (bf16[8,30208]{1,0:T(8,128)(2,1)S(1)}, bf16[8,30208]{1,0:T(8,128)(2,1)S(1)}, u32[]{:S(2)}, u32[]{:S(2)}) collective-permute-start(bf16[8,30208]{1,0:T(8,128)(2,1)S(1)} %get-tuple-element.76), channel_id=1, source_target_pairs={{0,4},{2,6},{4,0},{6,2},{8,12},{10,14},{12,8},{14,10},{16,20},{18,... | collective-permute-start | bytes 1449992 | tf_op jit(solution)/shard_map/send_24/ppermute | solution.py:384
  87.8 45.1 %copy-start.3 = (s32[1024]{0:T(1024)S(1)}, s32[1024]{0:T(1024)}, u32[]{:S(2)}) copy-start(s32[1024]{0:T(1024)} %param.10) | copy-start | bytes 12292
  88.0 48.0 %copy-start.4 = (f32[1024]{0:T(1024)S(1)}, f32[1024]{0:T(1024)}, u32[]{:S(2)}) copy-start(f32[1024]{0:T(1024)} %param.11) | copy-start | bytes 12292
  99.1 13.0 %collective-permute-start.20 = (bf16[8,30208]{1,0:T(8,128)(2,1)S(1)}, bf16[8,30208]{1,0:T(8,128)(2,1)S(1)}, u32[]{:S(2)}, u32[]{:S(2)}) collective-permute-start(bf16[8,30208]{1,0:T(8,128)(2,1)S(1)} %add_convert_fusion.6), channel_id=1, source_target_pairs={{0,8},{2,10},{4,12},{6,14},{8,16},{10,18},{12,20},{14,22},{16,24},... | collective-permute-start | bytes 1449992 | tf_op jit(solution)/shard_map/send_29/ppermute | solution.py:384
  99.2 11.2 %collective-permute-start.25 = (bf16[8,30208]{1,0:T(8,128)(2,1)S(1)}, bf16[8,30208]{1,0:T(8,128)(2,1)S(1)}, u32[]{:S(2)}, u32[]{:S(2)}) collective-permute-start(bf16[8,30208]{1,0:T(8,128)(2,1)S(1)} %get-tuple-element.77), channel_id=1, source_target_pairs={{0,4},{2,6},{4,0},{6,2},{8,12},{10,14},{12,8},{14,10},{16,20},{18,... | collective-permute-start | bytes 1449992 | tf_op jit(solution)/shard_map/send_27/ppermute | solution.py:384
  99.6 11.1 %collective-permute-start.28 = (bf16[8,30208]{1,0:T(8,128)(2,1)S(1)}, bf16[8,30208]{1,0:T(8,128)(2,1)S(1)}, u32[]{:S(2)}, u32[]{:S(2)}) collective-permute-start(bf16[8,30208]{1,0:T(8,128)(2,1)S(1)} %add_convert_fusion.2), channel_id=1, source_target_pairs={{0,2},{2,0},{4,6},{6,4},{8,10},{10,8},{12,14},{14,12},{16,18},{18,... | collective-permute-start | bytes 1449992 | tf_op jit(solution)/shard_map/send_28/ppermute | solution.py:384
  110.4 11.2 %collective-permute-start.26 = (bf16[8,30208]{1,0:T(8,128)(2,1)S(1)}, bf16[8,30208]{1,0:T(8,128)(2,1)S(1)}, u32[]{:S(2)}, u32[]{:S(2)}) collective-permute-start(bf16[8,30208]{1,0:T(8,128)(2,1)S(1)} %add_convert_fusion.4), channel_id=1, source_target_pairs={{0,4},{2,6},{4,0},{6,2},{8,12},{10,14},{12,8},{14,10},{16,20},{18,... | collective-permute-start | bytes 1449992 | tf_op jit(solution)/shard_map/send_30/ppermute | solution.py:384
  110.8 11.2 %collective-permute-start.29 = (bf16[8,30208]{1,0:T(8,128)(2,1)S(1)}, bf16[8,30208]{1,0:T(8,128)(2,1)S(1)}, u32[]{:S(2)}, u32[]{:S(2)}) collective-permute-start(bf16[8,30208]{1,0:T(8,128)(2,1)S(1)} %get-tuple-element.84), channel_id=1, source_target_pairs={{0,2},{2,0},{4,6},{6,4},{8,10},{10,8},{12,14},{14,12},{16,18},{18,... | collective-permute-start | bytes 1449992 | tf_op jit(solution)/shard_map/send_31/ppermute | solution.py:384
  112.2 10.9 %collective-permute-start.31 = (bf16[8,30208]{1,0:T(8,128)(2,1)S(1)}, bf16[8,30208]{1,0:T(8,128)(2,1)S(1)}, u32[]{:S(2)}, u32[]{:S(2)}) collective-permute-start(bf16[8,30208]{1,0:T(8,128)(2,1)S(1)} %add_convert_fusion.1), channel_id=1, source_target_pairs={{0,24},{2,26},{4,28},{6,30},{8,0},{10,2},{12,4},{14,6},{16,8},{18,... | collective-permute-start | bytes 1449992 | tf_op jit(solution)/shard_map/send_32/ppermute | solution.py:384
  121.6 9.4 %collective-permute-start.27 = (bf16[8,30208]{1,0:T(8,128)(2,1)S(1)}, bf16[8,30208]{1,0:T(8,128)(2,1)S(1)}, u32[]{:S(2)}, u32[]{:S(2)}) collective-permute-start(bf16[8,30208]{1,0:T(8,128)(2,1)S(1)} %add_convert_fusion.5), channel_id=1, source_target_pairs={{0,4},{2,6},{4,0},{6,2},{8,12},{10,14},{12,8},{14,10},{16,20},{18,... | collective-permute-start | bytes 1449992 | tf_op jit(solution)/shard_map/send_33/ppermute | solution.py:384
  122.0 9.2 %collective-permute-start.30 = (bf16[8,30208]{1,0:T(8,128)(2,1)S(1)}, bf16[8,30208]{1,0:T(8,128)(2,1)S(1)}, u32[]{:S(2)}, u32[]{:S(2)}) collective-permute-start(bf16[8,30208]{1,0:T(8,128)(2,1)S(1)} %add_convert_fusion.3), channel_id=1, source_target_pairs={{0,2},{2,0},{4,6},{6,4},{8,10},{10,8},{12,14},{14,12},{16,18},{18,... | collective-permute-start | bytes 1449992 | tf_op jit(solution)/shard_map/send_34/ppermute | solution.py:384
  123.3 9.5 %collective-permute-start.32 = (bf16[8,30208]{1,0:T(8,128)(2,1)S(1)}, bf16[8,30208]{1,0:T(8,128)(2,1)S(1)}, u32[]{:S(2)}, u32[]{:S(2)}) collective-permute-start(bf16[8,30208]{1,0:T(8,128)(2,1)S(1)} %add_convert_fusion), channel_id=1, source_target_pairs={{0,24},{2,26},{4,28},{6,30},{8,0},{10,2},{12,4},{14,6},{16,8},{18,... | collective-permute-start | bytes 1449992 | tf_op jit(solution)/shard_map/send_35/ppermute | solution.py:384
  134.7 1.2 collective-permute-start.33

commit v4 on v3

v4 whole, which is shorter than its diff:
```python
import functools

import jax
import jax.numpy as jnp
from jax import lax
from jax.experimental import pallas as pl
from jax.experimental.pallas import tpu as pltpu
from jax.sharding import PartitionSpec as P

SMOOTH = 0.25
Z, Y, X = 0, 1, 2
GATHER, REDUCE, FLOWS, GRADS = 0, 1, 2, 3


def chip_box(count):
    bits = (count // 2).bit_length() - 1
    nx = 1 << (bits // 2)
    return count // (2 * nx), 2, nx


PLAN = [
    (GATHER, Z, -1, (-1, 0, 0), ()),
    (GATHER, X, 1, (0, 0, 1), ()),
    (GATHER, Y, 1, (0, 1, 0), ()),
    (GATHER, Z, -1, (2, 0, 0), (0,)),
    (GATHER, X, 1, (-1, 0, 1), (1,)),
    (GATHER, Y, 1, (0, 1, 1), (2,)),
    (GATHER, Z, 1, (1, 1, 0), (3,)),
    (GATHER, X, 1, (2, 0, 1), (4,)),
    (GATHER, Y, 1, (-1, 1, 1), (5,)),
    (FLOWS, 0, [(0, 0, 0), (-1, 0, 0), (0, 0, 1), (0, 1, 0), (2, 0, 0), (-1, 0, 1), (0, 1, 1), (1, 1, 0), (2, 0, 1), (-1, 1, 1)], ()),
    (GRADS, 0),
    (GATHER, Z, 1, (1, 0, 0), (6,)),
    (GATHER, X, 1, (1, 1, 1), (7,)),
    (GATHER, Y, 1, (2, 1, 1), (8,)),
    (GATHER, Z, 1, (2, 1, 0), (9, 11)),
    (GATHER, X, 1, (1, 0, 1), (9, 12)),
    (GATHER, Y, 1, (-1, 1, 0), (9, 13)),
    (FLOWS, 1, [(1, 0, 0), (1, 1, 1), (2, 1, 1), (2, 1, 0), (1, 0, 1), (-1, 1, 0)], ()),
    (GRADS, 1),
    (REDUCE, Y, 1, (0, 1, 1), (16,)),
    (REDUCE, X, 1, (-1, 1, 1), (15,)),
    (REDUCE, Z, -1, (-1, 0, 1), (14,)),
    (REDUCE, Y, 1, (2, 1, 1), (17, 19)),
    (REDUCE, X, 1, (1, 1, 1), (17, 20)),
    (REDUCE, Z, -1, (-1, 0, 0), (17, 21)),
    (REDUCE, Y, 1, (2, 1, 0), (22,)),
    (REDUCE, X, 1, (2, 0, 1), (23,)),
    (REDUCE, Z, -1, (-1, 1, 0), (24,)),
    (REDUCE, Y, 1, (1, 1, 0), (25,)),
    (REDUCE, X, 1, (1, 0, 1), (26,)),
    (REDUCE, Z, 1, (2, 0, 0), (27,)),
    (REDUCE, Y, 1, (0, 1, 0), (28,)),
    (REDUCE, X, 1, (0, 0, 1), (29,)),
    (REDUCE, Z, 1, (1, 0, 0), (30,)),
]


def greedy(box):
    labels = [(z, y, x) for z in range(box[0]) for y in range(box[1]) for x in range(box[2])]
    have, sends = {(0, 0, 0)}, []
    while len(have) < len(labels):
        taken = set()
        for axis in (Z, X, Y):
            shifts = (1, -1) if box[axis] > 2 else (1,)
            options = [
                (shift, label)
                for label in labels
                if label not in have and label not in taken
                for shift in shifts
                if step_back(label, axis, shift, box) in have
            ]
            if options:
                shift, label = options[0]
                sends.append((axis, shift, label))
                taken.add(label)
        have |= taken
    return sends


def step_back(label, axis, shift, box):
    moved = list(label)
    moved[axis] = (moved[axis] - shift) % box[axis]
    return tuple(moved)


def plan(box):
    if box == (4, 2, 2):
        wrap = lambda label: tuple(c % n for c, n in zip(label, box))
        steps = []
        for step in PLAN:
            if step[0] in (GATHER, REDUCE):
                step = (*step[:3], wrap(step[3]), step[4])
            elif step[0] == FLOWS:
                step = (*step[:2], [wrap(label) for label in step[2]], step[3])
            steps.append(step)
        return steps
    sends = greedy(box)
    steps = [(GATHER, *send, ()) for send in sends]
    steps += [(FLOWS, 0, [(0, 0, 0)] + [label for _, _, label in sends], ()), (GRADS, 0)]
    return steps + [(REDUCE, *send, ()) for send in reversed(sends)]


def moves(axis, shift, box):
    pairs = []
    for z in range(box[0]):
        for y in range(box[1]):
            for x in range(box[2]):
                to = step_back((z, y, x), axis, -shift, box)
                pairs.append(((z * box[1] + y) * box[2] + x, (to[0] * box[1] + to[1]) * box[2] + to[2]))
    return pairs


def after(value, earlier):
    if not earlier:
        return value
    return lax.optimization_barrier((value, *earlier))[0]


def tile_of(width, group):
    groups = width // group
    return group * max(n for n in range(1, 65) if groups % n == 0)


GROUP = 256


def scatter_lanes(column):
    lane = lax.broadcasted_iota(jnp.int32, (GROUP, column.shape[1]), 0)
    return jnp.where(lane == column % GROUP, 1.0, 0.0).astype(jnp.bfloat16)


def split_high(value):
    high = value.astype(jnp.bfloat16)
    return high, (value - high.astype(jnp.float32)).astype(jnp.bfloat16)


def place_of(bus_ref, column, groups):
    tile = bus_ref[0] * pl.num_programs(0) + pl.program_id(0)
    return column // GROUP - tile * groups


def inject_kernel(bus_ref, release_ref, efficiency_ref, plant_ref, net_ref, out_ref):
    rows, width = net_ref.shape
    groups = width // GROUP
    column = plant_ref[...]
    lanes = scatter_lanes(column)
    place = place_of(bus_ref, column, groups)

    def spread(values):
        picked = [jnp.where(place == group, values, 0.0) for group in range(groups)]
        return lax.dot_general(
            jnp.concatenate(picked, axis=0).astype(jnp.bfloat16),
            lanes,
            (((1,), (1,)), ((), ())),
            preferred_element_type=jnp.float32,
        )

    high, low = split_high(release_ref[...] * efficiency_ref[...])
    added = spread(high.astype(jnp.float32)) + spread(low.astype(jnp.float32))
    for group in range(groups):
        at = slice(group * GROUP, (group + 1) * GROUP)
        total = net_ref[:, at].astype(jnp.float32) + added[group * rows : (group + 1) * rows]
        out_ref[:, at] = total.astype(jnp.bfloat16)


FREE = pl.CostEstimate(flops=0, bytes_accessed=0, transcendentals=0)


def vmem(mebibytes):
    return pltpu.CompilerParams(vmem_limit_bytes=mebibytes << 20)


def inject_of(bus, net_load, release, efficiency, plant_bus):
    rows, width = net_load.shape
    short = -rows % 8
    if short:
        net_load = jnp.pad(net_load, ((0, short), (0, 0)))
        release = jnp.pad(release, ((0, short), (0, 0)))
    tile = tile_of(width, GROUP)
    plants = release.shape[1]
    whole = pl.BlockSpec((1, plants), lambda i: (0, 0))
    tiled = pl.BlockSpec((rows + short, tile), lambda i: (0, i))
    out = pl.pallas_call(
        inject_kernel,
        grid=(width // tile,),
        in_specs=[
            pl.BlockSpec(memory_space=pltpu.SMEM),
            pl.BlockSpec((rows + short, plants), lambda i: (0, 0)),
            whole,
            whole,
            tiled,
        ],
        out_specs=tiled,
        out_shape=jax.ShapeDtypeStruct(net_load.shape, jnp.bfloat16),
        compiler_params=vmem(60),
        cost_estimate=FREE,
        name="inject",
    )(bus, release, efficiency[None, :], plant_bus[None, :], net_load)
    return out[:rows] if short else out


RESIDENT = pl.BlockSpec(memory_space=pltpu.VMEM)


def flows_kernel(tile, *refs):
    *blocks, ptdf_ref, out_ref = refs
    total = jnp.zeros(out_ref.shape, jnp.float32)

    def add(i, total):
        at = pl.ds(pl.multiple_of(i * tile, 128), tile)
        rows = jnp.concatenate([block[:, at].astype(jnp.float32) for block in blocks], axis=0)
        return total + lax.dot_general(
            rows.astype(jnp.bfloat16), ptdf_ref[:, at], (((1,), (1,)), ((), ())), preferred_element_type=jnp.float32
        )

    out_ref[...] = lax.fori_loop(0, ptdf_ref.shape[1] // tile, add, total)


def flows_of(blocks, ptdf):
    rows = blocks[0].shape[0]
    branches, width = ptdf.shape
    if rows % 8:
        short = -rows * len(blocks) % 8
        blocks = [jnp.pad(jnp.concatenate(blocks, axis=0), ((0, short), (0, 0)))]
        rows = blocks[0].shape[0]
    count = len(blocks)
    return pl.pallas_call(
        functools.partial(flows_kernel, tile_of(width, 128)),
        in_specs=[RESIDENT] * (count + 1),
        out_specs=RESIDENT,
        out_shape=jax.ShapeDtypeStruct((count * rows, branches), jnp.float32),
        compiler_params=vmem(16),
        cost_estimate=FREE,
        name="flows",
    )(*blocks, ptdf)


def grad_flow_of(flows, limit, price):
    upper = jax.nn.sigmoid((flows - limit) / SMOOTH)
    lower = jax.nn.sigmoid((-flows - limit) / SMOOTH)
    return (price * (upper - lower)).astype(jnp.bfloat16)


def grads_kernel(tile, mine_ref, other_ref, limit_ref, price_ref, ptdf_ref, *out_refs):
    rows = out_refs[0].shape[0]
    grad_flow = grad_flow_of(mine_ref[...] + other_ref[...], limit_ref[...], price_ref[...])

    @pl.loop(0, ptdf_ref.shape[1] // tile)
    def _(i):
        at = pl.ds(pl.multiple_of(i * tile, 128), tile)
        grads = jnp.dot(grad_flow, ptdf_ref[:, at], preferred_element_type=jnp.float32)
        for index, out_ref in enumerate(out_refs):
            out_ref[:, at] = grads[index * rows : (index + 1) * rows].astype(out_ref.dtype)


def grads_of(mine, other, limit, price, ptdf, rows, types):
    width = ptdf.shape[1]
    if rows % 8:
        grads = jnp.dot(grad_flow_of(mine + other, limit, price), ptdf, preferred_element_type=jnp.float32)
        return [grads[i * rows : (i + 1) * rows] for i in range(len(types))]
    return pl.pallas_call(
        functools.partial(grads_kernel, tile_of(width, 128)),
        in_specs=[RESIDENT] * 5,
        out_specs=[RESIDENT] * len(types),
        out_shape=[jax.ShapeDtypeStruct((rows, width), dtype) for dtype in types],
        compiler_params=vmem(16),
        cost_estimate=FREE,
        name="grads",
    )(mine, other, limit, price, ptdf)


def finish_kernel(bus_ref, plant_ref, *refs):
    *terms, grad_ref, found_ref = refs
    rows, width = grad_ref.shape
    groups = width // GROUP
    column = plant_ref[...]
    lanes = scatter_lanes(column)
    grad = sum(term[...].astype(jnp.float32) for term in terms)
    grad_ref[...] = grad
    place = place_of(bus_ref, column, groups)
    high, low = split_high(jnp.concatenate([grad[:, g * GROUP : (g + 1) * GROUP] for g in range(groups)], axis=0))
    found = jnp.dot(
        jnp.concatenate([high, low], axis=1),
        jnp.concatenate([lanes, lanes], axis=0),
        preferred_element_type=jnp.float32,
    )
    picked = jnp.zeros(found_ref.shape, jnp.float32)
    for group in range(groups):
        picked += jnp.where(place == group, found[group * rows : (group + 1) * rows], 0.0)
    found_ref[...] = picked


def finish_of(bus, plant_bus, terms):
    rows, width = terms[0].shape
    short = -rows % 8
    if short:
        terms = [jnp.pad(term, ((0, short), (0, 0))) for term in terms]
    plants = plant_bus.shape[0]
    whole = pl.BlockSpec((rows + short, width), lambda i: (0, 0))
    grad, found = pl.pallas_call(
        finish_kernel,
        grid=(1,),
        in_specs=[pl.BlockSpec(memory_space=pltpu.SMEM), pl.BlockSpec((1, plants), lambda i: (0, 0))]
        + [whole] * len(terms),
        out_specs=[whole, pl.BlockSpec((rows + short, plants), lambda i: (0, 0))],
        out_shape=[
            jax.ShapeDtypeStruct((rows + short, width), jnp.float32),
            jax.ShapeDtypeStruct((rows + short, plants), jnp.float32),
        ],
        compiler_params=vmem(48),
        cost_estimate=FREE,
        name="finish",
    )(bus, plant_bus[None, :], *terms)
    return (grad[:rows], found[:rows]) if short else (grad, found)


def total_of(terms):
    return sum(term.astype(jnp.float32) for term in terms).astype(jnp.bfloat16)


def make_shards(box, buses):
    steps = plan(box)
    targets = {step_back(step[3], step[1], step[2], box) for step in steps if step[0] == REDUCE}
    own = (0, 0, 0)

    def shards(net_load, release, plant_bus, efficiency, ptdf, branch_class, class_limit, class_price):
        rows = net_load.shape[0]
        bus = lax.axis_index("bus").astype(jnp.int32)[None]
        inject = inject_of(bus, net_load, release, efficiency, plant_bus)
        onehot = (branch_class[:, None] == jnp.arange(class_limit.shape[0])[None, :]).astype(jnp.float32)
        limit = jnp.sum(onehot * class_limit[None, :], axis=1)[None, :]
        price = jnp.sum(onehot * class_price[None, :], axis=1)[None, :]

        def over_bus(value):
            if buses == 2:
                return value, lax.ppermute(value, "bus", [(0, 1), (1, 0)])
            return lax.psum(value, "bus"), jnp.zeros_like(value)

        have, terms, flows, over = {own: inject}, {}, {}, []
        for step in steps:
            if step[0] == FLOWS:
                _, batch, labels, waits = step
                blocks = [have[label] for label in labels]
                blocks[-1] = after(blocks[-1], [over[i] for i in waits])
                flows[batch] = labels, over_bus(flows_of(blocks, ptdf))
                over.append(flows[batch][1][0])
            elif step[0] == GRADS:
                labels, sides = flows[step[1]]
                types = [jnp.float32 if label in targets else jnp.bfloat16 for label in labels]
                parts = grads_of(*sides, limit, price, ptdf, rows, types)
                terms.update((label, [part]) for label, part in zip(labels, parts))
                over.append(parts[0])
            else:
                kind, axis, shift, label, waits = step
                near = step_back(label, axis, shift, box)
                block = have[near] if kind == GATHER else total_of(terms[label])
                waits = [over[i] for i in waits]
                pairs = moves(axis, shift if kind == GATHER else -shift, box)
                with jax.named_scope(f"send_{len(over)}"):
                    came = lax.ppermute(after(block, waits), "br", pairs)
                if kind == GATHER:
                    have[label] = came
                else:
                    terms[near].append(came)
                over.append(came)
        grad_bus, found = finish_of(bus, plant_bus, terms[own])
        mine, other = over_bus(found)
        grad_release = (mine + other) * efficiency[None, :]
        return (grad_bus, grad_release)

    return shards


def solution(mesh):
    placed = (P("br", "bus"), P("br", None), P(), P(), P("br", "bus"), P("br"), P(), P())
    return jax.shard_map(
        make_shards(chip_box(mesh.shape["br"]), mesh.shape["bus"]),
        mesh=mesh,
        in_specs=placed,
        out_specs=(P("br", "bus"), P("br", None)),
        check_vma=False,
    )
```

time: 137 us -> 134 us (0.978)
  Pallas kernels: 24.4 us -> 14.4 us
  waiting for transfers between devices: 65.3 us -> 71.2 us
    pallas_call x8 -> x6, Pallas kernels: 24.4 us -> 14.4 us  [the longest x2 6.36 us: flows_of(): pl.pallas_call(functools.partial(flows_kernel, tile_of(width, 128)), in_s...]
    ppermute x30, waiting for transfers between devices: 63 us -> 67.7 us  [shards(): came = lax.ppermute(after(block, waits), 'br', pairs)]
    ppermute x30, starting transfers between devices: 39.6 us -> 41 us  [shards(): came = lax.ppermute(after(block, waits), 'br', pairs)]
    ppermute x4 -> x3, waiting for transfers between devices: 2.32 us -> 3.49 us  [over_bus(): return (value, lax.ppermute(value, 'bus', [(0, 1), (1, 0)]))]
  transfers between devices with their start and end apart: 34 -> 33, of which waited for: 18 -> 18; matrix products, arithmetic and copies ran while one was open for 1% -> 1% of each run, Pallas kernels for 13% -> 7%
where the time goes in v4:
time: 134 us; the launch traced here: 133 us
  waiting for transfers between devices  71.2 us (53%)
  starting transfers between devices  41.2 us (31%)
  Pallas kernels  14.4 us (11%)
  local copies, waits for them, and re-layouts  4.25 us (3%)
  other arithmetic  1.61 us (1%)
    ppermute x30, waiting for transfers between devices, shards(): came = lax.ppermute(after(block, waits), 'br', pairs)  67.7 us
    ppermute x30, starting transfers between devices, shards(): came = lax.ppermute(after(block, waits), 'br', pairs)  41 us
    pallas_call x2, Pallas kernels, flows_of(): pl.pallas_call(functools.partial(flows_kernel, tile_of(width, 128)), in_s...  6.36 us
    unnamed x16, local copies, waits for them, and re-layouts  4.25 us
    pallas_call x2, Pallas kernels, grads_of(): pl.pallas_call(functools.partial(grads_kernel, tile_of(width, 128)), in_s...  3.55 us
    ppermute x3, waiting for transfers between devices, over_bus(): return (value, lax.ppermute(value, 'bus', [(0, 1), (1, 0)]))  3.49 us
    pallas_call x1, Pallas kernels, inject_of(): pl.pallas_call(inject_kernel, grid=(width // tile,), in_specs=[pl.BlockSp...  3.14 us
  transfers between devices with their start and end apart: 33, of which 18 were waited for; matrix products, arithmetic and copies ran while one was open for 1% of the time, Pallas kernels for 7%

profile of v4, /device:TPU:0, one launch (start us, length us, event | category | flops | bytes accessed | tf_op | source)
XLA Modules:
  0.0 133.5 jit_solution(14700582019361325243)
XLA Ops:
  0.7 3.1 %inject.1.refs_0_ = bf16[8,30208]{1,0:T(8,128)(2,1)} custom-call(s32[1]{0:T(128)} %bitcast.bus_ref, f32[8,1024]{1,0:T(8,128)} %release_ref.1, f32[1,1024]{1,0:T(1,128)} %bitcast.11, s32[1,1024]{1,0:T(1,128)} %bitcast.5, bf16[8,30208]{1,0:T(8,128)(2,1)} %net_ref.1), custom_call_target="tpu_custom_call" | custom-call | tf_op jit(solution)/shard_map/inject/pallas_call | solution.py:184
  3.8 5.0 %collective-permute-start = (bf16[8,30208]{1,0:T(8,128)(2,1)}, bf16[8,30208]{1,0:T(8,128)(2,1)S(1)}, u32[]{:S(2)}, u32[]{:S(2)}) collective-permute-start(bf16[8,30208]{1,0:T(8,128)(2,1)} %inject.1.refs_0_), channel_id=1, source_target_pairs={{0,24},{2,26},{4,28},{6,30},{8,0},{10,2},{12,4},{14,6},{16,8},{18,... | collective-permute-start | bytes 1449992 | tf_op jit(solution)/shard_map/send_0/ppermute | solution.py:361
  8.9 1.5 %collective-permute-start.1 = (bf16[8,30208]{1,0:T(8,128)(2,1)}, bf16[8,30208]{1,0:T(8,128)(2,1)S(1)}, u32[]{:S(2)}, u32[]{:S(2)}) collective-permute-start(bf16[8,30208]{1,0:T(8,128)(2,1)} %inject.1.refs_0_), channel_id=1, source_target_pairs={{0,2},{2,0},{4,6},{6,4},{8,10},{10,8},{12,14},{14,12},{16,18},{18,... | collective-permute-start | bytes 1449992 | tf_op jit(solution)/shard_map/send_1/ppermute | solution.py:361
  10.3 1.5 %collective-permute-start.2 = (bf16[8,30208]{1,0:T(8,128)(2,1)}, bf16[8,30208]{1,0:T(8,128)(2,1)S(1)}, u32[]{:S(2)}, u32[]{:S(2)}) collective-permute-start(bf16[8,30208]{1,0:T(8,128)(2,1)} %inject.1.refs_0_), channel_id=1, source_target_pairs={{0,4},{2,6},{4,0},{6,2},{8,12},{10,14},{12,8},{14,10},{16,20},{18,... | collective-permute-start | bytes 1449992 | tf_op jit(solution)/shard_map/send_2/ppermute | solution.py:361
  11.9 7.6 %collective-permute-done.refs_1_ = bf16[8,30208]{1,0:T(8,128)(2,1)S(1)} collective-permute-done((bf16[8,30208]{1,0:T(8,128)(2,1)}, bf16[8,30208]{1,0:T(8,128)(2,1)S(1)}, u32[]{:S(2)}, u32[]{:S(2)}) %collective-permute-start) | collective-permute-done | bytes 483360 | tf_op jit(solution)/shard_map/send_0/ppermute | solution.py:361
  19.5 4.2 %collective-permute-start.3 = (bf16[8,30208]{1,0:T(8,128)(2,1)S(1)}, bf16[8,30208]{1,0:T(8,128)(2,1)S(1)}, u32[]{:S(2)}, u32[]{:S(2)}) collective-permute-start(bf16[8,30208]{1,0:T(8,128)(2,1)S(1)} %collective-permute-done.refs_1_), channel_id=1, source_target_pairs={{0,24},{2,26},{4,28},{6,30},{8,0},{10,2},{12,4},{14,6},{16,8},{18,... | collective-permute-start | bytes 1449992 | tf_op jit(solution)/shard_map/send_3/ppermute | solution.py:361
  23.7 1.5 %collective-permute-start.4 = (bf16[8,30208]{1,0:T(8,128)(2,1)S(1)}, bf16[8,30208]{1,0:T(8,128)(2,1)S(1)}, u32[]{:S(2)}, u32[]{:S(2)}) collective-permute-start(bf16[8,30208]{1,0:T(8,128)(2,1)S(1)} %collective-permute-done.refs_1_), channel_id=1, source_target_pairs={{0,2},{2,0},{4,6},{6,4},{8,10},{10,8},{12,14},{14,12},{16,18},{18,... | collective-permute-start | bytes 1449992 | tf_op jit(solution)/shard_map/send_4/ppermute | solution.py:361
  25.2 1.5 %collective-permute-start.5 = (bf16[8,30208]{1,0:T(8,128)(2,1)S(1)}, bf16[8,30208]{1,0:T(8,128)(2,1)S(1)}, u32[]{:S(2)}, u32[]{:S(2)}) collective-permute-start(bf16[8,30208]{1,0:T(8,128)(2,1)S(1)} %collective-permute-done.1.refs_2_), channel_id=1, source_target_pairs={{0,4},{2,6},{4,0},{6,2},{8,12},{10,14},{12,8},{14,10},{16,20},{18,... | collective-permute-start | bytes 1449992 | tf_op jit(solution)/shard_map/send_5/ppermute | solution.py:361
  26.7 7.9 %collective-permute-done.3.refs_4_ = bf16[8,30208]{1,0:T(8,128)(2,1)S(1)} collective-permute-done((bf16[8,30208]{1,0:T(8,128)(2,1)S(1)}, bf16[8,30208]{1,0:T(8,128)(2,1)S(1)}, u32[]{:S(2)}, u32[]{:S(2)}) %collective-permute-start.3) | collective-permute-done | bytes 483360 | tf_op jit(solution)/shard_map/send_3/ppermute | solution.py:361
  34.6 0.7 collective-permute-done.4.refs_5_
  35.3 1.5 %collective-permute-start.7 = (bf16[8,30208]{1,0:T(8,128)(2,1)S(1)}, bf16[8,30208]{1,0:T(8,128)(2,1)S(1)}, u32[]{:S(2)}, u32[]{:S(2)}) collective-permute-start(bf16[8,30208]{1,0:T(8,128)(2,1)S(1)} %collective-permute-done.3.refs_4_), channel_id=1, source_target_pairs={{0,2},{2,0},{4,6},{6,4},{8,10},{10,8},{12,14},{14,12},{16,18},{18,... | collective-permute-start | bytes 1449992 | tf_op jit(solution)/shard_map/send_7/ppermute | solution.py:361
  36.8 1.5 %collective-permute-start.8 = (bf16[8,30208]{1,0:T(8,128)(2,1)S(1)}, bf16[8,30208]{1,0:T(8,128)(2,1)S(1)}, u32[]{:S(2)}, u32[]{:S(2)}) collective-permute-start(bf16[8,30208]{1,0:T(8,128)(2,1)S(1)} %collective-permute-done.4.refs_5_), channel_id=1, source_target_pairs={{0,4},{2,6},{4,0},{6,2},{8,12},{10,14},{12,8},{14,10},{16,20},{18,... | collective-permute-start | bytes 1449992 | tf_op jit(solution)/shard_map/send_8/ppermute | solution.py:361
  38.3 8.3 %collective-permute-done.6.refs_7_ = bf16[8,30208]{1,0:T(8,128)(2,1)S(1)} collective-permute-done((bf16[8,30208]{1,0:T(8,128)(2,1)S(1)}, bf16[8,30208]{1,0:T(8,128)(2,1)S(1)}, u32[]{:S(2)}, u32[]{:S(2)}) %collective-permute-start.6) | collective-permute-done | bytes 483360 | tf_op jit(solution)/shard_map/send_6/ppermute | solution.py:361
  46.6 1.5 %collective-permute-start.11 = (bf16[8,30208]{1,0:T(8,128)(2,1)S(1)}, bf16[8,30208]{1,0:T(8,128)(2,1)S(1)}, u32[]{:S(2)}, u32[]{:S(2)}) collective-permute-start(bf16[8,30208]{1,0:T(8,128)(2,1)S(1)} %collective-permute-done.6.refs_7_), channel_id=1, source_target_pairs={{0,2},{2,0},{4,6},{6,4},{8,10},{10,8},{12,14},{14,12},{16,18},{18,... | collective-permute-start | bytes 1449992 | tf_op jit(solution)/shard_map/send_12/ppermute | solution.py:361
  48.1 1.5 %collective-permute-start.12 = (bf16[8,30208]{1,0:T(8,128)(2,1)S(1)}, bf16[8,30208]{1,0:T(8,128)(2,1)S(1)}, u32[]{:S(2)}, u32[]{:S(2)}) collective-permute-start(bf16[8,30208]{1,0:T(8,128)(2,1)S(1)} %collective-permute-done.7.refs_8_), channel_id=1, source_target_pairs={{0,4},{2,6},{4,0},{6,2},{8,12},{10,14},{12,8},{14,10},{16,20},{18,... | collective-permute-start | bytes 1449992 | tf_op jit(solution)/shard_map/send_13/ppermute | solution.py:361
  49.6 3.2 %copy-done = bf16[128,30208]{1,0:T(8,128)(2,1)S(1)} copy-done((bf16[128,30208]{1,0:T(8,128)(2,1)S(1)}, bf16[128,30208]{1,0:T(8,128)(2,1)}, u32[]{:S(2)}) %copy-start) | copy-done | bytes 7733272
  52.8 1.0 copy-done.2
  53.9 3.2 %flows.2.mine_ref = f32[80,128]{1,0:T(8,128)S(1)} custom-call(bf16[8,30208]{1,0:T(8,128)(2,1)S(1)} %copy-done.2, bf16[8,30208]{1,0:T(8,128)(2,1)S(1)} %collective-permute-done.refs_1_, bf16[8,30208]{1,0:T(8,128)(2,1)S(1)} %collective-permute-done.1.refs_2_, bf16[8,30208]{1,0:T(8,128)(2,1)S(1)} %collective-permute-done.2.refs_3_, ...), custom_call_target="tpu_custom_call" | custom-call | tf_op jit(solution)/shard_map/flows/pallas_call | solution.py:228
  57.1 0.4 collective-permute-done.10.refs_0_
  57.5 1.0 collective-permute-start.13
  58.5 1.0 collective-permute-start.14
  59.5 1.6 %collective-permute-start.15 = (bf16[8,30208]{1,0:T(8,128)(2,1)S(1)}, bf16[8,30208]{1,0:T(8,128)(2,1)S(1)}, u32[]{:S(2)}, u32[]{:S(2)}) collective-permute-start(bf16[8,30208]{1,0:T(8,128)(2,1)S(1)} %collective-permute-done.refs_1_), channel_id=1, source_target_pairs={{0,4},{2,6},{4,0},{6,2},{8,12},{10,14},{12,8},{14,10},{16,20},{18,... | collective-permute-start | bytes 1449992 | tf_op jit(solution)/shard_map/send_16/ppermute | solution.py:361
  61.1 0.1 select_reduce_fusion
  61.2 1.1 collective-permute-done.9.other_ref
  62.3 1.9 %grads.2 = (f32[8,30208]{1,0:T(8,128)S(1)}, bf16[8,30208]{1,0:T(8,128)(2,1)S(1)}, f32[8,30208]{1,0:T(8,128)S(1)}, f32[8,30208]{1,0:T(8,128)S(1)}, f32[8,30208]{1...) custom-call(f32[80,128]{1,0:T(8,128)S(1)} %flows.2.mine_ref, ...), custom_call_target="tpu_custom_call" | custom-call | tf_op jit(solution)/shard_map/grads/pallas_call | solution.py:262
  64.2 4.0 %collective-permute-done.13.refs_3_ = bf16[8,30208]{1,0:T(8,128)(2,1)S(1)} collective-permute-done((bf16[8,30208]{1,0:T(8,128)(2,1)S(1)}, bf16[8,30208]{1,0:T(8,128)(2,1)S(1)}, u32[]{:S(2)}, u32[]{:S(2)}) %collective-permute-start.13) | collective-permute-done | bytes 483360 | tf_op jit(solution)/shard_map/send_14/ppermute | solution.py:361
  68.2 1.1 collective-permute-start.16
  69.3 1.0 collective-permute-start.19
  70.4 2.5 %collective-permute-start.22 = (bf16[8,30208]{1,0:T(8,128)(2,1)S(1)}, bf16[8,30208]{1,0:T(8,128)(2,1)S(1)}, u32[]{:S(2)}, u32[]{:S(2)}) collective-permute-start(bf16[8,30208]{1,0:T(8,128)(2,1)S(1)} %get-tuple-element.75), channel_id=1, source_target_pairs={{0,4},{2,6},{4,0},{6,2},{8,12},{10,14},{12,8},{14,10},{16,20},{18,... | collective-permute-start | bytes 1449992 | tf_op jit(solution)/shard_map/send_19/ppermute | solution.py:361
  72.8 3.1 %flows.3.mine_ref = f32[48,128]{1,0:T(8,128)S(1)} custom-call(bf16[8,30208]{1,0:T(8,128)(2,1)S(1)} %collective-permute-done.10.refs_0_, bf16[8,30208]{1,0:T(8,128)(2,1)S(1)} %collective-permute-done.11.refs_1_, bf16[8,30208]{1,0:T(8,128)(2,1)S(1)} %collective-permute-done.12.refs_2_, bf16[8,30208]{1,0:T(8,128)(2,1)S(1)} %collective-permute-done.13.refs_3_, ...), custom_call_target="tpu_custom_call" | custom-call | tf_op jit(solution)/shard_map/flows/pallas_call | solution.py:228
  76.0 0.1 collective-permute-start.18
  76.0 1.2 collective-permute-done.18.other_ref
  77.2 1.6 %grads.3 = (f32[8,30208]{1,0:T(8,128)S(1)}, bf16[8,30208]{1,0:T(8,128)(2,1)S(1)}, bf16[8,30208]{1,0:T(8,128)(2,1)S(1)}, bf16[8,30208]{1,0:T(8,128)(2,1)S(1)}, bf...) custom-call(f32[48,128]{1,0:T(8,128)S(1)} %flows.3.mine_ref, f32[48,128]{1,0:T(8,128)S(1)} %collective-permute-done.18.other_ref, ...), custom_call_target="tpu_custom_call" | custom-call | tf_op jit(solution)/shard_map/grads/pallas_call | solution.py:262
  78.9 0.6 collective-permute-done.16
  79.5 0.1 collective-permute-start.17
  79.6 1.3 %collective-permute-start.21 = (bf16[8,30208]{1,0:T(8,128)(2,1)S(1)}, bf16[8,30208]{1,0:T(8,128)(2,1)S(1)}, u32[]{:S(2)}, u32[]{:S(2)}) collective-permute-start(bf16[8,30208]{1,0:T(8,128)(2,1)S(1)} %get-tuple-element.71), channel_id=1, source_target_pairs={{0,2},{2,0},{4,6},{6,4},{8,10},{10,8},{12,14},{14,12},{16,18},{18,... | collective-permute-start | bytes 1449992 | tf_op jit(solution)/shard_map/send_23/ppermute | solution.py:361
  80.9 2.5 %collective-permute-start.23 = (bf16[8,30208]{1,0:T(8,128)(2,1)S(1)}, bf16[8,30208]{1,0:T(8,128)(2,1)S(1)}, u32[]{:S(2)}, u32[]{:S(2)}) collective-permute-start(bf16[8,30208]{1,0:T(8,128)(2,1)S(1)} %get-tuple-element.76), channel_id=1, source_target_pairs={{0,4},{2,6},{4,0},{6,2},{8,12},{10,14},{12,8},{14,10},{16,20},{18,... | collective-permute-start | bytes 1449992 | tf_op jit(solution)/shard_map/send_22/ppermute | solution.py:361
  83.4 0.1 add_convert_fusion.3
  83.5 0.0 copy-start.4
  83.5 0.1 add_convert_fusion.6
  83.6 10.5 %collective-permute-done.17.refs_1_ = bf16[8,30208]{1,0:T(8,128)(2,1)S(1)} collective-permute-done((bf16[8,30208]{1,0:T(8,128)(2,1)S(1)}, bf16[8,30208]{1,0:T(8,128)(2,1)S(1)}, u32[]{:S(2)}, u32[]{:S(2)}) %collective-permute-start.17) | collective-permute-done | bytes 483360 | tf_op jit(solution)/shard_map/send_24/ppermute | solution.py:361
  94.1 0.1 add_convert_fusion.2
  94.2 0.6 collective-permute-start.27
  94.8 0.1 add_convert_fusion.4
  94.9 11.2 %collective-permute-done.24 = bf16[8,30208]{1,0:T(8,128)(2,1)S(1)} collective-permute-done((bf16[8,30208]{1,0:T(8,128)(2,1)S(1)}, bf16[8,30208]{1,0:T(8,128)(2,1)S(1)}, u32[]{:S(2)}, u32[]{:S(2)}) %collective-permute-start.24) | collective-permute-done | bytes 483360 | tf_op jit(solution)/shard_map/send_25/ppermute | solution.py:361
  106.1 0.3 collective-permute-start.25
  106.4 0.2 collective-permute-start.28
  106.6 0.1 add_convert_fusion.1
  106.7 1.2 collective-permute-done.20
  107.9 2.4 %collective-permute-start.30 = (bf16[8,30208]{1,0:T(8,128)(2,1)S(1)}, bf16[8,30208]{1,0:T(8,128)(2,1)S(1)}, u32[]{:S(2)}, u32[]{:S(2)}) collective-permute-start(bf16[8,30208]{1,0:T(8,128)(2,1)S(1)} %add_convert_fusion.1), channel_id=1, source_target_pairs={{0,24},{2,26},{4,28},{6,30},{8,0},{10,2},{12,4},{14,6},{16,8},{18,... | collective-permute-start | bytes 1449992 | tf_op jit(solution)/shard_map/send_30/ppermute | solution.py:361
  110.3 0.1 add_convert_fusion.5
  110.4 6.9 %collective-permute-done.25 = bf16[8,30208]{1,0:T(8,128)(2,1)S(1)} collective-permute-done((bf16[8,30208]{1,0:T(8,128)(2,1)S(1)}, bf16[8,30208]{1,0:T(8,128)(2,1)S(1)}, u32[]{:S(2)}, u32[]{:S(2)}) %collective-permute-start.25) | collective-permute-done | bytes 483360 | tf_op jit(solution)/shard_map/send_28/ppermute | solution.py:361
  117.3 0.4 collective-permute-start.26
  117.7 0.0 collective-permute-start.29
  117.7 1.2 collective-permute-done.30
  118.9 0.2 add_convert_fusion
  119.2 3.8 %collective-permute-start.31 = (bf16[8,30208]{1,0:T(8,128)(2,1)S(1)}, bf16[8,30208]{1,0:T(8,128)(2,1)S(1)}, u32[]{:S(2)}, u32[]{:S(2)}) collective-permute-start(bf16[8,30208]{1,0:T(8,128)(2,1)S(1)} %add_convert_fusion), channel_id=1, source_target_pairs={{0,24},{2,26},{4,28},{6,30},{8,0},{10,2},{12,4},{14,6},{16,8},{18,... | collective-permute-start | bytes 1449992 | tf_op jit(solution)/shard_map/send_33/ppermute | solution.py:361
  123.0 4.5 %collective-permute-done.26.refs_2_ = bf16[8,30208]{1,0:T(8,128)(2,1)S(1)} collective-permute-done((bf16[8,30208]{1,0:T(8,128)(2,1)S(1)}, bf16[8,30208]{1,0:T(8,128)(2,1)S(1)}, u32[]{:S(2)}, u32[]{:S(2)}) %collective-permute-start.26) | collective-permute-done | bytes 483360 | tf_op jit(solution)/shard_map/send_31/ppermute | solution.py:361
  127.5 0.3 collective-permute-done.29.refs_3_
  127.8 2.3 %collective-permute-done.31.refs_4_ = bf16[8,30208]{1,0:T(8,128)(2,1)S(1)} collective-permute-done((bf16[8,30208]{1,0:T(8,128)(2,1)S(1)}, bf16[8,30208]{1,0:T(8,128)(2,1)S(1)}, u32[]{:S(2)}, u32[]{:S(2)}) %collective-permute-start.31) | collective-permute-done | bytes 483360 | tf_op jit(solution)/shard_map/send_33/ppermute | solution.py:361
  130.2 1.4 %finish.1 = (f32[8,30208]{1,0:T(8,128)}, f32[8,1024]{1,0:T(8,128)S(1)}) custom-call(s32[1]{0:T(128)} %bitcast.bus_ref, s32[1,1024]{1,0:T(1,128)S(1)} %bitcast.6, f32[8,30208]{1,0:T(8,128)S(1)} %get-tuple-element.53.refs_0_, bf16[8,30208]{1,0:T(8,128)(2,1)S(1)} %collective-permute-done.17.refs_1_, bf16[8,30208]{1,0:T(8,128)(2,1)S(1)} %collective-permute-done.26.refs_2_, ...), custom_call_target="tpu_custom_call" | custom-call | tf_op jit(solution)/shard_map/finish/pallas_call | solution.py:301
  131.6 0.1 collective-permute-start.32
  131.7 1.2 collective-permute-done.32
  132.9 0.6 add_multiply_fusion
  (33 shorter events, 0.1 us)
Async XLA Ops:
  0.6 60.4 %copy-start.5 = (f32[16]{0:T(128)S(1)}, f32[16]{0:T(128)}, u32[]{:S(2)}) copy-start(f32[16]{0:T(128)} %param.15) | copy-start | bytes 196
  0.6 60.4 %copy-start.6 = (s32[128]{0:T(128)S(1)}, s32[128]{0:T(128)}, u32[]{:S(2)}) copy-start(s32[128]{0:T(128)} %param.13) | copy-start | bytes 1540
  0.7 60.4 %copy-start.7 = (f32[16]{0:T(128)S(1)}, f32[16]{0:T(128)}, u32[]{:S(2)}) copy-start(f32[16]{0:T(128)} %param.14) | copy-start | bytes 196
  3.8 15.7 %collective-permute-start = (bf16[8,30208]{1,0:T(8,128)(2,1)}, bf16[8,30208]{1,0:T(8,128)(2,1)S(1)}, u32[]{:S(2)}, u32[]{:S(2)}) collective-permute-start(bf16[8,30208]{1,0:T(8,128)(2,1)} %inject.1.refs_0_), channel_id=1, source_target_pairs={{0,24},{2,26},{4,28},{6,30},{8,0},{10,2},{12,4},{14,6},{16,8},{18,... | collective-permute-start | bytes 1449992 | tf_op jit(solution)/shard_map/send_0/ppermute | solution.py:361
  8.9 14.8 %collective-permute-start.1 = (bf16[8,30208]{1,0:T(8,128)(2,1)}, bf16[8,30208]{1,0:T(8,128)(2,1)S(1)}, u32[]{:S(2)}, u32[]{:S(2)}) collective-permute-start(bf16[8,30208]{1,0:T(8,128)(2,1)} %inject.1.refs_0_), channel_id=1, source_target_pairs={{0,2},{2,0},{4,6},{6,4},{8,10},{10,8},{12,14},{14,12},{16,18},{18,... | collective-permute-start | bytes 1449992 | tf_op jit(solution)/shard_map/send_1/ppermute | solution.py:361
  10.3 14.8 %collective-permute-start.2 = (bf16[8,30208]{1,0:T(8,128)(2,1)}, bf16[8,30208]{1,0:T(8,128)(2,1)S(1)}, u32[]{:S(2)}, u32[]{:S(2)}) collective-permute-start(bf16[8,30208]{1,0:T(8,128)(2,1)} %inject.1.refs_0_), channel_id=1, source_target_pairs={{0,4},{2,6},{4,0},{6,2},{8,12},{10,14},{12,8},{14,10},{16,20},{18,... | collective-permute-start | bytes 1449992 | tf_op jit(solution)/shard_map/send_2/ppermute | solution.py:361
  19.5 15.1 %collective-permute-start.3 = (bf16[8,30208]{1,0:T(8,128)(2,1)S(1)}, bf16[8,30208]{1,0:T(8,128)(2,1)S(1)}, u32[]{:S(2)}, u32[]{:S(2)}) collective-permute-start(bf16[8,30208]{1,0:T(8,128)(2,1)S(1)} %collective-permute-done.refs_1_), channel_id=1, source_target_pairs={{0,24},{2,26},{4,28},{6,30},{8,0},{10,2},{12,4},{14,6},{16,8},{18,... | collective-permute-start | bytes 1449992 | tf_op jit(solution)/shard_map/send_3/ppermute | solution.py:361
  23.7 11.6 %collective-permute-start.4 = (bf16[8,30208]{1,0:T(8,128)(2,1)S(1)}, bf16[8,30208]{1,0:T(8,128)(2,1)S(1)}, u32[]{:S(2)}, u32[]{:S(2)}) collective-permute-start(bf16[8,30208]{1,0:T(8,128)(2,1)S(1)} %collective-permute-done.refs_1_), channel_id=1, source_target_pairs={{0,2},{2,0},{4,6},{6,4},{8,10},{10,8},{12,14},{14,12},{16,18},{18,... | collective-permute-start | bytes 1449992 | tf_op jit(solution)/shard_map/send_4/ppermute | solution.py:361
  25.2 11.6 %collective-permute-start.5 = (bf16[8,30208]{1,0:T(8,128)(2,1)S(1)}, bf16[8,30208]{1,0:T(8,128)(2,1)S(1)}, u32[]{:S(2)}, u32[]{:S(2)}) collective-permute-start(bf16[8,30208]{1,0:T(8,128)(2,1)S(1)} %collective-permute-done.1.refs_2_), channel_id=1, source_target_pairs={{0,4},{2,6},{4,0},{6,2},{8,12},{10,14},{12,8},{14,10},{16,20},{18,... | collective-permute-start | bytes 1449992 | tf_op jit(solution)/shard_map/send_5/ppermute | solution.py:361
  34.6 12.0 %collective-permute-start.6 = (bf16[8,30208]{1,0:T(8,128)(2,1)S(1)}, bf16[8,30208]{1,0:T(8,128)(2,1)S(1)}, u32[]{:S(2)}, u32[]{:S(2)}) collective-permute-start(bf16[8,30208]{1,0:T(8,128)(2,1)S(1)} %collective-permute-done.2.refs_3_), channel_id=1, source_target_pairs={{0,8},{2,10},{4,12},{6,14},{8,16},{10,18},{12,20},{14,22},{16,24},... | collective-permute-start | bytes 1449992 | tf_op jit(solution)/shard_map/send_6/ppermute | solution.py:361
  35.3 11.3 %collective-permute-start.7 = (bf16[8,30208]{1,0:T(8,128)(2,1)S(1)}, bf16[8,30208]{1,0:T(8,128)(2,1)S(1)}, u32[]{:S(2)}, u32[]{:S(2)}) collective-permute-start(bf16[8,30208]{1,0:T(8,128)(2,1)S(1)} %collective-permute-done.3.refs_4_), channel_id=1, source_target_pairs={{0,2},{2,0},{4,6},{6,4},{8,10},{10,8},{12,14},{14,12},{16,18},{18,... | collective-permute-start | bytes 1449992 | tf_op jit(solution)/shard_map/send_7/ppermute | solution.py:361
  36.8 11.3 %collective-permute-start.8 = (bf16[8,30208]{1,0:T(8,128)(2,1)S(1)}, bf16[8,30208]{1,0:T(8,128)(2,1)S(1)}, u32[]{:S(2)}, u32[]{:S(2)}) collective-permute-start(bf16[8,30208]{1,0:T(8,128)(2,1)S(1)} %collective-permute-done.4.refs_5_), channel_id=1, source_target_pairs={{0,4},{2,6},{4,0},{6,2},{8,12},{10,14},{12,8},{14,10},{16,20},{18,... | collective-permute-start | bytes 1449992 | tf_op jit(solution)/shard_map/send_8/ppermute | solution.py:361
  46.6 10.9 %collective-permute-start.10 = (bf16[8,30208]{1,0:T(8,128)(2,1)}, bf16[8,30208]{1,0:T(8,128)(2,1)S(1)}, u32[]{:S(2)}, u32[]{:S(2)}) collective-permute-start(bf16[8,30208]{1,0:T(8,128)(2,1)} %inject.1.refs_0_), channel_id=1, source_target_pairs={{0,8},{2,10},{4,12},{6,14},{8,16},{10,18},{12,20},{14,22},{16,24},... | collective-permute-start | bytes 1449992 | tf_op jit(solution)/shard_map/send_11/ppermute | solution.py:361
  46.6 11.8 %collective-permute-start.11 = (bf16[8,30208]{1,0:T(8,128)(2,1)S(1)}, bf16[8,30208]{1,0:T(8,128)(2,1)S(1)}, u32[]{:S(2)}, u32[]{:S(2)}) collective-permute-start(bf16[8,30208]{1,0:T(8,128)(2,1)S(1)} %collective-permute-done.6.refs_7_), channel_id=1, source_target_pairs={{0,2},{2,0},{4,6},{6,4},{8,10},{10,8},{12,14},{14,12},{16,18},{18,... | collective-permute-start | bytes 1449992 | tf_op jit(solution)/shard_map/send_12/ppermute | solution.py:361
  48.1 11.4 %collective-permute-start.12 = (bf16[8,30208]{1,0:T(8,128)(2,1)S(1)}, bf16[8,30208]{1,0:T(8,128)(2,1)S(1)}, u32[]{:S(2)}, u32[]{:S(2)}) collective-permute-start(bf16[8,30208]{1,0:T(8,128)(2,1)S(1)} %collective-permute-done.7.refs_8_), channel_id=1, source_target_pairs={{0,4},{2,6},{4,0},{6,2},{8,12},{10,14},{12,8},{14,10},{16,20},{18,... | collective-permute-start | bytes 1449992 | tf_op jit(solution)/shard_map/send_13/ppermute | solution.py:361
  49.6 3.2 %copy-start = (bf16[128,30208]{1,0:T(8,128)(2,1)S(1)}, bf16[128,30208]{1,0:T(8,128)(2,1)}, u32[]{:S(2)}) copy-start(bf16[128,30208]{1,0:T(8,128)(2,1)} %ptdf_ref.3) | copy-start | bytes 23199748
  52.8 1.0 copy-start.2
  53.9 8.4 %copy-start.1 = (bf16[128,30208]{1,0:T(8,128)(2,1)S(1)}, bf16[128,30208]{1,0:T(8,128)(2,1)}, u32[]{:S(2)}) copy-start(bf16[128,30208]{1,0:T(8,128)(2,1)} %ptdf_ref.3) | copy-start | bytes 23199748
  57.5 10.8 %collective-permute-start.13 = (bf16[8,30208]{1,0:T(8,128)(2,1)S(1)}, bf16[8,30208]{1,0:T(8,128)(2,1)S(1)}, u32[]{:S(2)}, u32[]{:S(2)}) collective-permute-start(bf16[8,30208]{1,0:T(8,128)(2,1)S(1)} %collective-permute-done.6.refs_7_), channel_id=1, source_target_pairs={{0,8},{2,10},{4,12},{6,14},{8,16},{10,18},{12,20},{14,22},{16,24},... | collective-permute-start | bytes 1449992 | tf_op jit(solution)/shard_map/send_14/ppermute | solution.py:361
  58.5 10.9 %collective-permute-start.14 = (bf16[8,30208]{1,0:T(8,128)(2,1)S(1)}, bf16[8,30208]{1,0:T(8,128)(2,1)S(1)}, u32[]{:S(2)}, u32[]{:S(2)}) collective-permute-start(bf16[8,30208]{1,0:T(8,128)(2,1)S(1)} %collective-permute-done.10.refs_0_), channel_id=1, source_target_pairs={{0,2},{2,0},{4,6},{6,4},{8,10},{10,8},{12,14},{14,12},{16,18},{18,... | collective-permute-start | bytes 1449992 | tf_op jit(solution)/shard_map/send_15/ppermute | solution.py:361
  59.5 10.9 %collective-permute-start.15 = (bf16[8,30208]{1,0:T(8,128)(2,1)S(1)}, bf16[8,30208]{1,0:T(8,128)(2,1)S(1)}, u32[]{:S(2)}, u32[]{:S(2)}) collective-permute-start(bf16[8,30208]{1,0:T(8,128)(2,1)S(1)} %collective-permute-done.refs_1_), channel_id=1, source_target_pairs={{0,4},{2,6},{4,0},{6,2},{8,12},{10,14},{12,8},{14,10},{16,20},{18,... | collective-permute-start | bytes 1449992 | tf_op jit(solution)/shard_map/send_16/ppermute | solution.py:361
  61.1 1.2 collective-permute-start.9
  68.2 11.2 %collective-permute-start.16 = (bf16[8,30208]{1,0:T(8,128)(2,1)S(1)}, bf16[8,30208]{1,0:T(8,128)(2,1)S(1)}, u32[]{:S(2)}, u32[]{:S(2)}) collective-permute-start(bf16[8,30208]{1,0:T(8,128)(2,1)S(1)} %get-tuple-element.62), channel_id=1, source_target_pairs={{0,8},{2,10},{4,12},{6,14},{8,16},{10,18},{12,20},{14,22},{16,24},... | collective-permute-start | bytes 1449992 | tf_op jit(solution)/shard_map/send_21/ppermute | solution.py:361
  69.3 10.2 %collective-permute-start.19 = (bf16[8,30208]{1,0:T(8,128)(2,1)S(1)}, bf16[8,30208]{1,0:T(8,128)(2,1)S(1)}, u32[]{:S(2)}, u32[]{:S(2)}) collective-permute-start(bf16[8,30208]{1,0:T(8,128)(2,1)S(1)} %get-tuple-element.67), channel_id=1, source_target_pairs={{0,2},{2,0},{4,6},{6,4},{8,10},{10,8},{12,14},{14,12},{16,18},{18,... | collective-permute-start | bytes 1449992 | tf_op jit(solution)/shard_map/send_20/ppermute | solution.py:361
  70.4 10.5 %collective-permute-start.22 = (bf16[8,30208]{1,0:T(8,128)(2,1)S(1)}, bf16[8,30208]{1,0:T(8,128)(2,1)S(1)}, u32[]{:S(2)}, u32[]{:S(2)}) collective-permute-start(bf16[8,30208]{1,0:T(8,128)(2,1)S(1)} %get-tuple-element.75), channel_id=1, source_target_pairs={{0,4},{2,6},{4,0},{6,2},{8,12},{10,14},{12,8},{14,10},{16,20},{18,... | collective-permute-start | bytes 1449992 | tf_op jit(solution)/shard_map/send_19/ppermute | solution.py:361
  76.0 1.3 collective-permute-start.18
  79.5 14.6 %collective-permute-start.17 = (bf16[8,30208]{1,0:T(8,128)(2,1)S(1)}, bf16[8,30208]{1,0:T(8,128)(2,1)S(1)}, u32[]{:S(2)}, u32[]{:S(2)}) collective-permute-start(bf16[8,30208]{1,0:T(8,128)(2,1)S(1)} %get-tuple-element.63), channel_id=1, source_target_pairs={{0,8},{2,10},{4,12},{6,14},{8,16},{10,18},{12,20},{14,22},{16,24},... | collective-permute-start | bytes 1449992 | tf_op jit(solution)/shard_map/send_24/ppermute | solution.py:361
  79.6 14.7 %collective-permute-start.21 = (bf16[8,30208]{1,0:T(8,128)(2,1)S(1)}, bf16[8,30208]{1,0:T(8,128)(2,1)S(1)}, u32[]{:S(2)}, u32[]{:S(2)}) collective-permute-start(bf16[8,30208]{1,0:T(8,128)(2,1)S(1)} %get-tuple-element.71), channel_id=1, source_target_pairs={{0,2},{2,0},{4,6},{6,4},{8,10},{10,8},{12,14},{14,12},{16,18},{18,... | collective-permute-start | bytes 1449992 | tf_op jit(solution)/shard_map/send_23/ppermute | solution.py:361
  80.9 13.2 %collective-permute-start.23 = (bf16[8,30208]{1,0:T(8,128)(2,1)S(1)}, bf16[8,30208]{1,0:T(8,128)(2,1)S(1)}, u32[]{:S(2)}, u32[]{:S(2)}) collective-permute-start(bf16[8,30208]{1,0:T(8,128)(2,1)S(1)} %get-tuple-element.76), channel_id=1, source_target_pairs={{0,4},{2,6},{4,0},{6,2},{8,12},{10,14},{12,8},{14,10},{16,20},{18,... | collective-permute-start | bytes 1449992 | tf_op jit(solution)/shard_map/send_22/ppermute | solution.py:361
  83.4 46.8 %copy-start.3 = (s32[1024]{0:T(1024)S(1)}, s32[1024]{0:T(1024)}, u32[]{:S(2)}) copy-start(s32[1024]{0:T(1024)} %param.10) | copy-start | bytes 12292
  83.5 49.3 %copy-start.4 = (f32[1024]{0:T(1024)S(1)}, f32[1024]{0:T(1024)}, u32[]{:S(2)}) copy-start(f32[1024]{0:T(1024)} %param.11) | copy-start | bytes 12292
  94.1 13.8 %collective-permute-start.20 = (bf16[8,30208]{1,0:T(8,128)(2,1)S(1)}, bf16[8,30208]{1,0:T(8,128)(2,1)S(1)}, u32[]{:S(2)}, u32[]{:S(2)}) collective-permute-start(bf16[8,30208]{1,0:T(8,128)(2,1)S(1)} %add_convert_fusion.6), channel_id=1, source_target_pairs={{0,8},{2,10},{4,12},{6,14},{8,16},{10,18},{12,20},{14,22},{16,24},... | collective-permute-start | bytes 1449992 | tf_op jit(solution)/shard_map/send_27/ppermute | solution.py:361
  94.1 12.0 %collective-permute-start.24 = (bf16[8,30208]{1,0:T(8,128)(2,1)S(1)}, bf16[8,30208]{1,0:T(8,128)(2,1)S(1)}, u32[]{:S(2)}, u32[]{:S(2)}) collective-permute-start(bf16[8,30208]{1,0:T(8,128)(2,1)S(1)} %get-tuple-element.77), channel_id=1, source_target_pairs={{0,4},{2,6},{4,0},{6,2},{8,12},{10,14},{12,8},{14,10},{16,20},{18,... | collective-permute-start | bytes 1449992 | tf_op jit(solution)/shard_map/send_25/ppermute | solution.py:361
  94.2 12.2 %collective-permute-start.27 = (bf16[8,30208]{1,0:T(8,128)(2,1)S(1)}, bf16[8,30208]{1,0:T(8,128)(2,1)S(1)}, u32[]{:S(2)}, u32[]{:S(2)}) collective-permute-start(bf16[8,30208]{1,0:T(8,128)(2,1)S(1)} %add_convert_fusion.2), channel_id=1, source_target_pairs={{0,2},{2,0},{4,6},{6,4},{8,10},{10,8},{12,14},{14,12},{16,18},{18,... | collective-permute-start | bytes 1449992 | tf_op jit(solution)/shard_map/send_26/ppermute | solution.py:361
  106.1 11.2 %collective-permute-start.25 = (bf16[8,30208]{1,0:T(8,128)(2,1)S(1)}, bf16[8,30208]{1,0:T(8,128)(2,1)S(1)}, u32[]{:S(2)}, u32[]{:S(2)}) collective-permute-start(bf16[8,30208]{1,0:T(8,128)(2,1)S(1)} %add_convert_fusion.4), channel_id=1, source_target_pairs={{0,4},{2,6},{4,0},{6,2},{8,12},{10,14},{12,8},{14,10},{16,20},{18,... | collective-permute-start | bytes 1449992 | tf_op jit(solution)/shard_map/send_28/ppermute | solution.py:361
  106.4 11.3 %collective-permute-start.28 = (bf16[8,30208]{1,0:T(8,128)(2,1)S(1)}, bf16[8,30208]{1,0:T(8,128)(2,1)S(1)}, u32[]{:S(2)}, u32[]{:S(2)}) collective-permute-start(bf16[8,30208]{1,0:T(8,128)(2,1)S(1)} %get-tuple-element.84), channel_id=1, source_target_pairs={{0,2},{2,0},{4,6},{6,4},{8,10},{10,8},{12,14},{14,12},{16,18},{18,... | collective-permute-start | bytes 1449992 | tf_op jit(solution)/shard_map/send_29/ppermute | solution.py:361
  107.9 11.1 %collective-permute-start.30 = (bf16[8,30208]{1,0:T(8,128)(2,1)S(1)}, bf16[8,30208]{1,0:T(8,128)(2,1)S(1)}, u32[]{:S(2)}, u32[]{:S(2)}) collective-permute-start(bf16[8,30208]{1,0:T(8,128)(2,1)S(1)} %add_convert_fusion.1), channel_id=1, source_target_pairs={{0,24},{2,26},{4,28},{6,30},{8,0},{10,2},{12,4},{14,6},{16,8},{18,... | collective-permute-start | bytes 1449992 | tf_op jit(solution)/shard_map/send_30/ppermute | solution.py:361
  117.3 10.2 %collective-permute-start.26 = (bf16[8,30208]{1,0:T(8,128)(2,1)S(1)}, bf16[8,30208]{1,0:T(8,128)(2,1)S(1)}, u32[]{:S(2)}, u32[]{:S(2)}) collective-permute-start(bf16[8,30208]{1,0:T(8,128)(2,1)S(1)} %add_convert_fusion.5), channel_id=1, source_target_pairs={{0,4},{2,6},{4,0},{6,2},{8,12},{10,14},{12,8},{14,10},{16,20},{18,... | collective-permute-start | bytes 1449992 | tf_op jit(solution)/shard_map/send_31/ppermute | solution.py:361
  117.7 10.1 %collective-permute-start.29 = (bf16[8,30208]{1,0:T(8,128)(2,1)S(1)}, bf16[8,30208]{1,0:T(8,128)(2,1)S(1)}, u32[]{:S(2)}, u32[]{:S(2)}) collective-permute-start(bf16[8,30208]{1,0:T(8,128)(2,1)S(1)} %add_convert_fusion.3), channel_id=1, source_target_pairs={{0,2},{2,0},{4,6},{6,4},{8,10},{10,8},{12,14},{14,12},{16,18},{18,... | collective-permute-start | bytes 1449992 | tf_op jit(solution)/shard_map/send_32/ppermute | solution.py:361
  119.2 11.0 %collective-permute-start.31 = (bf16[8,30208]{1,0:T(8,128)(2,1)S(1)}, bf16[8,30208]{1,0:T(8,128)(2,1)S(1)}, u32[]{:S(2)}, u32[]{:S(2)}) collective-permute-start(bf16[8,30208]{1,0:T(8,128)(2,1)S(1)} %add_convert_fusion), channel_id=1, source_target_pairs={{0,24},{2,26},{4,28},{6,30},{8,0},{10,2},{12,4},{14,6},{16,8},{18,... | collective-permute-start | bytes 1449992 | tf_op jit(solution)/shard_map/send_33/ppermute | solution.py:361
  131.6 1.3 collective-permute-start.32

commit v5 on v4

--- a/solution.py
+++ b/solution.py
@@ -19,40 +19,40 @@
 
 
 PLAN = [
-    (GATHER, Z, -1, (-1, 0, 0), ()),
+    (GATHER, Z, 1, (1, 0, 0), ()),
     (GATHER, X, 1, (0, 0, 1), ()),
     (GATHER, Y, 1, (0, 1, 0), ()),
-    (GATHER, Z, -1, (2, 0, 0), (0,)),
-    (GATHER, X, 1, (-1, 0, 1), (1,)),
+    (GATHER, Z, 1, (2, 0, 0), (0,)),
+    (GATHER, X, 1, (1, 0, 1), (1,)),
     (GATHER, Y, 1, (0, 1, 1), (2,)),
-    (GATHER, Z, 1, (1, 1, 0), (3,)),
+    (GATHER, Z, -1, (-1, 0, 1), (3,)),
     (GATHER, X, 1, (2, 0, 1), (4,)),
-    (GATHER, Y, 1, (-1, 1, 1), (5,)),
-    (FLOWS, 0, [(0, 0, 0), (-1, 0, 0), (0, 0, 1), (0, 1, 0), (2, 0, 0), (-1, 0, 1), (0, 1, 1), (1, 1, 0), (2, 0, 1), (-1, 1, 1)], ()),
+    (GATHER, Y, 1, (1, 1, 1), (5,)),
+    (FLOWS, 0, [(0, 0, 0), (1, 0, 0), (0, 0, 1), (0, 1, 0), (2, 0, 0), (1, 0, 1), (0, 1, 1), (-1, 0, 1), (2, 0, 1), (1, 1, 1)], ()),
     (GRADS, 0),
-    (GATHER, Z, 1, (1, 0, 0), (6,)),
-    (GATHER, X, 1, (1, 1, 1), (7,)),
+    (GATHER, Z, -1, (-1, 1, 1), (6,)),
+    (GATHER, X, 1, (-1, 0, 0), (7,)),
     (GATHER, Y, 1, (2, 1, 1), (8,)),
-    (GATHER, Z, 1, (2, 1, 0), (9, 11)),
-    (GATHER, X, 1, (1, 0, 1), (9, 12)),
-    (GATHER, Y, 1, (-1, 1, 0), (9, 13)),
-    (FLOWS, 1, [(1, 0, 0), (1, 1, 1), (2, 1, 1), (2, 1, 0), (1, 0, 1), (-1, 1, 0)], ()),
+    (GATHER, Z, -1, (-1, 1, 0), (9, 11)),
+    (GATHER, X, 1, (1, 1, 0), (9, 12)),
+    (GATHER, Y, 1, (2, 1, 0), (9, 13)),
+    (FLOWS, 1, [(-1, 1, 1), (-1, 0, 0), (2, 1, 1), (-1, 1, 0), (1, 1, 0), (2, 1, 0)], ()),
     (GRADS, 1),
     (REDUCE, Y, 1, (0, 1, 1), (16,)),
-    (REDUCE, X, 1, (-1, 1, 1), (15,)),
-    (REDUCE, Z, -1, (-1, 0, 1), (14,)),
+    (REDUCE, X, 1, (1, 1, 1), (15,)),
+    (REDUCE, Z, 1, (1, 0, 0), (14,)),
     (REDUCE, Y, 1, (2, 1, 1), (17, 19)),
-    (REDUCE, X, 1, (1, 1, 1), (17, 20)),
-    (REDUCE, Z, -1, (-1, 0, 0), (17, 21)),
+    (REDUCE, X, 1, (-1, 1, 1), (17, 20)),
+    (REDUCE, Z, 1, (1, 0, 1), (17, 21)),
     (REDUCE, Y, 1, (2, 1, 0), (22,)),
     (REDUCE, X, 1, (2, 0, 1), (23,)),
-    (REDUCE, Z, -1, (-1, 1, 0), (24,)),
-    (REDUCE, Y, 1, (1, 1, 0), (25,)),
-    (REDUCE, X, 1, (1, 0, 1), (26,)),
-    (REDUCE, Z, 1, (2, 0, 0), (27,)),
+    (REDUCE, Z, 1, (1, 1, 0), (24,)),
+    (REDUCE, Y, 1, (-1, 1, 0), (25,)),
+    (REDUCE, X, 1, (-1, 0, 1), (26,)),
+    (REDUCE, Z, -1, (2, 0, 0), (27,)),
     (REDUCE, Y, 1, (0, 1, 0), (28,)),
     (REDUCE, X, 1, (0, 0, 1), (29,)),
-    (REDUCE, Z, 1, (1, 0, 0), (30,)),
+    (REDUCE, Z, -1, (-1, 0, 0), (30,)),
 ]
 
 

time: 134 us -> 132 us (0.985)
  starting transfers between devices: 41.2 us -> 37.6 us
  waiting for transfers between devices: 71.2 us -> 72.7 us
    ppermute x30, starting transfers between devices: 41 us -> 37.4 us  [shards(): came = lax.ppermute(after(block, waits), 'br', pairs)]
    ppermute x30, waiting for transfers between devices: 67.7 us -> 69.2 us  [shards(): came = lax.ppermute(after(block, waits), 'br', pairs)]
  transfers between devices with their start and end apart: 33 -> 33, of which waited for: 18 -> 14; matrix products, arithmetic and copies ran while one was open for 1% -> 1% of each run, Pallas kernels for 7% -> 8%
where the time goes in v5:
time: 132 us; the launch traced here: 131 us
  waiting for transfers between devices  72.7 us (55%)
  starting transfers between devices  37.6 us (28%)
  Pallas kernels  14.4 us (11%)
  local copies, waits for them, and re-layouts  4.25 us (3%)
  other arithmetic  1.63 us (1%)
    ppermute x30, waiting for transfers between devices, shards(): came = lax.ppermute(after(block, waits), 'br', pairs)  69.2 us
    ppermute x30, starting transfers between devices, shards(): came = lax.ppermute(after(block, waits), 'br', pairs)  37.4 us
    pallas_call x2, Pallas kernels, flows_of(): pl.pallas_call(functools.partial(flows_kernel, tile_of(width, 128)), in_s...  6.36 us
    unnamed x16, local copies, waits for them, and re-layouts  4.25 us
    pallas_call x2, Pallas kernels, grads_of(): pl.pallas_call(functools.partial(grads_kernel, tile_of(width, 128)), in_s...  3.55 us
    ppermute x3, waiting for transfers between devices, over_bus(): return (value, lax.ppermute(value, 'bus', [(0, 1), (1, 0)]))  3.49 us
    pallas_call x1, Pallas kernels, inject_of(): pl.pallas_call(inject_kernel, grid=(width // tile,), in_specs=[pl.BlockSp...  3.14 us
  transfers between devices with their start and end apart: 33, of which 14 were waited for; matrix products, arithmetic and copies ran while one was open for 1% of the time, Pallas kernels for 8%

profile of v5, /device:TPU:0, one launch (start us, length us, event | category | flops | bytes accessed | tf_op | source)
XLA Modules:
  0.0 131.4 jit_solution(8351529614004577799)
XLA Ops:
  0.7 3.1 %inject.1.refs_0_ = bf16[8,30208]{1,0:T(8,128)(2,1)} custom-call(s32[1]{0:T(128)} %bitcast.bus_ref, f32[8,1024]{1,0:T(8,128)} %release_ref.1, f32[1,1024]{1,0:T(1,128)} %bitcast.11, s32[1,1024]{1,0:T(1,128)} %bitcast.5, bf16[8,30208]{1,0:T(8,128)(2,1)} %net_ref.1), custom_call_target="tpu_custom_call" | custom-call | tf_op jit(solution)/shard_map/inject/pallas_call | solution.py:184
  3.8 3.0 %collective-permute-start = (bf16[8,30208]{1,0:T(8,128)(2,1)}, bf16[8,30208]{1,0:T(8,128)(2,1)S(1)}, u32[]{:S(2)}, u32[]{:S(2)}) collective-permute-start(bf16[8,30208]{1,0:T(8,128)(2,1)} %inject.1.refs_0_), channel_id=1, source_target_pairs={{0,8},{2,10},{4,12},{6,14},{8,16},{10,18},{12,20},{14,22},{16,24},... | collective-permute-start | bytes 1449992 | tf_op jit(solution)/shard_map/send_0/ppermute | solution.py:361
  6.8 1.5 %collective-permute-start.1 = (bf16[8,30208]{1,0:T(8,128)(2,1)}, bf16[8,30208]{1,0:T(8,128)(2,1)S(1)}, u32[]{:S(2)}, u32[]{:S(2)}) collective-permute-start(bf16[8,30208]{1,0:T(8,128)(2,1)} %inject.1.refs_0_), channel_id=1, source_target_pairs={{0,2},{2,0},{4,6},{6,4},{8,10},{10,8},{12,14},{14,12},{16,18},{18,... | collective-permute-start | bytes 1449992 | tf_op jit(solution)/shard_map/send_1/ppermute | solution.py:361
  8.3 1.5 %collective-permute-start.2 = (bf16[8,30208]{1,0:T(8,128)(2,1)}, bf16[8,30208]{1,0:T(8,128)(2,1)S(1)}, u32[]{:S(2)}, u32[]{:S(2)}) collective-permute-start(bf16[8,30208]{1,0:T(8,128)(2,1)} %inject.1.refs_0_), channel_id=1, source_target_pairs={{0,4},{2,6},{4,0},{6,2},{8,12},{10,14},{12,8},{14,10},{16,20},{18,... | collective-permute-start | bytes 1449992 | tf_op jit(solution)/shard_map/send_2/ppermute | solution.py:361
  9.8 10.3 %collective-permute-done.refs_1_ = bf16[8,30208]{1,0:T(8,128)(2,1)S(1)} collective-permute-done((bf16[8,30208]{1,0:T(8,128)(2,1)}, bf16[8,30208]{1,0:T(8,128)(2,1)S(1)}, u32[]{:S(2)}, u32[]{:S(2)}) %collective-permute-start) | collective-permute-done | bytes 483360 | tf_op jit(solution)/shard_map/send_0/ppermute | solution.py:361
  20.1 1.5 %collective-permute-start.4 = (bf16[8,30208]{1,0:T(8,128)(2,1)S(1)}, bf16[8,30208]{1,0:T(8,128)(2,1)S(1)}, u32[]{:S(2)}, u32[]{:S(2)}) collective-permute-start(bf16[8,30208]{1,0:T(8,128)(2,1)S(1)} %collective-permute-done.refs_1_), channel_id=1, source_target_pairs={{0,2},{2,0},{4,6},{6,4},{8,10},{10,8},{12,14},{14,12},{16,18},{18,... | collective-permute-start | bytes 1449992 | tf_op jit(solution)/shard_map/send_4/ppermute | solution.py:361
  21.6 1.5 %collective-permute-start.5 = (bf16[8,30208]{1,0:T(8,128)(2,1)S(1)}, bf16[8,30208]{1,0:T(8,128)(2,1)S(1)}, u32[]{:S(2)}, u32[]{:S(2)}) collective-permute-start(bf16[8,30208]{1,0:T(8,128)(2,1)S(1)} %collective-permute-done.1.refs_2_), channel_id=1, source_target_pairs={{0,4},{2,6},{4,0},{6,2},{8,12},{10,14},{12,8},{14,10},{16,20},{18,... | collective-permute-start | bytes 1449992 | tf_op jit(solution)/shard_map/send_5/ppermute | solution.py:361
  23.1 12.2 %collective-permute-done.3.refs_4_ = bf16[8,30208]{1,0:T(8,128)(2,1)S(1)} collective-permute-done((bf16[8,30208]{1,0:T(8,128)(2,1)S(1)}, bf16[8,30208]{1,0:T(8,128)(2,1)S(1)}, u32[]{:S(2)}, u32[]{:S(2)}) %collective-permute-start.3) | collective-permute-done | bytes 483360 | tf_op jit(solution)/shard_map/send_3/ppermute | solution.py:361
  35.3 1.1 collective-permute-start.7
  36.4 1.5 %collective-permute-start.8 = (bf16[8,30208]{1,0:T(8,128)(2,1)S(1)}, bf16[8,30208]{1,0:T(8,128)(2,1)S(1)}, u32[]{:S(2)}, u32[]{:S(2)}) collective-permute-start(bf16[8,30208]{1,0:T(8,128)(2,1)S(1)} %collective-permute-done.4.refs_5_), channel_id=1, source_target_pairs={{0,4},{2,6},{4,0},{6,2},{8,12},{10,14},{12,8},{14,10},{16,20},{18,... | collective-permute-start | bytes 1449992 | tf_op jit(solution)/shard_map/send_8/ppermute | solution.py:361
  37.9 8.3 %collective-permute-done.6.refs_7_ = bf16[8,30208]{1,0:T(8,128)(2,1)S(1)} collective-permute-done((bf16[8,30208]{1,0:T(8,128)(2,1)S(1)}, bf16[8,30208]{1,0:T(8,128)(2,1)S(1)}, u32[]{:S(2)}, u32[]{:S(2)}) %collective-permute-start.6) | collective-permute-done | bytes 483360 | tf_op jit(solution)/shard_map/send_6/ppermute | solution.py:361
  46.2 1.3 collective-permute-start.10
  47.5 1.0 collective-permute-start.13
  48.5 1.5 %collective-permute-start.14 = (bf16[8,30208]{1,0:T(8,128)(2,1)S(1)}, bf16[8,30208]{1,0:T(8,128)(2,1)S(1)}, u32[]{:S(2)}, u32[]{:S(2)}) collective-permute-start(bf16[8,30208]{1,0:T(8,128)(2,1)S(1)} %collective-permute-done.7.refs_8_), channel_id=1, source_target_pairs={{0,4},{2,6},{4,0},{6,2},{8,12},{10,14},{12,8},{14,10},{16,20},{18,... | collective-permute-start | bytes 1449992 | tf_op jit(solution)/shard_map/send_13/ppermute | solution.py:361
  50.1 3.2 %copy-done = bf16[128,30208]{1,0:T(8,128)(2,1)S(1)} copy-done((bf16[128,30208]{1,0:T(8,128)(2,1)S(1)}, bf16[128,30208]{1,0:T(8,128)(2,1)}, u32[]{:S(2)}) %copy-start) | copy-done | bytes 7733272
  53.3 1.0 copy-done.2
  54.3 3.2 %flows.2.mine_ref = f32[80,128]{1,0:T(8,128)S(1)} custom-call(bf16[8,30208]{1,0:T(8,128)(2,1)S(1)} %copy-done.2, bf16[8,30208]{1,0:T(8,128)(2,1)S(1)} %collective-permute-done.refs_1_, bf16[8,30208]{1,0:T(8,128)(2,1)S(1)} %collective-permute-done.1.refs_2_, bf16[8,30208]{1,0:T(8,128)(2,1)S(1)} %collective-permute-done.2.refs_3_, ...), custom_call_target="tpu_custom_call" | custom-call | tf_op jit(solution)/shard_map/flows/pallas_call | solution.py:228
  57.5 1.3 collective-permute-start.11
  58.8 0.9 collective-permute-start.15
  59.8 1.5 %collective-permute-start.16 = (bf16[8,30208]{1,0:T(8,128)(2,1)S(1)}, bf16[8,30208]{1,0:T(8,128)(2,1)S(1)}, u32[]{:S(2)}, u32[]{:S(2)}) collective-permute-start(bf16[8,30208]{1,0:T(8,128)(2,1)S(1)} %collective-permute-done.3.refs_4_), channel_id=1, source_target_pairs={{0,4},{2,6},{4,0},{6,2},{8,12},{10,14},{12,8},{14,10},{16,20},{18,... | collective-permute-start | bytes 1449992 | tf_op jit(solution)/shard_map/send_16/ppermute | solution.py:361
  61.3 0.1 select_reduce_fusion
  61.4 1.1 collective-permute-done.9.other_ref
  62.5 1.9 %grads.2 = (f32[8,30208]{1,0:T(8,128)S(1)}, bf16[8,30208]{1,0:T(8,128)(2,1)S(1)}, f32[8,30208]{1,0:T(8,128)S(1)}, f32[8,30208]{1,0:T(8,128)S(1)}, f32[8,30208]{1...) custom-call(f32[80,128]{1,0:T(8,128)S(1)} %flows.2.mine_ref, ...), custom_call_target="tpu_custom_call" | custom-call | tf_op jit(solution)/shard_map/grads/pallas_call | solution.py:262
  64.4 1.9 %collective-permute-done.11.refs_3_ = bf16[8,30208]{1,0:T(8,128)(2,1)S(1)} collective-permute-done((bf16[8,30208]{1,0:T(8,128)(2,1)S(1)}, bf16[8,30208]{1,0:T(8,128)(2,1)S(1)}, u32[]{:S(2)}, u32[]{:S(2)}) %collective-permute-start.11) | collective-permute-done | bytes 483360 | tf_op jit(solution)/shard_map/send_14/ppermute | solution.py:361
  66.3 3.0 %collective-permute-start.12 = (bf16[8,30208]{1,0:T(8,128)(2,1)S(1)}, bf16[8,30208]{1,0:T(8,128)(2,1)S(1)}, u32[]{:S(2)}, u32[]{:S(2)}) collective-permute-start(bf16[8,30208]{1,0:T(8,128)(2,1)S(1)} %get-tuple-element.57), channel_id=1, source_target_pairs={{0,24},{2,26},{4,28},{6,30},{8,0},{10,2},{12,4},{14,6},{16,8},{18,... | collective-permute-start | bytes 1449992 | tf_op jit(solution)/shard_map/send_21/ppermute | solution.py:361
  69.3 1.3 collective-permute-start.18
  70.7 2.0 %collective-permute-start.22 = (bf16[8,30208]{1,0:T(8,128)(2,1)S(1)}, bf16[8,30208]{1,0:T(8,128)(2,1)S(1)}, u32[]{:S(2)}, u32[]{:S(2)}) collective-permute-start(bf16[8,30208]{1,0:T(8,128)(2,1)S(1)} %get-tuple-element.75), channel_id=1, source_target_pairs={{0,4},{2,6},{4,0},{6,2},{8,12},{10,14},{12,8},{14,10},{16,20},{18,... | collective-permute-start | bytes 1449992 | tf_op jit(solution)/shard_map/send_19/ppermute | solution.py:361
  72.6 3.1 %flows.3.mine_ref = f32[48,128]{1,0:T(8,128)S(1)} custom-call(bf16[8,30208]{1,0:T(8,128)(2,1)S(1)} %collective-permute-done.10.refs_0_, bf16[8,30208]{1,0:T(8,128)(2,1)S(1)} %collective-permute-done.13.refs_1_, bf16[8,30208]{1,0:T(8,128)(2,1)S(1)} %collective-permute-done.14.refs_2_, bf16[8,30208]{1,0:T(8,128)(2,1)S(1)} %collective-permute-done.11.refs_3_, ...), custom_call_target="tpu_custom_call" | custom-call | tf_op jit(solution)/shard_map/flows/pallas_call | solution.py:228
  75.8 0.1 collective-permute-start.17
  75.8 1.2 collective-permute-done.17.other_ref
  77.0 1.6 %grads.3 = (bf16[8,30208]{1,0:T(8,128)(2,1)S(1)}, f32[8,30208]{1,0:T(8,128)S(1)}, bf16[8,30208]{1,0:T(8,128)(2,1)S(1)}, f32[8,30208]{1,0:T(8,128)S(1)}, f32[8,30...) custom-call(f32[48,128]{1,0:T(8,128)S(1)} %flows.3.mine_ref, f32[48,128]{1,0:T(8,128)S(1)} %collective-permute-done.17.other_ref, ...), custom_call_target="tpu_custom_call" | custom-call | tf_op jit(solution)/shard_map/grads/pallas_call | solution.py:262
  78.7 1.2 collective-permute-start.19
  79.9 1.3 collective-permute-start.21
  81.2 2.0 %collective-permute-start.23 = (bf16[8,30208]{1,0:T(8,128)(2,1)S(1)}, bf16[8,30208]{1,0:T(8,128)(2,1)S(1)}, u32[]{:S(2)}, u32[]{:S(2)}) collective-permute-start(bf16[8,30208]{1,0:T(8,128)(2,1)S(1)} %get-tuple-element.76), channel_id=1, source_target_pairs={{0,4},{2,6},{4,0},{6,2},{8,12},{10,14},{12,8},{14,10},{16,20},{18,... | collective-permute-start | bytes 1449992 | tf_op jit(solution)/shard_map/send_22/ppermute | solution.py:361
  83.2 0.1 add_convert_fusion.6
  83.3 8.5 %collective-permute-done.19 = bf16[8,30208]{1,0:T(8,128)(2,1)S(1)} collective-permute-done((bf16[8,30208]{1,0:T(8,128)(2,1)S(1)}, bf16[8,30208]{1,0:T(8,128)(2,1)S(1)}, u32[]{:S(2)}, u32[]{:S(2)}) %collective-permute-start.19) | collective-permute-done | bytes 483360 | tf_op jit(solution)/shard_map/send_24/ppermute | solution.py:361
  91.8 2.1 %collective-permute-start.20 = (bf16[8,30208]{1,0:T(8,128)(2,1)S(1)}, bf16[8,30208]{1,0:T(8,128)(2,1)S(1)}, u32[]{:S(2)}, u32[]{:S(2)}) collective-permute-start(bf16[8,30208]{1,0:T(8,128)(2,1)S(1)} %add_convert_fusion.6), channel_id=1, source_target_pairs={{0,24},{2,26},{4,28},{6,30},{8,0},{10,2},{12,4},{14,6},{16,8},{18,... | collective-permute-start | bytes 1449992 | tf_op jit(solution)/shard_map/send_27/ppermute | solution.py:361
  93.9 0.1 collective-permute-start.24
  94.0 0.1 add_convert_fusion.2
  94.1 0.0 copy-start.4
  94.1 0.8 collective-permute-start.27
  94.9 0.2 add_convert_fusion.3
  95.0 0.1 add_convert_fusion.4
  95.1 10.0 %collective-permute-done.24 = bf16[8,30208]{1,0:T(8,128)(2,1)S(1)} collective-permute-done((bf16[8,30208]{1,0:T(8,128)(2,1)S(1)}, bf16[8,30208]{1,0:T(8,128)(2,1)S(1)}, u32[]{:S(2)}, u32[]{:S(2)}) %collective-permute-start.24) | collective-permute-done | bytes 483360 | tf_op jit(solution)/shard_map/send_25/ppermute | solution.py:361
  105.1 0.1 collective-permute-start.25
  105.2 0.0 collective-permute-done.27
  105.3 0.5 collective-permute-start.28
  105.8 0.2 add_convert_fusion.1
  105.9 1.8 %collective-permute-start.30 = (bf16[8,30208]{1,0:T(8,128)(2,1)S(1)}, bf16[8,30208]{1,0:T(8,128)(2,1)S(1)}, u32[]{:S(2)}, u32[]{:S(2)}) collective-permute-start(bf16[8,30208]{1,0:T(8,128)(2,1)S(1)} %add_convert_fusion.1), channel_id=1, source_target_pairs={{0,8},{2,10},{4,12},{6,14},{8,16},{10,18},{12,20},{14,22},{16,24},... | collective-permute-start | bytes 1449992 | tf_op jit(solution)/shard_map/send_30/ppermute | solution.py:361
  107.7 0.1 add_convert_fusion.5
  107.8 8.5 %collective-permute-done.25 = bf16[8,30208]{1,0:T(8,128)(2,1)S(1)} collective-permute-done((bf16[8,30208]{1,0:T(8,128)(2,1)S(1)}, bf16[8,30208]{1,0:T(8,128)(2,1)S(1)}, u32[]{:S(2)}, u32[]{:S(2)}) %collective-permute-start.25) | collective-permute-done | bytes 483360 | tf_op jit(solution)/shard_map/send_28/ppermute | solution.py:361
  116.3 0.1 collective-permute-start.26
  116.4 0.0 collective-permute-done.28
  116.5 0.5 collective-permute-start.29
  117.0 0.3 collective-permute-done.30
  117.3 0.2 add_convert_fusion
  117.5 1.5 %collective-permute-start.31 = (bf16[8,30208]{1,0:T(8,128)(2,1)S(1)}, bf16[8,30208]{1,0:T(8,128)(2,1)S(1)}, u32[]{:S(2)}, u32[]{:S(2)}) collective-permute-start(bf16[8,30208]{1,0:T(8,128)(2,1)S(1)} %add_convert_fusion), channel_id=1, source_target_pairs={{0,8},{2,10},{4,12},{6,14},{8,16},{10,18},{12,20},{14,22},{16,24},... | collective-permute-start | bytes 1449992 | tf_op jit(solution)/shard_map/send_33/ppermute | solution.py:361
  119.0 6.7 %collective-permute-done.26.refs_2_ = bf16[8,30208]{1,0:T(8,128)(2,1)S(1)} collective-permute-done((bf16[8,30208]{1,0:T(8,128)(2,1)S(1)}, bf16[8,30208]{1,0:T(8,128)(2,1)S(1)}, u32[]{:S(2)}, u32[]{:S(2)}) %collective-permute-start.26) | collective-permute-done | bytes 483360 | tf_op jit(solution)/shard_map/send_31/ppermute | solution.py:361
  125.7 0.2 collective-permute-done.29.refs_3_
  125.8 2.3 %collective-permute-done.31.refs_4_ = bf16[8,30208]{1,0:T(8,128)(2,1)S(1)} collective-permute-done((bf16[8,30208]{1,0:T(8,128)(2,1)S(1)}, bf16[8,30208]{1,0:T(8,128)(2,1)S(1)}, u32[]{:S(2)}, u32[]{:S(2)}) %collective-permute-start.31) | collective-permute-done | bytes 483360 | tf_op jit(solution)/shard_map/send_33/ppermute | solution.py:361
  128.1 1.4 %finish.1 = (f32[8,30208]{1,0:T(8,128)}, f32[8,1024]{1,0:T(8,128)S(1)}) custom-call(s32[1]{0:T(128)} %bitcast.bus_ref, s32[1,1024]{1,0:T(1,128)S(1)} %bitcast.6, f32[8,30208]{1,0:T(8,128)S(1)} %get-tuple-element.53.refs_0_, bf16[8,30208]{1,0:T(8,128)(2,1)S(1)} %collective-permute-done.12.refs_1_, bf16[8,30208]{1,0:T(8,128)(2,1)S(1)} %collective-permute-done.26.refs_2_, ...), custom_call_target="tpu_custom_call" | custom-call | tf_op jit(solution)/shard_map/finish/pallas_call | solution.py:301
  129.5 0.1 collective-permute-start.32
  129.6 1.2 collective-permute-done.32
  130.8 0.6 add_multiply_fusion
  (33 shorter events, 0.1 us)
Async XLA Ops:
  0.6 60.6 %copy-start.5 = (f32[16]{0:T(128)S(1)}, f32[16]{0:T(128)}, u32[]{:S(2)}) copy-start(f32[16]{0:T(128)} %param.15) | copy-start | bytes 196
  0.6 60.6 %copy-start.6 = (s32[128]{0:T(128)S(1)}, s32[128]{0:T(128)}, u32[]{:S(2)}) copy-start(s32[128]{0:T(128)} %param.13) | copy-start | bytes 1540
  0.7 60.6 %copy-start.7 = (f32[16]{0:T(128)S(1)}, f32[16]{0:T(128)}, u32[]{:S(2)}) copy-start(f32[16]{0:T(128)} %param.14) | copy-start | bytes 196
  3.8 16.3 %collective-permute-start = (bf16[8,30208]{1,0:T(8,128)(2,1)}, bf16[8,30208]{1,0:T(8,128)(2,1)S(1)}, u32[]{:S(2)}, u32[]{:S(2)}) collective-permute-start(bf16[8,30208]{1,0:T(8,128)(2,1)} %inject.1.refs_0_), channel_id=1, source_target_pairs={{0,8},{2,10},{4,12},{6,14},{8,16},{10,18},{12,20},{14,22},{16,24},... | collective-permute-start | bytes 1449992 | tf_op jit(solution)/shard_map/send_0/ppermute | solution.py:361
  6.8 13.3 %collective-permute-start.1 = (bf16[8,30208]{1,0:T(8,128)(2,1)}, bf16[8,30208]{1,0:T(8,128)(2,1)S(1)}, u32[]{:S(2)}, u32[]{:S(2)}) collective-permute-start(bf16[8,30208]{1,0:T(8,128)(2,1)} %inject.1.refs_0_), channel_id=1, source_target_pairs={{0,2},{2,0},{4,6},{6,4},{8,10},{10,8},{12,14},{14,12},{16,18},{18,... | collective-permute-start | bytes 1449992 | tf_op jit(solution)/shard_map/send_1/ppermute | solution.py:361
  8.3 13.3 %collective-permute-start.2 = (bf16[8,30208]{1,0:T(8,128)(2,1)}, bf16[8,30208]{1,0:T(8,128)(2,1)S(1)}, u32[]{:S(2)}, u32[]{:S(2)}) collective-permute-start(bf16[8,30208]{1,0:T(8,128)(2,1)} %inject.1.refs_0_), channel_id=1, source_target_pairs={{0,4},{2,6},{4,0},{6,2},{8,12},{10,14},{12,8},{14,10},{16,20},{18,... | collective-permute-start | bytes 1449992 | tf_op jit(solution)/shard_map/send_2/ppermute | solution.py:361
  20.1 15.2 %collective-permute-start.3 = (bf16[8,30208]{1,0:T(8,128)(2,1)S(1)}, bf16[8,30208]{1,0:T(8,128)(2,1)S(1)}, u32[]{:S(2)}, u32[]{:S(2)}) collective-permute-start(bf16[8,30208]{1,0:T(8,128)(2,1)S(1)} %collective-permute-done.refs_1_), channel_id=1, source_target_pairs={{0,8},{2,10},{4,12},{6,14},{8,16},{10,18},{12,20},{14,22},{16,24},... | collective-permute-start | bytes 1449992 | tf_op jit(solution)/shard_map/send_3/ppermute | solution.py:361
  20.1 15.2 %collective-permute-start.4 = (bf16[8,30208]{1,0:T(8,128)(2,1)S(1)}, bf16[8,30208]{1,0:T(8,128)(2,1)S(1)}, u32[]{:S(2)}, u32[]{:S(2)}) collective-permute-start(bf16[8,30208]{1,0:T(8,128)(2,1)S(1)} %collective-permute-done.refs_1_), channel_id=1, source_target_pairs={{0,2},{2,0},{4,6},{6,4},{8,10},{10,8},{12,14},{14,12},{16,18},{18,... | collective-permute-start | bytes 1449992 | tf_op jit(solution)/shard_map/send_4/ppermute | solution.py:361
  21.6 14.8 %collective-permute-start.5 = (bf16[8,30208]{1,0:T(8,128)(2,1)S(1)}, bf16[8,30208]{1,0:T(8,128)(2,1)S(1)}, u32[]{:S(2)}, u32[]{:S(2)}) collective-permute-start(bf16[8,30208]{1,0:T(8,128)(2,1)S(1)} %collective-permute-done.1.refs_2_), channel_id=1, source_target_pairs={{0,4},{2,6},{4,0},{6,2},{8,12},{10,14},{12,8},{14,10},{16,20},{18,... | collective-permute-start | bytes 1449992 | tf_op jit(solution)/shard_map/send_5/ppermute | solution.py:361
  35.3 10.9 %collective-permute-start.6 = (bf16[8,30208]{1,0:T(8,128)(2,1)S(1)}, bf16[8,30208]{1,0:T(8,128)(2,1)S(1)}, u32[]{:S(2)}, u32[]{:S(2)}) collective-permute-start(bf16[8,30208]{1,0:T(8,128)(2,1)S(1)} %collective-permute-done.1.refs_2_), channel_id=1, source_target_pairs={{0,24},{2,26},{4,28},{6,30},{8,0},{10,2},{12,4},{14,6},{16,8},{18,... | collective-permute-start | bytes 1449992 | tf_op jit(solution)/shard_map/send_6/ppermute | solution.py:361
  35.3 12.2 %collective-permute-start.7 = (bf16[8,30208]{1,0:T(8,128)(2,1)S(1)}, bf16[8,30208]{1,0:T(8,128)(2,1)S(1)}, u32[]{:S(2)}, u32[]{:S(2)}) collective-permute-start(bf16[8,30208]{1,0:T(8,128)(2,1)S(1)} %collective-permute-done.3.refs_4_), channel_id=1, source_target_pairs={{0,2},{2,0},{4,6},{6,4},{8,10},{10,8},{12,14},{14,12},{16,18},{18,... | collective-permute-start | bytes 1449992 | tf_op jit(solution)/shard_map/send_7/ppermute | solution.py:361
  36.4 12.1 %collective-permute-start.8 = (bf16[8,30208]{1,0:T(8,128)(2,1)S(1)}, bf16[8,30208]{1,0:T(8,128)(2,1)S(1)}, u32[]{:S(2)}, u32[]{:S(2)}) collective-permute-start(bf16[8,30208]{1,0:T(8,128)(2,1)S(1)} %collective-permute-done.4.refs_5_), channel_id=1, source_target_pairs={{0,4},{2,6},{4,0},{6,2},{8,12},{10,14},{12,8},{14,10},{16,20},{18,... | collective-permute-start | bytes 1449992 | tf_op jit(solution)/shard_map/send_8/ppermute | solution.py:361
  46.2 11.3 %collective-permute-start.10 = (bf16[8,30208]{1,0:T(8,128)(2,1)S(1)}, bf16[8,30208]{1,0:T(8,128)(2,1)S(1)}, u32[]{:S(2)}, u32[]{:S(2)}) collective-permute-start(bf16[8,30208]{1,0:T(8,128)(2,1)S(1)} %collective-permute-done.5.refs_6_), channel_id=1, source_target_pairs={{0,24},{2,26},{4,28},{6,30},{8,0},{10,2},{12,4},{14,6},{16,8},{18,... | collective-permute-start | bytes 1449992 | tf_op jit(solution)/shard_map/send_11/ppermute | solution.py:361
  47.5 11.3 %collective-permute-start.13 = (bf16[8,30208]{1,0:T(8,128)(2,1)S(1)}, bf16[8,30208]{1,0:T(8,128)(2,1)S(1)}, u32[]{:S(2)}, u32[]{:S(2)}) collective-permute-start(bf16[8,30208]{1,0:T(8,128)(2,1)S(1)} %collective-permute-done.6.refs_7_), channel_id=1, source_target_pairs={{0,2},{2,0},{4,6},{6,4},{8,10},{10,8},{12,14},{14,12},{16,18},{18,... | collective-permute-start | bytes 1449992 | tf_op jit(solution)/shard_map/send_12/ppermute | solution.py:361
  48.5 11.2 %collective-permute-start.14 = (bf16[8,30208]{1,0:T(8,128)(2,1)S(1)}, bf16[8,30208]{1,0:T(8,128)(2,1)S(1)}, u32[]{:S(2)}, u32[]{:S(2)}) collective-permute-start(bf16[8,30208]{1,0:T(8,128)(2,1)S(1)} %collective-permute-done.7.refs_8_), channel_id=1, source_target_pairs={{0,4},{2,6},{4,0},{6,2},{8,12},{10,14},{12,8},{14,10},{16,20},{18,... | collective-permute-start | bytes 1449992 | tf_op jit(solution)/shard_map/send_13/ppermute | solution.py:361
  50.1 3.2 %copy-start = (bf16[128,30208]{1,0:T(8,128)(2,1)S(1)}, bf16[128,30208]{1,0:T(8,128)(2,1)}, u32[]{:S(2)}) copy-start(bf16[128,30208]{1,0:T(8,128)(2,1)} %ptdf_ref.3) | copy-start | bytes 23199748
  53.3 1.0 copy-start.2
  54.3 8.2 %copy-start.1 = (bf16[128,30208]{1,0:T(8,128)(2,1)S(1)}, bf16[128,30208]{1,0:T(8,128)(2,1)}, u32[]{:S(2)}) copy-start(bf16[128,30208]{1,0:T(8,128)(2,1)} %ptdf_ref.3) | copy-start | bytes 23199748
  57.5 8.8 %collective-permute-start.11 = (bf16[8,30208]{1,0:T(8,128)(2,1)S(1)}, bf16[8,30208]{1,0:T(8,128)(2,1)S(1)}, u32[]{:S(2)}, u32[]{:S(2)}) collective-permute-start(bf16[8,30208]{1,0:T(8,128)(2,1)S(1)} %collective-permute-done.2.refs_3_), channel_id=1, source_target_pairs={{0,24},{2,26},{4,28},{6,30},{8,0},{10,2},{12,4},{14,6},{16,8},{18,... | collective-permute-start | bytes 1449992 | tf_op jit(solution)/shard_map/send_14/ppermute | solution.py:361
  58.8 10.5 %collective-permute-start.15 = (bf16[8,30208]{1,0:T(8,128)(2,1)S(1)}, bf16[8,30208]{1,0:T(8,128)(2,1)S(1)}, u32[]{:S(2)}, u32[]{:S(2)}) collective-permute-start(bf16[8,30208]{1,0:T(8,128)(2,1)S(1)} %collective-permute-done.8.refs_9_), channel_id=1, source_target_pairs={{0,2},{2,0},{4,6},{6,4},{8,10},{10,8},{12,14},{14,12},{16,18},{18,... | collective-permute-start | bytes 1449992 | tf_op jit(solution)/shard_map/send_15/ppermute | solution.py:361
  59.8 10.9 %collective-permute-start.16 = (bf16[8,30208]{1,0:T(8,128)(2,1)S(1)}, bf16[8,30208]{1,0:T(8,128)(2,1)S(1)}, u32[]{:S(2)}, u32[]{:S(2)}) collective-permute-start(bf16[8,30208]{1,0:T(8,128)(2,1)S(1)} %collective-permute-done.3.refs_4_), channel_id=1, source_target_pairs={{0,4},{2,6},{4,0},{6,2},{8,12},{10,14},{12,8},{14,10},{16,20},{18,... | collective-permute-start | bytes 1449992 | tf_op jit(solution)/shard_map/send_16/ppermute | solution.py:361
  61.3 1.2 collective-permute-start.9
  66.3 12.3 %collective-permute-start.12 = (bf16[8,30208]{1,0:T(8,128)(2,1)S(1)}, bf16[8,30208]{1,0:T(8,128)(2,1)S(1)}, u32[]{:S(2)}, u32[]{:S(2)}) collective-permute-start(bf16[8,30208]{1,0:T(8,128)(2,1)S(1)} %get-tuple-element.57), channel_id=1, source_target_pairs={{0,24},{2,26},{4,28},{6,30},{8,0},{10,2},{12,4},{14,6},{16,8},{18,... | collective-permute-start | bytes 1449992 | tf_op jit(solution)/shard_map/send_21/ppermute | solution.py:361
  69.3 10.5 %collective-permute-start.18 = (bf16[8,30208]{1,0:T(8,128)(2,1)S(1)}, bf16[8,30208]{1,0:T(8,128)(2,1)S(1)}, u32[]{:S(2)}, u32[]{:S(2)}) collective-permute-start(bf16[8,30208]{1,0:T(8,128)(2,1)S(1)} %get-tuple-element.65), channel_id=1, source_target_pairs={{0,2},{2,0},{4,6},{6,4},{8,10},{10,8},{12,14},{14,12},{16,18},{18,... | collective-permute-start | bytes 1449992 | tf_op jit(solution)/shard_map/send_20/ppermute | solution.py:361
  70.7 10.5 %collective-permute-start.22 = (bf16[8,30208]{1,0:T(8,128)(2,1)S(1)}, bf16[8,30208]{1,0:T(8,128)(2,1)S(1)}, u32[]{:S(2)}, u32[]{:S(2)}) collective-permute-start(bf16[8,30208]{1,0:T(8,128)(2,1)S(1)} %get-tuple-element.75), channel_id=1, source_target_pairs={{0,4},{2,6},{4,0},{6,2},{8,12},{10,14},{12,8},{14,10},{16,20},{18,... | collective-permute-start | bytes 1449992 | tf_op jit(solution)/shard_map/send_19/ppermute | solution.py:361
  75.8 1.3 collective-permute-start.17
  78.7 13.2 %collective-permute-start.19 = (bf16[8,30208]{1,0:T(8,128)(2,1)S(1)}, bf16[8,30208]{1,0:T(8,128)(2,1)S(1)}, u32[]{:S(2)}, u32[]{:S(2)}) collective-permute-start(bf16[8,30208]{1,0:T(8,128)(2,1)S(1)} %get-tuple-element.67), channel_id=1, source_target_pairs={{0,24},{2,26},{4,28},{6,30},{8,0},{10,2},{12,4},{14,6},{16,8},{18,... | collective-permute-start | bytes 1449992 | tf_op jit(solution)/shard_map/send_24/ppermute | solution.py:361
  79.9 14.2 %collective-permute-start.21 = (bf16[8,30208]{1,0:T(8,128)(2,1)S(1)}, bf16[8,30208]{1,0:T(8,128)(2,1)S(1)}, u32[]{:S(2)}, u32[]{:S(2)}) collective-permute-start(bf16[8,30208]{1,0:T(8,128)(2,1)S(1)} %get-tuple-element.71), channel_id=1, source_target_pairs={{0,2},{2,0},{4,6},{6,4},{8,10},{10,8},{12,14},{14,12},{16,18},{18,... | collective-permute-start | bytes 1449992 | tf_op jit(solution)/shard_map/send_23/ppermute | solution.py:361
  81.2 12.7 %collective-permute-start.23 = (bf16[8,30208]{1,0:T(8,128)(2,1)S(1)}, bf16[8,30208]{1,0:T(8,128)(2,1)S(1)}, u32[]{:S(2)}, u32[]{:S(2)}) collective-permute-start(bf16[8,30208]{1,0:T(8,128)(2,1)S(1)} %get-tuple-element.76), channel_id=1, source_target_pairs={{0,4},{2,6},{4,0},{6,2},{8,12},{10,14},{12,8},{14,10},{16,20},{18,... | collective-permute-start | bytes 1449992 | tf_op jit(solution)/shard_map/send_22/ppermute | solution.py:361
  83.2 45.0 %copy-start.3 = (s32[1024]{0:T(1024)S(1)}, s32[1024]{0:T(1024)}, u32[]{:S(2)}) copy-start(s32[1024]{0:T(1024)} %param.10) | copy-start | bytes 12292
  91.8 14.1 %collective-permute-start.20 = (bf16[8,30208]{1,0:T(8,128)(2,1)S(1)}, bf16[8,30208]{1,0:T(8,128)(2,1)S(1)}, u32[]{:S(2)}, u32[]{:S(2)}) collective-permute-start(bf16[8,30208]{1,0:T(8,128)(2,1)S(1)} %add_convert_fusion.6), channel_id=1, source_target_pairs={{0,24},{2,26},{4,28},{6,30},{8,0},{10,2},{12,4},{14,6},{16,8},{18,... | collective-permute-start | bytes 1449992 | tf_op jit(solution)/shard_map/send_27/ppermute | solution.py:361
  93.9 11.2 %collective-permute-start.24 = (bf16[8,30208]{1,0:T(8,128)(2,1)S(1)}, bf16[8,30208]{1,0:T(8,128)(2,1)S(1)}, u32[]{:S(2)}, u32[]{:S(2)}) collective-permute-start(bf16[8,30208]{1,0:T(8,128)(2,1)S(1)} %get-tuple-element.77), channel_id=1, source_target_pairs={{0,4},{2,6},{4,0},{6,2},{8,12},{10,14},{12,8},{14,10},{16,20},{18,... | collective-permute-start | bytes 1449992 | tf_op jit(solution)/shard_map/send_25/ppermute | solution.py:361
  94.1 36.7 %copy-start.4 = (f32[1024]{0:T(1024)S(1)}, f32[1024]{0:T(1024)}, u32[]{:S(2)}) copy-start(f32[1024]{0:T(1024)} %param.11) | copy-start | bytes 12292
  94.1 11.2 %collective-permute-start.27 = (bf16[8,30208]{1,0:T(8,128)(2,1)S(1)}, bf16[8,30208]{1,0:T(8,128)(2,1)S(1)}, u32[]{:S(2)}, u32[]{:S(2)}) collective-permute-start(bf16[8,30208]{1,0:T(8,128)(2,1)S(1)} %add_convert_fusion.2), channel_id=1, source_target_pairs={{0,2},{2,0},{4,6},{6,4},{8,10},{10,8},{12,14},{14,12},{16,18},{18,... | collective-permute-start | bytes 1449992 | tf_op jit(solution)/shard_map/send_26/ppermute | solution.py:361
  105.1 11.2 %collective-permute-start.25 = (bf16[8,30208]{1,0:T(8,128)(2,1)S(1)}, bf16[8,30208]{1,0:T(8,128)(2,1)S(1)}, u32[]{:S(2)}, u32[]{:S(2)}) collective-permute-start(bf16[8,30208]{1,0:T(8,128)(2,1)S(1)} %add_convert_fusion.4), channel_id=1, source_target_pairs={{0,4},{2,6},{4,0},{6,2},{8,12},{10,14},{12,8},{14,10},{16,20},{18,... | collective-permute-start | bytes 1449992 | tf_op jit(solution)/shard_map/send_28/ppermute | solution.py:361
  105.3 11.2 %collective-permute-start.28 = (bf16[8,30208]{1,0:T(8,128)(2,1)S(1)}, bf16[8,30208]{1,0:T(8,128)(2,1)S(1)}, u32[]{:S(2)}, u32[]{:S(2)}) collective-permute-start(bf16[8,30208]{1,0:T(8,128)(2,1)S(1)} %get-tuple-element.84), channel_id=1, source_target_pairs={{0,2},{2,0},{4,6},{6,4},{8,10},{10,8},{12,14},{14,12},{16,18},{18,... | collective-permute-start | bytes 1449992 | tf_op jit(solution)/shard_map/send_29/ppermute | solution.py:361
  105.9 11.3 %collective-permute-start.30 = (bf16[8,30208]{1,0:T(8,128)(2,1)S(1)}, bf16[8,30208]{1,0:T(8,128)(2,1)S(1)}, u32[]{:S(2)}, u32[]{:S(2)}) collective-permute-start(bf16[8,30208]{1,0:T(8,128)(2,1)S(1)} %add_convert_fusion.1), channel_id=1, source_target_pairs={{0,8},{2,10},{4,12},{6,14},{8,16},{10,18},{12,20},{14,22},{16,24},... | collective-permute-start | bytes 1449992 | tf_op jit(solution)/shard_map/send_30/ppermute | solution.py:361
  116.3 9.3 %collective-permute-start.26 = (bf16[8,30208]{1,0:T(8,128)(2,1)S(1)}, bf16[8,30208]{1,0:T(8,128)(2,1)S(1)}, u32[]{:S(2)}, u32[]{:S(2)}) collective-permute-start(bf16[8,30208]{1,0:T(8,128)(2,1)S(1)} %add_convert_fusion.5), channel_id=1, source_target_pairs={{0,4},{2,6},{4,0},{6,2},{8,12},{10,14},{12,8},{14,10},{16,20},{18,... | collective-permute-start | bytes 1449992 | tf_op jit(solution)/shard_map/send_31/ppermute | solution.py:361
  116.5 9.4 %collective-permute-start.29 = (bf16[8,30208]{1,0:T(8,128)(2,1)S(1)}, bf16[8,30208]{1,0:T(8,128)(2,1)S(1)}, u32[]{:S(2)}, u32[]{:S(2)}) collective-permute-start(bf16[8,30208]{1,0:T(8,128)(2,1)S(1)} %add_convert_fusion.3), channel_id=1, source_target_pairs={{0,2},{2,0},{4,6},{6,4},{8,10},{10,8},{12,14},{14,12},{16,18},{18,... | collective-permute-start | bytes 1449992 | tf_op jit(solution)/shard_map/send_32/ppermute | solution.py:361
  117.5 10.6 %collective-permute-start.31 = (bf16[8,30208]{1,0:T(8,128)(2,1)S(1)}, bf16[8,30208]{1,0:T(8,128)(2,1)S(1)}, u32[]{:S(2)}, u32[]{:S(2)}) collective-permute-start(bf16[8,30208]{1,0:T(8,128)(2,1)S(1)} %add_convert_fusion), channel_id=1, source_target_pairs={{0,8},{2,10},{4,12},{6,14},{8,16},{10,18},{12,20},{14,22},{16,24},... | collective-permute-start | bytes 1449992 | tf_op jit(solution)/shard_map/send_33/ppermute | solution.py:361
  129.5 1.3 collective-permute-start.32

commit v6 on v5

--- a/solution.py
+++ b/solution.py
@@ -205,16 +205,16 @@
 
 def flows_kernel(tile, *refs):
     *blocks, ptdf_ref, out_ref = refs
-    total = jnp.zeros(out_ref.shape, jnp.float32)
+    total = jnp.zeros(out_ref.shape[::-1], jnp.float32)
 
     def add(i, total):
         at = pl.ds(pl.multiple_of(i * tile, 128), tile)
         rows = jnp.concatenate([block[:, at].astype(jnp.float32) for block in blocks], axis=0)
         return total + lax.dot_general(
-            rows.astype(jnp.bfloat16), ptdf_ref[:, at], (((1,), (1,)), ((), ())), preferred_element_type=jnp.float32
+            ptdf_ref[:, at], rows.astype(jnp.bfloat16), (((1,), (1,)), ((), ())), preferred_element_type=jnp.float32
         )
 
-    out_ref[...] = lax.fori_loop(0, ptdf_ref.shape[1] // tile, add, total)
+    out_ref[...] = lax.fori_loop(0, ptdf_ref.shape[1] // tile, add, total).T
 
 
 def flows_of(blocks, ptdf):

time: 132 us -> 131 us (level)
  transfers between devices with their start and end apart: 33 -> 33, of which waited for: 14 -> 16; matrix products, arithmetic and copies ran while one was open for 1% -> 1% of each run, Pallas kernels for 8% -> 7%
where the time goes in v6:
time: 131 us
  waiting for transfers between devices  72.1 us (55%)
  starting transfers between devices  38.6 us (29%)
  Pallas kernels  13.4 us (10%)
  local copies, waits for them, and re-layouts  4.25 us (3%)
  other arithmetic  1.63 us (1%)
    ppermute x30, waiting for transfers between devices, shards(): came = lax.ppermute(after(block, waits), 'br', pairs)  68.6 us
    ppermute x30, starting transfers between devices, shards(): came = lax.ppermute(after(block, waits), 'br', pairs)  38.5 us
    pallas_call x2, Pallas kernels, flows_of(): pl.pallas_call(functools.partial(flows_kernel, tile_of(width, 128)), in_s...  5.35 us
    unnamed x16, local copies, waits for them, and re-layouts  4.25 us
    pallas_call x2, Pallas kernels, grads_of(): pl.pallas_call(functools.partial(grads_kernel, tile_of(width, 128)), in_s...  3.56 us
    ppermute x3, waiting for transfers between devices, over_bus(): return (value, lax.ppermute(value, 'bus', [(0, 1), (1, 0)]))  3.49 us
    pallas_call x1, Pallas kernels, inject_of(): pl.pallas_call(inject_kernel, grid=(width // tile,), in_specs=[pl.BlockSp...  3.14 us
  transfers between devices with their start and end apart: 33, of which 16 were waited for; matrix products, arithmetic and copies ran while one was open for 1% of the time, Pallas kernels for 7%

profile of v6, /device:TPU:0, one launch (start us, length us, event | category | flops | bytes accessed | tf_op | source)
XLA Modules:
  0.0 130.8 jit_solution(10907494907381932867)
XLA Ops:
  0.7 3.1 %inject.1.refs_0_ = bf16[8,30208]{1,0:T(8,128)(2,1)} custom-call(s32[1]{0:T(128)} %bitcast.bus_ref, f32[8,1024]{1,0:T(8,128)} %release_ref.1, f32[1,1024]{1,0:T(1,128)} %bitcast.11, s32[1,1024]{1,0:T(1,128)} %bitcast.5, bf16[8,30208]{1,0:T(8,128)(2,1)} %net_ref.1), custom_call_target="tpu_custom_call" | custom-call | tf_op jit(solution)/shard_map/inject/pallas_call | solution.py:184
  3.8 3.0 %collective-permute-start = (bf16[8,30208]{1,0:T(8,128)(2,1)}, bf16[8,30208]{1,0:T(8,128)(2,1)S(1)}, u32[]{:S(2)}, u32[]{:S(2)}) collective-permute-start(bf16[8,30208]{1,0:T(8,128)(2,1)} %inject.1.refs_0_), channel_id=1, source_target_pairs={{0,8},{2,10},{4,12},{6,14},{8,16},{10,18},{12,20},{14,22},{16,24},... | collective-permute-start | bytes 1449992 | tf_op jit(solution)/shard_map/send_0/ppermute | solution.py:361
  6.8 1.5 %collective-permute-start.1 = (bf16[8,30208]{1,0:T(8,128)(2,1)}, bf16[8,30208]{1,0:T(8,128)(2,1)S(1)}, u32[]{:S(2)}, u32[]{:S(2)}) collective-permute-start(bf16[8,30208]{1,0:T(8,128)(2,1)} %inject.1.refs_0_), channel_id=1, source_target_pairs={{0,2},{2,0},{4,6},{6,4},{8,10},{10,8},{12,14},{14,12},{16,18},{18,... | collective-permute-start | bytes 1449992 | tf_op jit(solution)/shard_map/send_1/ppermute | solution.py:361
  8.3 1.5 %collective-permute-start.2 = (bf16[8,30208]{1,0:T(8,128)(2,1)}, bf16[8,30208]{1,0:T(8,128)(2,1)S(1)}, u32[]{:S(2)}, u32[]{:S(2)}) collective-permute-start(bf16[8,30208]{1,0:T(8,128)(2,1)} %inject.1.refs_0_), channel_id=1, source_target_pairs={{0,4},{2,6},{4,0},{6,2},{8,12},{10,14},{12,8},{14,10},{16,20},{18,... | collective-permute-start | bytes 1449992 | tf_op jit(solution)/shard_map/send_2/ppermute | solution.py:361
  9.8 10.3 %collective-permute-done.refs_1_ = bf16[8,30208]{1,0:T(8,128)(2,1)S(1)} collective-permute-done((bf16[8,30208]{1,0:T(8,128)(2,1)}, bf16[8,30208]{1,0:T(8,128)(2,1)S(1)}, u32[]{:S(2)}, u32[]{:S(2)}) %collective-permute-start) | collective-permute-done | bytes 483360 | tf_op jit(solution)/shard_map/send_0/ppermute | solution.py:361
  20.1 1.5 %collective-permute-start.4 = (bf16[8,30208]{1,0:T(8,128)(2,1)S(1)}, bf16[8,30208]{1,0:T(8,128)(2,1)S(1)}, u32[]{:S(2)}, u32[]{:S(2)}) collective-permute-start(bf16[8,30208]{1,0:T(8,128)(2,1)S(1)} %collective-permute-done.refs_1_), channel_id=1, source_target_pairs={{0,2},{2,0},{4,6},{6,4},{8,10},{10,8},{12,14},{14,12},{16,18},{18,... | collective-permute-start | bytes 1449992 | tf_op jit(solution)/shard_map/send_4/ppermute | solution.py:361
  21.6 1.5 %collective-permute-start.5 = (bf16[8,30208]{1,0:T(8,128)(2,1)S(1)}, bf16[8,30208]{1,0:T(8,128)(2,1)S(1)}, u32[]{:S(2)}, u32[]{:S(2)}) collective-permute-start(bf16[8,30208]{1,0:T(8,128)(2,1)S(1)} %collective-permute-done.1.refs_2_), channel_id=1, source_target_pairs={{0,4},{2,6},{4,0},{6,2},{8,12},{10,14},{12,8},{14,10},{16,20},{18,... | collective-permute-start | bytes 1449992 | tf_op jit(solution)/shard_map/send_5/ppermute | solution.py:361
  23.1 12.2 %collective-permute-done.3.refs_4_ = bf16[8,30208]{1,0:T(8,128)(2,1)S(1)} collective-permute-done((bf16[8,30208]{1,0:T(8,128)(2,1)S(1)}, bf16[8,30208]{1,0:T(8,128)(2,1)S(1)}, u32[]{:S(2)}, u32[]{:S(2)}) %collective-permute-start.3) | collective-permute-done | bytes 483360 | tf_op jit(solution)/shard_map/send_3/ppermute | solution.py:361
  35.3 1.1 collective-permute-start.7
  36.4 1.5 %collective-permute-start.8 = (bf16[8,30208]{1,0:T(8,128)(2,1)S(1)}, bf16[8,30208]{1,0:T(8,128)(2,1)S(1)}, u32[]{:S(2)}, u32[]{:S(2)}) collective-permute-start(bf16[8,30208]{1,0:T(8,128)(2,1)S(1)} %collective-permute-done.4.refs_5_), channel_id=1, source_target_pairs={{0,4},{2,6},{4,0},{6,2},{8,12},{10,14},{12,8},{14,10},{16,20},{18,... | collective-permute-start | bytes 1449992 | tf_op jit(solution)/shard_map/send_8/ppermute | solution.py:361
  37.9 8.3 %collective-permute-done.6.refs_7_ = bf16[8,30208]{1,0:T(8,128)(2,1)S(1)} collective-permute-done((bf16[8,30208]{1,0:T(8,128)(2,1)S(1)}, bf16[8,30208]{1,0:T(8,128)(2,1)S(1)}, u32[]{:S(2)}, u32[]{:S(2)}) %collective-permute-start.6) | collective-permute-done | bytes 483360 | tf_op jit(solution)/shard_map/send_6/ppermute | solution.py:361
  46.2 1.3 collective-permute-start.10
  47.5 1.0 collective-permute-start.13
  48.5 1.5 %collective-permute-start.14 = (bf16[8,30208]{1,0:T(8,128)(2,1)S(1)}, bf16[8,30208]{1,0:T(8,128)(2,1)S(1)}, u32[]{:S(2)}, u32[]{:S(2)}) collective-permute-start(bf16[8,30208]{1,0:T(8,128)(2,1)S(1)} %collective-permute-done.7.refs_8_), channel_id=1, source_target_pairs={{0,4},{2,6},{4,0},{6,2},{8,12},{10,14},{12,8},{14,10},{16,20},{18,... | collective-permute-start | bytes 1449992 | tf_op jit(solution)/shard_map/send_13/ppermute | solution.py:361
  50.1 3.2 %copy-done = bf16[128,30208]{1,0:T(8,128)(2,1)S(1)} copy-done((bf16[128,30208]{1,0:T(8,128)(2,1)S(1)}, bf16[128,30208]{1,0:T(8,128)(2,1)}, u32[]{:S(2)}) %copy-start) | copy-done | bytes 7733272
  53.3 1.0 copy-done.2
  54.3 2.7 %flows.2.mine_ref = f32[80,128]{1,0:T(8,128)S(1)} custom-call(bf16[8,30208]{1,0:T(8,128)(2,1)S(1)} %copy-done.2, bf16[8,30208]{1,0:T(8,128)(2,1)S(1)} %collective-permute-done.refs_1_, bf16[8,30208]{1,0:T(8,128)(2,1)S(1)} %collective-permute-done.1.refs_2_, bf16[8,30208]{1,0:T(8,128)(2,1)S(1)} %collective-permute-done.2.refs_3_, ...), custom_call_target="tpu_custom_call" | custom-call | tf_op jit(solution)/shard_map/flows/pallas_call | solution.py:228
  57.0 1.8 %collective-permute-start.11 = (bf16[8,30208]{1,0:T(8,128)(2,1)S(1)}, bf16[8,30208]{1,0:T(8,128)(2,1)S(1)}, u32[]{:S(2)}, u32[]{:S(2)}) collective-permute-start(bf16[8,30208]{1,0:T(8,128)(2,1)S(1)} %collective-permute-done.2.refs_3_), channel_id=1, source_target_pairs={{0,24},{2,26},{4,28},{6,30},{8,0},{10,2},{12,4},{14,6},{16,8},{18,... | collective-permute-start | bytes 1449992 | tf_op jit(solution)/shard_map/send_14/ppermute | solution.py:361
  58.8 0.9 collective-permute-start.15
  59.8 1.5 %collective-permute-start.16 = (bf16[8,30208]{1,0:T(8,128)(2,1)S(1)}, bf16[8,30208]{1,0:T(8,128)(2,1)S(1)}, u32[]{:S(2)}, u32[]{:S(2)}) collective-permute-start(bf16[8,30208]{1,0:T(8,128)(2,1)S(1)} %collective-permute-done.3.refs_4_), channel_id=1, source_target_pairs={{0,4},{2,6},{4,0},{6,2},{8,12},{10,14},{12,8},{14,10},{16,20},{18,... | collective-permute-start | bytes 1449992 | tf_op jit(solution)/shard_map/send_16/ppermute | solution.py:361
  61.3 0.1 select_reduce_fusion
  61.4 1.1 collective-permute-done.9.other_ref
  62.5 1.9 %grads.2 = (f32[8,30208]{1,0:T(8,128)S(1)}, bf16[8,30208]{1,0:T(8,128)(2,1)S(1)}, f32[8,30208]{1,0:T(8,128)S(1)}, f32[8,30208]{1,0:T(8,128)S(1)}, f32[8,30208]{1...) custom-call(f32[80,128]{1,0:T(8,128)S(1)} %flows.2.mine_ref, ...), custom_call_target="tpu_custom_call" | custom-call | tf_op jit(solution)/shard_map/grads/pallas_call | solution.py:262
  64.4 1.8 %collective-permute-done.11.refs_3_ = bf16[8,30208]{1,0:T(8,128)(2,1)S(1)} collective-permute-done((bf16[8,30208]{1,0:T(8,128)(2,1)S(1)}, bf16[8,30208]{1,0:T(8,128)(2,1)S(1)}, u32[]{:S(2)}, u32[]{:S(2)}) %collective-permute-start.11) | collective-permute-done | bytes 483360 | tf_op jit(solution)/shard_map/send_14/ppermute | solution.py:361
  66.3 3.1 %collective-permute-start.12 = (bf16[8,30208]{1,0:T(8,128)(2,1)S(1)}, bf16[8,30208]{1,0:T(8,128)(2,1)S(1)}, u32[]{:S(2)}, u32[]{:S(2)}) collective-permute-start(bf16[8,30208]{1,0:T(8,128)(2,1)S(1)} %get-tuple-element.57), channel_id=1, source_target_pairs={{0,24},{2,26},{4,28},{6,30},{8,0},{10,2},{12,4},{14,6},{16,8},{18,... | collective-permute-start | bytes 1449992 | tf_op jit(solution)/shard_map/send_21/ppermute | solution.py:361
  69.3 1.3 %collective-permute-start.18 = (bf16[8,30208]{1,0:T(8,128)(2,1)S(1)}, bf16[8,30208]{1,0:T(8,128)(2,1)S(1)}, u32[]{:S(2)}, u32[]{:S(2)}) collective-permute-start(bf16[8,30208]{1,0:T(8,128)(2,1)S(1)} %get-tuple-element.65), channel_id=1, source_target_pairs={{0,2},{2,0},{4,6},{6,4},{8,10},{10,8},{12,14},{14,12},{16,18},{18,... | collective-permute-start | bytes 1449992 | tf_op jit(solution)/shard_map/send_20/ppermute | solution.py:361
  70.7 2.0 %collective-permute-start.22 = (bf16[8,30208]{1,0:T(8,128)(2,1)S(1)}, bf16[8,30208]{1,0:T(8,128)(2,1)S(1)}, u32[]{:S(2)}, u32[]{:S(2)}) collective-permute-start(bf16[8,30208]{1,0:T(8,128)(2,1)S(1)} %get-tuple-element.75), channel_id=1, source_target_pairs={{0,4},{2,6},{4,0},{6,2},{8,12},{10,14},{12,8},{14,10},{16,20},{18,... | collective-permute-start | bytes 1449992 | tf_op jit(solution)/shard_map/send_19/ppermute | solution.py:361
  72.6 2.6 %flows.3.mine_ref = f32[48,128]{1,0:T(8,128)S(1)} custom-call(bf16[8,30208]{1,0:T(8,128)(2,1)S(1)} %collective-permute-done.10.refs_0_, bf16[8,30208]{1,0:T(8,128)(2,1)S(1)} %collective-permute-done.13.refs_1_, bf16[8,30208]{1,0:T(8,128)(2,1)S(1)} %collective-permute-done.14.refs_2_, bf16[8,30208]{1,0:T(8,128)(2,1)S(1)} %collective-permute-done.11.refs_3_, ...), custom_call_target="tpu_custom_call" | custom-call | tf_op jit(solution)/shard_map/flows/pallas_call | solution.py:228
  75.3 0.0 collective-permute-start.17
  75.3 1.2 collective-permute-done.17.other_ref
  76.5 1.6 %grads.3 = (bf16[8,30208]{1,0:T(8,128)(2,1)S(1)}, f32[8,30208]{1,0:T(8,128)S(1)}, bf16[8,30208]{1,0:T(8,128)(2,1)S(1)}, f32[8,30208]{1,0:T(8,128)S(1)}, f32[8,30...) custom-call(f32[48,128]{1,0:T(8,128)S(1)} %flows.3.mine_ref, f32[48,128]{1,0:T(8,128)S(1)} %collective-permute-done.17.other_ref, ...), custom_call_target="tpu_custom_call" | custom-call | tf_op jit(solution)/shard_map/grads/pallas_call | solution.py:262
  78.1 1.7 %collective-permute-start.19 = (bf16[8,30208]{1,0:T(8,128)(2,1)S(1)}, bf16[8,30208]{1,0:T(8,128)(2,1)S(1)}, u32[]{:S(2)}, u32[]{:S(2)}) collective-permute-start(bf16[8,30208]{1,0:T(8,128)(2,1)S(1)} %get-tuple-element.67), channel_id=1, source_target_pairs={{0,24},{2,26},{4,28},{6,30},{8,0},{10,2},{12,4},{14,6},{16,8},{18,... | collective-permute-start | bytes 1449992 | tf_op jit(solution)/shard_map/send_24/ppermute | solution.py:361
  79.9 1.3 %collective-permute-start.21 = (bf16[8,30208]{1,0:T(8,128)(2,1)S(1)}, bf16[8,30208]{1,0:T(8,128)(2,1)S(1)}, u32[]{:S(2)}, u32[]{:S(2)}) collective-permute-start(bf16[8,30208]{1,0:T(8,128)(2,1)S(1)} %get-tuple-element.71), channel_id=1, source_target_pairs={{0,2},{2,0},{4,6},{6,4},{8,10},{10,8},{12,14},{14,12},{16,18},{18,... | collective-permute-start | bytes 1449992 | tf_op jit(solution)/shard_map/send_23/ppermute | solution.py:361
  81.2 2.0 %collective-permute-start.23 = (bf16[8,30208]{1,0:T(8,128)(2,1)S(1)}, bf16[8,30208]{1,0:T(8,128)(2,1)S(1)}, u32[]{:S(2)}, u32[]{:S(2)}) collective-permute-start(bf16[8,30208]{1,0:T(8,128)(2,1)S(1)} %get-tuple-element.76), channel_id=1, source_target_pairs={{0,4},{2,6},{4,0},{6,2},{8,12},{10,14},{12,8},{14,10},{16,20},{18,... | collective-permute-start | bytes 1449992 | tf_op jit(solution)/shard_map/send_22/ppermute | solution.py:361
  83.2 0.1 add_convert_fusion.6
  83.3 8.0 %collective-permute-done.19 = bf16[8,30208]{1,0:T(8,128)(2,1)S(1)} collective-permute-done((bf16[8,30208]{1,0:T(8,128)(2,1)S(1)}, bf16[8,30208]{1,0:T(8,128)(2,1)S(1)}, u32[]{:S(2)}, u32[]{:S(2)}) %collective-permute-start.19) | collective-permute-done | bytes 483360 | tf_op jit(solution)/shard_map/send_24/ppermute | solution.py:361
  91.3 2.1 %collective-permute-start.20 = (bf16[8,30208]{1,0:T(8,128)(2,1)S(1)}, bf16[8,30208]{1,0:T(8,128)(2,1)S(1)}, u32[]{:S(2)}, u32[]{:S(2)}) collective-permute-start(bf16[8,30208]{1,0:T(8,128)(2,1)S(1)} %add_convert_fusion.6), channel_id=1, source_target_pairs={{0,24},{2,26},{4,28},{6,30},{8,0},{10,2},{12,4},{14,6},{16,8},{18,... | collective-permute-start | bytes 1449992 | tf_op jit(solution)/shard_map/send_27/ppermute | solution.py:361
  93.4 0.1 collective-permute-start.24
  93.5 0.1 add_convert_fusion.2
  93.5 0.0 copy-start.4
  93.6 0.8 collective-permute-start.27
  94.3 0.2 add_convert_fusion.3
  94.5 0.1 add_convert_fusion.4
  94.6 10.0 %collective-permute-done.24 = bf16[8,30208]{1,0:T(8,128)(2,1)S(1)} collective-permute-done((bf16[8,30208]{1,0:T(8,128)(2,1)S(1)}, bf16[8,30208]{1,0:T(8,128)(2,1)S(1)}, u32[]{:S(2)}, u32[]{:S(2)}) %collective-permute-start.24) | collective-permute-done | bytes 483360 | tf_op jit(solution)/shard_map/send_25/ppermute | solution.py:361
  104.6 0.1 collective-permute-start.25
  104.7 0.1 collective-permute-done.27
  104.7 0.6 collective-permute-start.28
  105.3 0.2 add_convert_fusion.1
  105.5 1.7 %collective-permute-start.30 = (bf16[8,30208]{1,0:T(8,128)(2,1)S(1)}, bf16[8,30208]{1,0:T(8,128)(2,1)S(1)}, u32[]{:S(2)}, u32[]{:S(2)}) collective-permute-start(bf16[8,30208]{1,0:T(8,128)(2,1)S(1)} %add_convert_fusion.1), channel_id=1, source_target_pairs={{0,8},{2,10},{4,12},{6,14},{8,16},{10,18},{12,20},{14,22},{16,24},... | collective-permute-start | bytes 1449992 | tf_op jit(solution)/shard_map/send_30/ppermute | solution.py:361
  107.2 0.1 add_convert_fusion.5
  107.3 8.5 %collective-permute-done.25 = bf16[8,30208]{1,0:T(8,128)(2,1)S(1)} collective-permute-done((bf16[8,30208]{1,0:T(8,128)(2,1)S(1)}, bf16[8,30208]{1,0:T(8,128)(2,1)S(1)}, u32[]{:S(2)}, u32[]{:S(2)}) %collective-permute-start.25) | collective-permute-done | bytes 483360 | tf_op jit(solution)/shard_map/send_28/ppermute | solution.py:361
  115.8 0.1 collective-permute-start.26
  115.9 0.1 collective-permute-done.28
  115.9 0.6 collective-permute-start.29
  116.5 0.2 collective-permute-done.30
  116.7 0.2 add_convert_fusion
  117.0 1.5 %collective-permute-start.31 = (bf16[8,30208]{1,0:T(8,128)(2,1)S(1)}, bf16[8,30208]{1,0:T(8,128)(2,1)S(1)}, u32[]{:S(2)}, u32[]{:S(2)}) collective-permute-start(bf16[8,30208]{1,0:T(8,128)(2,1)S(1)} %add_convert_fusion), channel_id=1, source_target_pairs={{0,8},{2,10},{4,12},{6,14},{8,16},{10,18},{12,20},{14,22},{16,24},... | collective-permute-start | bytes 1449992 | tf_op jit(solution)/shard_map/send_33/ppermute | solution.py:361
  118.5 6.1 %collective-permute-done.26.refs_2_ = bf16[8,30208]{1,0:T(8,128)(2,1)S(1)} collective-permute-done((bf16[8,30208]{1,0:T(8,128)(2,1)S(1)}, bf16[8,30208]{1,0:T(8,128)(2,1)S(1)}, u32[]{:S(2)}, u32[]{:S(2)}) %collective-permute-start.26) | collective-permute-done | bytes 483360 | tf_op jit(solution)/shard_map/send_31/ppermute | solution.py:361
  124.6 0.2 collective-permute-done.29.refs_3_
  124.8 2.8 %collective-permute-done.31.refs_4_ = bf16[8,30208]{1,0:T(8,128)(2,1)S(1)} collective-permute-done((bf16[8,30208]{1,0:T(8,128)(2,1)S(1)}, bf16[8,30208]{1,0:T(8,128)(2,1)S(1)}, u32[]{:S(2)}, u32[]{:S(2)}) %collective-permute-start.31) | collective-permute-done | bytes 483360 | tf_op jit(solution)/shard_map/send_33/ppermute | solution.py:361
  127.6 1.4 %finish.1 = (f32[8,30208]{1,0:T(8,128)}, f32[8,1024]{1,0:T(8,128)S(1)}) custom-call(s32[1]{0:T(128)} %bitcast.bus_ref, s32[1,1024]{1,0:T(1,128)S(1)} %bitcast.6, f32[8,30208]{1,0:T(8,128)S(1)} %get-tuple-element.53.refs_0_, bf16[8,30208]{1,0:T(8,128)(2,1)S(1)} %collective-permute-done.12.refs_1_, bf16[8,30208]{1,0:T(8,128)(2,1)S(1)} %collective-permute-done.26.refs_2_, ...), custom_call_target="tpu_custom_call" | custom-call | tf_op jit(solution)/shard_map/finish/pallas_call | solution.py:301
  128.9 0.1 collective-permute-start.32
  129.0 1.2 collective-permute-done.32
  130.2 0.6 add_multiply_fusion
  (33 shorter events, 0.1 us)
Async XLA Ops:
  0.6 60.6 %copy-start.5 = (f32[16]{0:T(128)S(1)}, f32[16]{0:T(128)}, u32[]{:S(2)}) copy-start(f32[16]{0:T(128)} %param.15) | copy-start | bytes 196
  0.6 60.6 %copy-start.6 = (s32[128]{0:T(128)S(1)}, s32[128]{0:T(128)}, u32[]{:S(2)}) copy-start(s32[128]{0:T(128)} %param.13) | copy-start | bytes 1540
  0.7 60.6 %copy-start.7 = (f32[16]{0:T(128)S(1)}, f32[16]{0:T(128)}, u32[]{:S(2)}) copy-start(f32[16]{0:T(128)} %param.14) | copy-start | bytes 196
  3.8 16.3 %collective-permute-start = (bf16[8,30208]{1,0:T(8,128)(2,1)}, bf16[8,30208]{1,0:T(8,128)(2,1)S(1)}, u32[]{:S(2)}, u32[]{:S(2)}) collective-permute-start(bf16[8,30208]{1,0:T(8,128)(2,1)} %inject.1.refs_0_), channel_id=1, source_target_pairs={{0,8},{2,10},{4,12},{6,14},{8,16},{10,18},{12,20},{14,22},{16,24},... | collective-permute-start | bytes 1449992 | tf_op jit(solution)/shard_map/send_0/ppermute | solution.py:361
  6.8 13.3 %collective-permute-start.1 = (bf16[8,30208]{1,0:T(8,128)(2,1)}, bf16[8,30208]{1,0:T(8,128)(2,1)S(1)}, u32[]{:S(2)}, u32[]{:S(2)}) collective-permute-start(bf16[8,30208]{1,0:T(8,128)(2,1)} %inject.1.refs_0_), channel_id=1, source_target_pairs={{0,2},{2,0},{4,6},{6,4},{8,10},{10,8},{12,14},{14,12},{16,18},{18,... | collective-permute-start | bytes 1449992 | tf_op jit(solution)/shard_map/send_1/ppermute | solution.py:361
  8.3 13.3 %collective-permute-start.2 = (bf16[8,30208]{1,0:T(8,128)(2,1)}, bf16[8,30208]{1,0:T(8,128)(2,1)S(1)}, u32[]{:S(2)}, u32[]{:S(2)}) collective-permute-start(bf16[8,30208]{1,0:T(8,128)(2,1)} %inject.1.refs_0_), channel_id=1, source_target_pairs={{0,4},{2,6},{4,0},{6,2},{8,12},{10,14},{12,8},{14,10},{16,20},{18,... | collective-permute-start | bytes 1449992 | tf_op jit(solution)/shard_map/send_2/ppermute | solution.py:361
  20.1 15.2 %collective-permute-start.3 = (bf16[8,30208]{1,0:T(8,128)(2,1)S(1)}, bf16[8,30208]{1,0:T(8,128)(2,1)S(1)}, u32[]{:S(2)}, u32[]{:S(2)}) collective-permute-start(bf16[8,30208]{1,0:T(8,128)(2,1)S(1)} %collective-permute-done.refs_1_), channel_id=1, source_target_pairs={{0,8},{2,10},{4,12},{6,14},{8,16},{10,18},{12,20},{14,22},{16,24},... | collective-permute-start | bytes 1449992 | tf_op jit(solution)/shard_map/send_3/ppermute | solution.py:361
  20.1 15.2 %collective-permute-start.4 = (bf16[8,30208]{1,0:T(8,128)(2,1)S(1)}, bf16[8,30208]{1,0:T(8,128)(2,1)S(1)}, u32[]{:S(2)}, u32[]{:S(2)}) collective-permute-start(bf16[8,30208]{1,0:T(8,128)(2,1)S(1)} %collective-permute-done.refs_1_), channel_id=1, source_target_pairs={{0,2},{2,0},{4,6},{6,4},{8,10},{10,8},{12,14},{14,12},{16,18},{18,... | collective-permute-start | bytes 1449992 | tf_op jit(solution)/shard_map/send_4/ppermute | solution.py:361
  21.6 14.8 %collective-permute-start.5 = (bf16[8,30208]{1,0:T(8,128)(2,1)S(1)}, bf16[8,30208]{1,0:T(8,128)(2,1)S(1)}, u32[]{:S(2)}, u32[]{:S(2)}) collective-permute-start(bf16[8,30208]{1,0:T(8,128)(2,1)S(1)} %collective-permute-done.1.refs_2_), channel_id=1, source_target_pairs={{0,4},{2,6},{4,0},{6,2},{8,12},{10,14},{12,8},{14,10},{16,20},{18,... | collective-permute-start | bytes 1449992 | tf_op jit(solution)/shard_map/send_5/ppermute | solution.py:361
  35.3 10.9 %collective-permute-start.6 = (bf16[8,30208]{1,0:T(8,128)(2,1)S(1)}, bf16[8,30208]{1,0:T(8,128)(2,1)S(1)}, u32[]{:S(2)}, u32[]{:S(2)}) collective-permute-start(bf16[8,30208]{1,0:T(8,128)(2,1)S(1)} %collective-permute-done.1.refs_2_), channel_id=1, source_target_pairs={{0,24},{2,26},{4,28},{6,30},{8,0},{10,2},{12,4},{14,6},{16,8},{18,... | collective-permute-start | bytes 1449992 | tf_op jit(solution)/shard_map/send_6/ppermute | solution.py:361
  35.3 12.2 %collective-permute-start.7 = (bf16[8,30208]{1,0:T(8,128)(2,1)S(1)}, bf16[8,30208]{1,0:T(8,128)(2,1)S(1)}, u32[]{:S(2)}, u32[]{:S(2)}) collective-permute-start(bf16[8,30208]{1,0:T(8,128)(2,1)S(1)} %collective-permute-done.3.refs_4_), channel_id=1, source_target_pairs={{0,2},{2,0},{4,6},{6,4},{8,10},{10,8},{12,14},{14,12},{16,18},{18,... | collective-permute-start | bytes 1449992 | tf_op jit(solution)/shard_map/send_7/ppermute | solution.py:361
  36.4 12.1 %collective-permute-start.8 = (bf16[8,30208]{1,0:T(8,128)(2,1)S(1)}, bf16[8,30208]{1,0:T(8,128)(2,1)S(1)}, u32[]{:S(2)}, u32[]{:S(2)}) collective-permute-start(bf16[8,30208]{1,0:T(8,128)(2,1)S(1)} %collective-permute-done.4.refs_5_), channel_id=1, source_target_pairs={{0,4},{2,6},{4,0},{6,2},{8,12},{10,14},{12,8},{14,10},{16,20},{18,... | collective-permute-start | bytes 1449992 | tf_op jit(solution)/shard_map/send_8/ppermute | solution.py:361
  46.2 10.8 %collective-permute-start.10 = (bf16[8,30208]{1,0:T(8,128)(2,1)S(1)}, bf16[8,30208]{1,0:T(8,128)(2,1)S(1)}, u32[]{:S(2)}, u32[]{:S(2)}) collective-permute-start(bf16[8,30208]{1,0:T(8,128)(2,1)S(1)} %collective-permute-done.5.refs_6_), channel_id=1, source_target_pairs={{0,24},{2,26},{4,28},{6,30},{8,0},{10,2},{12,4},{14,6},{16,8},{18,... | collective-permute-start | bytes 1449992 | tf_op jit(solution)/shard_map/send_11/ppermute | solution.py:361
  47.5 11.3 %collective-permute-start.13 = (bf16[8,30208]{1,0:T(8,128)(2,1)S(1)}, bf16[8,30208]{1,0:T(8,128)(2,1)S(1)}, u32[]{:S(2)}, u32[]{:S(2)}) collective-permute-start(bf16[8,30208]{1,0:T(8,128)(2,1)S(1)} %collective-permute-done.6.refs_7_), channel_id=1, source_target_pairs={{0,2},{2,0},{4,6},{6,4},{8,10},{10,8},{12,14},{14,12},{16,18},{18,... | collective-permute-start | bytes 1449992 | tf_op jit(solution)/shard_map/send_12/ppermute | solution.py:361
  48.5 11.2 %collective-permute-start.14 = (bf16[8,30208]{1,0:T(8,128)(2,1)S(1)}, bf16[8,30208]{1,0:T(8,128)(2,1)S(1)}, u32[]{:S(2)}, u32[]{:S(2)}) collective-permute-start(bf16[8,30208]{1,0:T(8,128)(2,1)S(1)} %collective-permute-done.7.refs_8_), channel_id=1, source_target_pairs={{0,4},{2,6},{4,0},{6,2},{8,12},{10,14},{12,8},{14,10},{16,20},{18,... | collective-permute-start | bytes 1449992 | tf_op jit(solution)/shard_map/send_13/ppermute | solution.py:361
  50.1 3.2 %copy-start = (bf16[128,30208]{1,0:T(8,128)(2,1)S(1)}, bf16[128,30208]{1,0:T(8,128)(2,1)}, u32[]{:S(2)}) copy-start(bf16[128,30208]{1,0:T(8,128)(2,1)} %ptdf_ref.3) | copy-start | bytes 23199748
  53.3 1.0 copy-start.2
  54.3 8.2 %copy-start.1 = (bf16[128,30208]{1,0:T(8,128)(2,1)S(1)}, bf16[128,30208]{1,0:T(8,128)(2,1)}, u32[]{:S(2)}) copy-start(bf16[128,30208]{1,0:T(8,128)(2,1)} %ptdf_ref.3) | copy-start | bytes 23199748
  57.0 9.3 %collective-permute-start.11 = (bf16[8,30208]{1,0:T(8,128)(2,1)S(1)}, bf16[8,30208]{1,0:T(8,128)(2,1)S(1)}, u32[]{:S(2)}, u32[]{:S(2)}) collective-permute-start(bf16[8,30208]{1,0:T(8,128)(2,1)S(1)} %collective-permute-done.2.refs_3_), channel_id=1, source_target_pairs={{0,24},{2,26},{4,28},{6,30},{8,0},{10,2},{12,4},{14,6},{16,8},{18,... | collective-permute-start | bytes 1449992 | tf_op jit(solution)/shard_map/send_14/ppermute | solution.py:361
  58.8 10.5 %collective-permute-start.15 = (bf16[8,30208]{1,0:T(8,128)(2,1)S(1)}, bf16[8,30208]{1,0:T(8,128)(2,1)S(1)}, u32[]{:S(2)}, u32[]{:S(2)}) collective-permute-start(bf16[8,30208]{1,0:T(8,128)(2,1)S(1)} %collective-permute-done.8.refs_9_), channel_id=1, source_target_pairs={{0,2},{2,0},{4,6},{6,4},{8,10},{10,8},{12,14},{14,12},{16,18},{18,... | collective-permute-start | bytes 1449992 | tf_op jit(solution)/shard_map/send_15/ppermute | solution.py:361
  59.8 10.9 %collective-permute-start.16 = (bf16[8,30208]{1,0:T(8,128)(2,1)S(1)}, bf16[8,30208]{1,0:T(8,128)(2,1)S(1)}, u32[]{:S(2)}, u32[]{:S(2)}) collective-permute-start(bf16[8,30208]{1,0:T(8,128)(2,1)S(1)} %collective-permute-done.3.refs_4_), channel_id=1, source_target_pairs={{0,4},{2,6},{4,0},{6,2},{8,12},{10,14},{12,8},{14,10},{16,20},{18,... | collective-permute-start | bytes 1449992 | tf_op jit(solution)/shard_map/send_16/ppermute | solution.py:361
  61.3 1.2 collective-permute-start.9
  66.3 11.9 %collective-permute-start.12 = (bf16[8,30208]{1,0:T(8,128)(2,1)S(1)}, bf16[8,30208]{1,0:T(8,128)(2,1)S(1)}, u32[]{:S(2)}, u32[]{:S(2)}) collective-permute-start(bf16[8,30208]{1,0:T(8,128)(2,1)S(1)} %get-tuple-element.57), channel_id=1, source_target_pairs={{0,24},{2,26},{4,28},{6,30},{8,0},{10,2},{12,4},{14,6},{16,8},{18,... | collective-permute-start | bytes 1449992 | tf_op jit(solution)/shard_map/send_21/ppermute | solution.py:361
  69.3 10.5 %collective-permute-start.18 = (bf16[8,30208]{1,0:T(8,128)(2,1)S(1)}, bf16[8,30208]{1,0:T(8,128)(2,1)S(1)}, u32[]{:S(2)}, u32[]{:S(2)}) collective-permute-start(bf16[8,30208]{1,0:T(8,128)(2,1)S(1)} %get-tuple-element.65), channel_id=1, source_target_pairs={{0,2},{2,0},{4,6},{6,4},{8,10},{10,8},{12,14},{14,12},{16,18},{18,... | collective-permute-start | bytes 1449992 | tf_op jit(solution)/shard_map/send_20/ppermute | solution.py:361
  70.7 10.5 %collective-permute-start.22 = (bf16[8,30208]{1,0:T(8,128)(2,1)S(1)}, bf16[8,30208]{1,0:T(8,128)(2,1)S(1)}, u32[]{:S(2)}, u32[]{:S(2)}) collective-permute-start(bf16[8,30208]{1,0:T(8,128)(2,1)S(1)} %get-tuple-element.75), channel_id=1, source_target_pairs={{0,4},{2,6},{4,0},{6,2},{8,12},{10,14},{12,8},{14,10},{16,20},{18,... | collective-permute-start | bytes 1449992 | tf_op jit(solution)/shard_map/send_19/ppermute | solution.py:361
  75.3 1.2 collective-permute-start.17
  78.1 13.2 %collective-permute-start.19 = (bf16[8,30208]{1,0:T(8,128)(2,1)S(1)}, bf16[8,30208]{1,0:T(8,128)(2,1)S(1)}, u32[]{:S(2)}, u32[]{:S(2)}) collective-permute-start(bf16[8,30208]{1,0:T(8,128)(2,1)S(1)} %get-tuple-element.67), channel_id=1, source_target_pairs={{0,24},{2,26},{4,28},{6,30},{8,0},{10,2},{12,4},{14,6},{16,8},{18,... | collective-permute-start | bytes 1449992 | tf_op jit(solution)/shard_map/send_24/ppermute | solution.py:361
  79.9 13.7 %collective-permute-start.21 = (bf16[8,30208]{1,0:T(8,128)(2,1)S(1)}, bf16[8,30208]{1,0:T(8,128)(2,1)S(1)}, u32[]{:S(2)}, u32[]{:S(2)}) collective-permute-start(bf16[8,30208]{1,0:T(8,128)(2,1)S(1)} %get-tuple-element.71), channel_id=1, source_target_pairs={{0,2},{2,0},{4,6},{6,4},{8,10},{10,8},{12,14},{14,12},{16,18},{18,... | collective-permute-start | bytes 1449992 | tf_op jit(solution)/shard_map/send_23/ppermute | solution.py:361
  81.2 12.2 %collective-permute-start.23 = (bf16[8,30208]{1,0:T(8,128)(2,1)S(1)}, bf16[8,30208]{1,0:T(8,128)(2,1)S(1)}, u32[]{:S(2)}, u32[]{:S(2)}) collective-permute-start(bf16[8,30208]{1,0:T(8,128)(2,1)S(1)} %get-tuple-element.76), channel_id=1, source_target_pairs={{0,4},{2,6},{4,0},{6,2},{8,12},{10,14},{12,8},{14,10},{16,20},{18,... | collective-permute-start | bytes 1449992 | tf_op jit(solution)/shard_map/send_22/ppermute | solution.py:361
  83.2 44.4 %copy-start.3 = (s32[1024]{0:T(1024)S(1)}, s32[1024]{0:T(1024)}, u32[]{:S(2)}) copy-start(s32[1024]{0:T(1024)} %param.10) | copy-start | bytes 12292
  91.3 14.2 %collective-permute-start.20 = (bf16[8,30208]{1,0:T(8,128)(2,1)S(1)}, bf16[8,30208]{1,0:T(8,128)(2,1)S(1)}, u32[]{:S(2)}, u32[]{:S(2)}) collective-permute-start(bf16[8,30208]{1,0:T(8,128)(2,1)S(1)} %add_convert_fusion.6), channel_id=1, source_target_pairs={{0,24},{2,26},{4,28},{6,30},{8,0},{10,2},{12,4},{14,6},{16,8},{18,... | collective-permute-start | bytes 1449992 | tf_op jit(solution)/shard_map/send_27/ppermute | solution.py:361
  93.4 11.2 %collective-permute-start.24 = (bf16[8,30208]{1,0:T(8,128)(2,1)S(1)}, bf16[8,30208]{1,0:T(8,128)(2,1)S(1)}, u32[]{:S(2)}, u32[]{:S(2)}) collective-permute-start(bf16[8,30208]{1,0:T(8,128)(2,1)S(1)} %get-tuple-element.77), channel_id=1, source_target_pairs={{0,4},{2,6},{4,0},{6,2},{8,12},{10,14},{12,8},{14,10},{16,20},{18,... | collective-permute-start | bytes 1449992 | tf_op jit(solution)/shard_map/send_25/ppermute | solution.py:361
  93.5 36.7 %copy-start.4 = (f32[1024]{0:T(1024)S(1)}, f32[1024]{0:T(1024)}, u32[]{:S(2)}) copy-start(f32[1024]{0:T(1024)} %param.11) | copy-start | bytes 12292
  93.6 11.2 %collective-permute-start.27 = (bf16[8,30208]{1,0:T(8,128)(2,1)S(1)}, bf16[8,30208]{1,0:T(8,128)(2,1)S(1)}, u32[]{:S(2)}, u32[]{:S(2)}) collective-permute-start(bf16[8,30208]{1,0:T(8,128)(2,1)S(1)} %add_convert_fusion.2), channel_id=1, source_target_pairs={{0,2},{2,0},{4,6},{6,4},{8,10},{10,8},{12,14},{14,12},{16,18},{18,... | collective-permute-start | bytes 1449992 | tf_op jit(solution)/shard_map/send_26/ppermute | solution.py:361
  104.6 11.2 %collective-permute-start.25 = (bf16[8,30208]{1,0:T(8,128)(2,1)S(1)}, bf16[8,30208]{1,0:T(8,128)(2,1)S(1)}, u32[]{:S(2)}, u32[]{:S(2)}) collective-permute-start(bf16[8,30208]{1,0:T(8,128)(2,1)S(1)} %add_convert_fusion.4), channel_id=1, source_target_pairs={{0,4},{2,6},{4,0},{6,2},{8,12},{10,14},{12,8},{14,10},{16,20},{18,... | collective-permute-start | bytes 1449992 | tf_op jit(solution)/shard_map/send_28/ppermute | solution.py:361
  104.7 11.2 %collective-permute-start.28 = (bf16[8,30208]{1,0:T(8,128)(2,1)S(1)}, bf16[8,30208]{1,0:T(8,128)(2,1)S(1)}, u32[]{:S(2)}, u32[]{:S(2)}) collective-permute-start(bf16[8,30208]{1,0:T(8,128)(2,1)S(1)} %get-tuple-element.84), channel_id=1, source_target_pairs={{0,2},{2,0},{4,6},{6,4},{8,10},{10,8},{12,14},{14,12},{16,18},{18,... | collective-permute-start | bytes 1449992 | tf_op jit(solution)/shard_map/send_29/ppermute | solution.py:361
  105.5 11.3 %collective-permute-start.30 = (bf16[8,30208]{1,0:T(8,128)(2,1)S(1)}, bf16[8,30208]{1,0:T(8,128)(2,1)S(1)}, u32[]{:S(2)}, u32[]{:S(2)}) collective-permute-start(bf16[8,30208]{1,0:T(8,128)(2,1)S(1)} %add_convert_fusion.1), channel_id=1, source_target_pairs={{0,8},{2,10},{4,12},{6,14},{8,16},{10,18},{12,20},{14,22},{16,24},... | collective-permute-start | bytes 1449992 | tf_op jit(solution)/shard_map/send_30/ppermute | solution.py:361
  115.8 8.8 %collective-permute-start.26 = (bf16[8,30208]{1,0:T(8,128)(2,1)S(1)}, bf16[8,30208]{1,0:T(8,128)(2,1)S(1)}, u32[]{:S(2)}, u32[]{:S(2)}) collective-permute-start(bf16[8,30208]{1,0:T(8,128)(2,1)S(1)} %add_convert_fusion.5), channel_id=1, source_target_pairs={{0,4},{2,6},{4,0},{6,2},{8,12},{10,14},{12,8},{14,10},{16,20},{18,... | collective-permute-start | bytes 1449992 | tf_op jit(solution)/shard_map/send_31/ppermute | solution.py:361
  115.9 8.8 %collective-permute-start.29 = (bf16[8,30208]{1,0:T(8,128)(2,1)S(1)}, bf16[8,30208]{1,0:T(8,128)(2,1)S(1)}, u32[]{:S(2)}, u32[]{:S(2)}) collective-permute-start(bf16[8,30208]{1,0:T(8,128)(2,1)S(1)} %add_convert_fusion.3), channel_id=1, source_target_pairs={{0,2},{2,0},{4,6},{6,4},{8,10},{10,8},{12,14},{14,12},{16,18},{18,... | collective-permute-start | bytes 1449992 | tf_op jit(solution)/shard_map/send_32/ppermute | solution.py:361
  117.0 10.6 %collective-permute-start.31 = (bf16[8,30208]{1,0:T(8,128)(2,1)S(1)}, bf16[8,30208]{1,0:T(8,128)(2,1)S(1)}, u32[]{:S(2)}, u32[]{:S(2)}) collective-permute-start(bf16[8,30208]{1,0:T(8,128)(2,1)S(1)} %add_convert_fusion), channel_id=1, source_target_pairs={{0,8},{2,10},{4,12},{6,14},{8,16},{10,18},{12,20},{14,22},{16,24},... | collective-permute-start | bytes 1449992 | tf_op jit(solution)/shard_map/send_33/ppermute | solution.py:361
  128.9 1.3 collective-permute-start.32
